TPU v7x, 32 devices: a whole 2x2x4 slice. The times are simulated.
32 devices in a mesh: band: 4 (over y, x), dom: 8 (over z, core).
Axes of the slice: x: 2, y: 2, z: 4, core: 2. Of those that a mesh axis runs over, the one named last changes fastest.
Arguments:
- orbitals: bfloat16 [8, 1408, 800], P('dom', 'band'), may hold values from -6 to 6
- rotation: bfloat16 [800, 800], replicated, may hold values from -0.21875 to 0.21875
- cell_stiffness: bfloat16 [729, 729], replicated, as said below
- cell_scale: float32 [8, 2], P('dom'), may hold values from 0.25 to 1
- potential: float32 [8, 1408], P('dom'), may hold values from 0.25 to 2
- cell_nodes: int32 [8, 2, 729], P('dom'), may hold values from 0 to 2055, as said below
- send_rows: int32 [8, 4, 162], P('dom'), may hold values from 0 to 1408, as said below
- domain_rows: int32 [8], P('dom'), may hold values from 729 to 1377, as said below
Outputs:
- filtered: bfloat16 [8, 1408, 800], P('dom', None, 'band')
Inputs may be any that keep to these rules, and one draw needn't show every extreme that they name: Domain d holds n_d cells with domain_rows[d] = 81 * (8 * n_d + 1) and n_d from 1 to 2; some domain holds 2 cells. `cell_nodes`: an entry below 1408 is an owned row of the domain, below its domain_rows for cells below its cell count; an entry 1408 + g * 162 + s is ghost slot s shared with domain d + o_g, o = (1, 8, -8, -1), and appears only where that domain exists. Consecutive cells of a domain share a layer of nodes. send_rows[e, g, s] is the owned row of domain e, below domain_rows[e], whose value ghost slot s of group g of domain e - o_g holds, o = (1, 8, -8, -1); 1408 marks a slot that no cell uses. Some domain fills all 162 slots of one group. `cell_stiffness`: A symmetric matrix.
All inputs are finite; a program needn't handle non-finite values.
Results may differ from a plain program's by a relative error of at most 0.0062.
Values may be sent and summed in bfloat16 or wider, within the bound.
No kernel may reach another device: no remote copies, remote signals or barrier semaphores. Data moves between devices by JAX's collectives and lax.ppermute only.
A program may use at most 64 MiB of HBM per device.

v0:
```python
import jax
import jax.numpy as jnp
from jax import lax
from jax.sharding import PartitionSpec as P

DEGREE = 8
FILTER_STEPS = 3
FACE_NODES = 81

OFFSETS = (1, 8, -8, -1)
CENTER = 5.0
HALF_WIDTH = 5.0


def round_up(value, multiple):
    return -(-value // multiple) * multiple


def swap(value, first):
    domains = lax.axis_size("dom")
    pairs = []
    for low in range(first, domains - 1, 2):
        pairs += [(low, low + 1), (low + 1, low)]
    return lax.ppermute(value, "dom", pairs)


def shift(value, by):
    domains = lax.axis_size("dom")
    pairs = [(i, i + by) for i in range(domains) if 0 <= i + by < domains]
    return lax.ppermute(value, "dom", pairs)


def far_groups(domains):
    return [g for g, offset in enumerate(OFFSETS) if abs(offset) > 1 and abs(offset) < domains]


def exchange(blocks, to_owner):
    far = far_groups(lax.axis_size("dom"))
    out = [swap(blocks[0], 0), swap(blocks[1], 1)]
    for block, group in zip(blocks[2:], far):
        out.append(shift(block, OFFSETS[group] if to_owner else -OFFSETS[group]))
    return out


def dot(a, b, contract):
    return lax.dot_general(a, b, (contract, ((), ())), preferred_element_type=jnp.float32)


def shards(
    orbitals, rotation, cell_stiffness, cell_scale, potential, cell_nodes, send_rows, domain_rows
):
    bf16 = jnp.bfloat16
    domains = lax.axis_size("dom")
    domain = lax.axis_index("dom")
    row_piece = orbitals[0]
    piece_rows = row_piece.shape[0]
    own_rows = domain_rows[0]
    first_row = lax.axis_index("band") * piece_rows
    row_keep = first_row + jnp.arange(piece_rows, dtype=jnp.int32) < own_rows
    row_piece = jnp.where(row_keep[:, None], row_piece, jnp.zeros_like(row_piece))
    rotated = dot(row_piece, rotation, ((1,), (0,))).astype(bf16)
    current = lax.all_to_all(rotated, "band", split_axis=1, concat_axis=0, tiled=True)

    capacity = potential.shape[1]
    cells, nodes = cell_nodes.shape[1:]
    slots = send_rows.shape[2]
    nodes_pad = round_up(nodes, 256)
    slots_pad = round_up(slots, 64)
    far = far_groups(domains)
    blocks = 2 + len(far)
    even = domain % 2 == 0
    send_lists = [
        jnp.where(even, send_rows[0, 3], send_rows[0, 0]),
        jnp.where(even, send_rows[0, 0], send_rows[0, 3]),
    ] + [send_rows[0, g] for g in far]
    send_list = jnp.stack(send_lists)
    send_list = jnp.pad(send_list, ((0, 0), (0, slots_pad - slots)), constant_values=capacity).reshape(-1)
    group = (cell_nodes[0] - capacity) // slots
    slot = (cell_nodes[0] - capacity) % slots
    block = jnp.where((group == 0) == even, 0, 1)
    for pos, g in enumerate(far):
        block = jnp.where(group == g, 2 + pos, block)
    ghost_index = block * slots_pad + slot
    is_own = cell_nodes[0] < capacity
    pad = ((0, 0), (0, nodes_pad - nodes))
    own_index = jnp.pad(jnp.where(is_own, cell_nodes[0], -1), pad, constant_values=-1).reshape(-1)
    ghost_index = jnp.pad(jnp.where(is_own, -1, ghost_index), pad, constant_values=-1).reshape(-1)
    own_iota = jnp.arange(capacity, dtype=jnp.int32)
    ghost_iota = jnp.arange(blocks * slots_pad, dtype=jnp.int32)
    pick_own = (own_index[:, None] == own_iota[None, :]).astype(bf16)
    pick_ghost = (ghost_index[:, None] == ghost_iota[None, :]).astype(bf16)
    pick_send = (send_list[:, None] == own_iota[None, :]).astype(bf16)
    stiffness = jnp.pad(cell_stiffness, ((0, nodes_pad - nodes), (0, nodes_pad - nodes)))

    cell_total = (own_rows - FACE_NODES) // (DEGREE * FACE_NODES)
    cell_live = jnp.arange(cell_scale.shape[1], dtype=jnp.int32) < cell_total
    cell_weight = jnp.where(cell_live, cell_scale[0], jnp.zeros_like(cell_scale[0]))
    node_potential = potential[0][:, None]
    previous = current
    width = current.shape[1]
    for filter_step in range(FILTER_STEPS):
        picked = dot(pick_send, current, ((1,), (0,))).astype(bf16).reshape(blocks, slots_pad, width)
        ghosts = jnp.concatenate(exchange([picked[b] for b in range(blocks)], False), axis=0)
        local = dot(pick_own, current, ((1,), (0,))) + dot(pick_ghost, ghosts, ((1,), (0,)))
        local = local.astype(bf16).reshape(cells, nodes_pad, width)
        product = jnp.stack([dot(stiffness, local[c], ((0,), (0,))) for c in range(cells)])
        product = (product * cell_weight[:, None, None]).astype(bf16).reshape(-1, width)
        terms = dot(pick_ghost, product, ((0,), (0,))).astype(bf16).reshape(blocks, slots_pad, width)
        arrived = jnp.concatenate(exchange([terms[b] for b in range(blocks)], True), axis=0)
        applied = dot(pick_own, product, ((0,), (0,))) + dot(pick_send, arrived, ((0,), (0,)))
        values = current.astype(jnp.float32)
        shifted = applied + (node_potential - CENTER) * values
        if filter_step == 0:
            following = shifted / HALF_WIDTH
        else:
            following = 2.0 * shifted / HALF_WIDTH - previous.astype(jnp.float32)
        previous, current = current, following.astype(bf16)
    return current[None]


def solution(mesh):
    return jax.shard_map(
        shards,
        mesh=mesh,
        in_specs=(
            P("dom", "band", None),
            P(),
            P(),
            P("dom", None),
            P("dom", None),
            P("dom", None, None),
            P("dom", None, None),
            P("dom"),
        ),
        out_specs=P("dom", None, "band"),
        check_vma=False,
    )
```

profile of v0, /device:TPU:1, one launch (start us, length us, event | category | flops | bytes accessed | tf_op | source)
XLA Modules:
  0.0 70.2 jit_solution(9602918460680431718)
XLA Ops:
  0.8 0.6 copy-done
  1.4 2.9 %convolution_convert_fusion = bf16[352,800]{0,1:T(8,128)(2,1)} fusion(bf16[800,800]{1,0:T(8,128)(2,1)S(1)} %copy-done, bf16[1,352,800]{1,2,0:T(8,128)(2,1)} %param.8, pred[352]{0:T(512)(128)(4,1)S(1)} %add_compare_fusion), kind=kOutput, calls=%fused_computation.44 | convolution fusion | flops 451123200 | bytes 2406752 | tf_op jit(solution)/shard_map/dot_general | solution.py:46
  4.3 4.4 %all-to-all-start = ((bf16[352,4,200]{0,2,1:T(8,128)(2,1)}), bf16[352,4,200]{0,2,1:T(8,128)(2,1)S(1)}, u32[]{:S(2)}, u32[]{:S(2)}) async-start(bf16[352,4,200]{0,2,1:T(8,128)(2,1)} %bitcast.3), calls=%async_computation | async-start | bytes 1228800 | tf_op jit(solution)/shard_map/all_to_all | solution.py:62
  9.1 7.9 %all-to-all-done = bf16[352,4,200]{0,2,1:T(8,128)(2,1)S(1)} async-done(((bf16[352,4,200]{0,2,1:T(8,128)(2,1)}), bf16[352,4,200]{0,2,1:T(8,128)(2,1)S(1)}, u32[]{:S(2)}, u32[]{:S(2)}) %all-to-all-start) | async-done | bytes 563232 | tf_op jit(solution)/shard_map/all_to_all | solution.py:62
  17.1 0.2 copy.10
  17.3 0.4 all_to_all.17
  17.7 0.7 fusion.39
  18.4 0.1 fusion.105
  18.5 1.7 %collective-permute-start = (bf16[192,200]{0,1:T(8,128)(2,1)S(1)}, bf16[192,200]{0,1:T(8,128)(2,1)S(1)}, u32[]{:S(2)}, u32[]{:S(2)}) collective-permute-start(bf16[192,200]{0,1:T(8,128)(2,1)S(1)} %get-tuple-element.15), channel_id=1, source_target_pairs={{0,1},{1,0},{2,3},{3,2},{4,5},{5,4},{6,7},{7,6},{8,9},{9,8},{10,11... | collective-permute-start | bytes 230408 | tf_op jit(solution)/shard_map/ppermute | solution.py:24
  20.2 3.1 %collective-permute-start.1 = (bf16[192,200]{0,1:T(8,128)(2,1)S(1)}, bf16[192,200]{0,1:T(8,128)(2,1)S(1)}, u32[]{:S(2)}, u32[]{:S(2)}) collective-permute-start(bf16[192,200]{0,1:T(8,128)(2,1)S(1)} %get-tuple-element.16), channel_id=1, source_target_pairs={{1,2},{2,1},{3,4},{4,3},{5,6},{6,5},{9,10},{10,9},{11,12},{12,11},... | collective-permute-start | bytes 230408 | tf_op jit(solution)/shard_map/ppermute | solution.py:24
  23.3 2.4 %fusion.5 = f32[1536,200]{0,1:T(8,128)S(1)} fusion(bf16[1408,200]{0,1:T(8,128)(2,1)S(1)} %all_to_all.17, s32[1536]{0:T(1024)S(1)} %eq.62), kind=kOutput, calls=%fused_computation.6 | convolution fusion | flops 867237888 | bytes 1798144 | tf_op jit(solution)/shard_map/dot_general | solution.py:46
  25.8 0.4 collective-permute-done.1
  26.2 0.8 %fusion.22 = bf16[1536,200]{0,1:T(8,128)(2,1)S(1)} fusion(f32[1536,200]{0,1:T(8,128)S(1)} %fusion.5, s32[1536]{0:T(1024)S(1)} %eq.70, bf16[192,200]{0,1:T(8,128)(2,1)S(1)} %collective-permute-done.1, bf16[192,200]{0,1:T(8,128)(2,1)S(1)} %collective-permute-done), kind=kOutput, calls=%fused_computation.29 | convolution fusion | flops 237441024 | bytes 2002944 | tf_op jit(solution)/shard_map/dot_general | solution.py:46
  27.0 0.4 convolution_bitcast_fusion.4
  27.4 0.4 convolution_bitcast_fusion.5
  27.9 0.1 maximum_bitcast_fusion
  28.0 0.1 copy.14
  28.1 0.6 fusion.42
  29.0 3.6 %collective-permute-start.3 = (bf16[192,200]{0,1:T(8,128)(2,1)S(1)}, bf16[192,200]{0,1:T(8,128)(2,1)S(1)}, u32[]{:S(2)}, u32[]{:S(2)}) collective-permute-start(bf16[192,200]{0,1:T(8,128)(2,1)S(1)} %get-tuple-element.14), channel_id=1, source_target_pairs={{1,2},{2,1},{3,4},{4,3},{5,6},{6,5},{9,10},{10,9},{11,12},{12,11},... | collective-permute-start | bytes 230408 | tf_op jit(solution)/shard_map/ppermute | solution.py:24
  32.6 1.8 %fusion.4 = f32[1408,200]{0,1:T(8,128)S(1)} fusion(s32[1536]{0:T(1024)S(1)} %eq.62, f32[1536,200]{0,1:T(8,128)S(1)} %bitcast.56, f32[1536]{0:T(1024)S(1)} %mul.62), kind=kOutput, calls=%fused_computation.5 | convolution fusion | flops 867852288 | bytes 2367488 | tf_op jit(solution)/shard_map/dot_general | solution.py:46
  34.4 0.5 collective-permute-done.3
  34.9 0.7 %fusion.25 = bf16[1408,200]{0,1:T(8,128)(2,1)S(1)} fusion(f32[1408,200]{0,1:T(8,128)S(1)} %fusion.4, bf16[1408,200]{0,1:T(8,128)(2,1)S(1)} %all_to_all.17, s32[384]{0:T(512)S(1)} %eq.74, f32[1408]{0:T(1024)S(1)} %add_reduce_fusion, bf16[192,200]{0,1:T(8,128)(2,1)S(1)} %collective-permute-done.3, bf16[192,200]{0,1:T(8,128)(2,1)S(1)} %collective-permute-done.2), kind=kOutput, calls=%fused_computation.32 | convolution fusion | flops 218806272 | bytes 2413568 | tf_op jit(solution)/shard_map/dot_general | solution.py:46
  35.7 0.7 fusion.40
  36.5 3.9 %collective-permute-start.5 = (bf16[192,200]{0,1:T(8,128)(2,1)S(1)}, bf16[192,200]{0,1:T(8,128)(2,1)S(1)}, u32[]{:S(2)}, u32[]{:S(2)}) collective-permute-start(bf16[192,200]{0,1:T(8,128)(2,1)S(1)} %get-tuple-element.12), channel_id=1, source_target_pairs={{1,2},{2,1},{3,4},{4,3},{5,6},{6,5},{9,10},{10,9},{11,12},{12,11},... | collective-permute-start | bytes 230408 | tf_op jit(solution)/shard_map/ppermute | solution.py:24
  40.4 2.4 %fusion.3 = f32[1536,200]{0,1:T(8,128)S(1)} fusion(bf16[1408,200]{0,1:T(8,128)(2,1)S(1)} %fusion.25, s32[1536]{0:T(1024)S(1)} %eq.62), kind=kOutput, calls=%fused_computation.4 | convolution fusion | flops 867237888 | bytes 1798144 | tf_op jit(solution)/shard_map/dot_general | solution.py:46
  42.9 0.8 %fusion.23 = bf16[1536,200]{0,1:T(8,128)(2,1)S(1)} fusion(f32[1536,200]{0,1:T(8,128)S(1)} %fusion.3, s32[1536]{0:T(1024)S(1)} %eq.70, bf16[192,200]{0,1:T(8,128)(2,1)S(1)} %collective-permute-done.5, bf16[192,200]{0,1:T(8,128)(2,1)S(1)} %collective-permute-done.4), kind=kOutput, calls=%fused_computation.30 | convolution fusion | flops 237441024 | bytes 2002944 | tf_op jit(solution)/shard_map/dot_general | solution.py:46
  43.7 0.4 convolution_bitcast_fusion.2
  44.1 0.4 convolution_bitcast_fusion.3
  44.6 0.1 maximum_bitcast_fusion.1
  44.7 0.1 copy.15
  44.8 0.6 fusion.43
  45.7 3.7 %collective-permute-start.7 = (bf16[192,200]{0,1:T(8,128)(2,1)S(1)}, bf16[192,200]{0,1:T(8,128)(2,1)S(1)}, u32[]{:S(2)}, u32[]{:S(2)}) collective-permute-start(bf16[192,200]{0,1:T(8,128)(2,1)S(1)} %get-tuple-element.10), channel_id=1, source_target_pairs={{1,2},{2,1},{3,4},{4,3},{5,6},{6,5},{9,10},{10,9},{11,12},{12,11},... | collective-permute-start | bytes 230408 | tf_op jit(solution)/shard_map/ppermute | solution.py:24
  49.4 1.8 %fusion.2 = f32[1408,200]{0,1:T(8,128)S(1)} fusion(s32[1536]{0:T(1024)S(1)} %eq.62, f32[1536,200]{0,1:T(8,128)S(1)} %bitcast.58, f32[1536]{0:T(1024)S(1)} %mul.62), kind=kOutput, calls=%fused_computation.3 | convolution fusion | flops 867852288 | bytes 2367488 | tf_op jit(solution)/shard_map/dot_general | solution.py:46
  51.2 0.5 collective-permute-done.7
  51.7 0.8 %fusion.21 = bf16[1408,200]{0,1:T(8,128)(2,1)S(1)} fusion(f32[1408,200]{0,1:T(8,128)S(1)} %fusion.2, bf16[1408,200]{0,1:T(8,128)(2,1)S(1)} %all_to_all.17, bf16[1408,200]{0,1:T(8,128)(2,1)S(1)} %fusion.25, s32[384]{0:T(512)S(1)} %eq.74, f32[1408]{0:T(1024)S(1)} %add_reduce_fusion, bf16[192,200]{0,1:T(8,128)(2,1)S(1)} %collective-permute-done.7, ...), kind=kOutput, calls=%fused_computation.28 | convolution fusion | flops 219369472 | bytes 2976768 | tf_op jit(solution)/shard_map/dot_general | solution.py:46
  52.5 0.7 fusion.41
  53.4 3.7 %collective-permute-start.9 = (bf16[192,200]{0,1:T(8,128)(2,1)S(1)}, bf16[192,200]{0,1:T(8,128)(2,1)S(1)}, u32[]{:S(2)}, u32[]{:S(2)}) collective-permute-start(bf16[192,200]{0,1:T(8,128)(2,1)S(1)} %get-tuple-element.8), channel_id=1, source_target_pairs={{1,2},{2,1},{3,4},{4,3},{5,6},{6,5},{9,10},{10,9},{11,12},{12,11},... | collective-permute-start | bytes 230408 | tf_op jit(solution)/shard_map/ppermute | solution.py:24
  57.1 2.4 %fusion.1 = f32[1536,200]{0,1:T(8,128)S(1)} fusion(bf16[1408,200]{0,1:T(8,128)(2,1)S(1)} %fusion.21, s32[1536]{0:T(1024)S(1)} %eq.62), kind=kOutput, calls=%fused_computation.2 | convolution fusion | flops 867237888 | bytes 1798144 | tf_op jit(solution)/shard_map/dot_general | solution.py:46
  59.6 0.8 %fusion.24 = bf16[1536,200]{0,1:T(8,128)(2,1)S(1)} fusion(f32[1536,200]{0,1:T(8,128)S(1)} %fusion.1, s32[1536]{0:T(1024)S(1)} %eq.70, bf16[192,200]{0,1:T(8,128)(2,1)S(1)} %collective-permute-done.9, bf16[192,200]{0,1:T(8,128)(2,1)S(1)} %collective-permute-done.8), kind=kOutput, calls=%fused_computation.31 | convolution fusion | flops 237441024 | bytes 2002944 | tf_op jit(solution)/shard_map/dot_general | solution.py:46
  60.4 0.4 convolution_bitcast_fusion
  60.8 0.4 convolution_bitcast_fusion.1
  61.3 0.1 maximum_bitcast_fusion.2
  61.4 0.1 copy.16
  61.5 0.6 fusion.44
  62.4 4.1 %collective-permute-start.11 = (bf16[192,200]{0,1:T(8,128)(2,1)S(1)}, bf16[192,200]{0,1:T(8,128)(2,1)S(1)}, u32[]{:S(2)}, u32[]{:S(2)}) collective-permute-start(bf16[192,200]{0,1:T(8,128)(2,1)S(1)} %get-tuple-element.6), channel_id=1, source_target_pairs={{1,2},{2,1},{3,4},{4,3},{5,6},{6,5},{9,10},{10,9},{11,12},{12,11},... | collective-permute-start | bytes 230408 | tf_op jit(solution)/shard_map/ppermute | solution.py:24
  66.5 1.8 %fusion = f32[1408,200]{0,1:T(8,128)S(1)} fusion(s32[1536]{0:T(1024)S(1)} %eq.62, f32[1536,200]{0,1:T(8,128)S(1)} %bitcast.54, f32[1536]{0:T(1024)S(1)} %mul.62), kind=kOutput, calls=%fused_computation.1 | convolution fusion | flops 867852288 | bytes 2367488 | tf_op jit(solution)/shard_map/dot_general | solution.py:46
  68.3 0.3 collective-permute-done.11
  68.6 1.6 %fusion.26 = bf16[1,1408,200]{1,2,0:T(8,128)(2,1)} fusion(f32[1408,200]{0,1:T(8,128)S(1)} %fusion, bf16[1408,200]{0,1:T(8,128)(2,1)S(1)} %fusion.25, bf16[1408,200]{0,1:T(8,128)(2,1)S(1)} %fusion.21, s32[384]{0:T(512)S(1)} %eq.74, f32[1408]{0:T(1024)S(1)} %add_reduce_fusion, bf16[192,200]{0,1:T(8,128)(2,1)S(1)} %collective-permute-done.11, ...), kind=kOutput, calls=%fused_computation.33 | convolution fusion | flops 219369472 | bytes 2976768 | tf_op jit(solution)/shard_map/dot_general | solution.py:46
  (43 shorter events, 1.2 us)
Async XLA Ops:
  0.0 1.4 %copy-start = (bf16[800,800]{1,0:T(8,128)(2,1)S(1)}, bf16[800,800]{1,0:T(8,128)(2,1)}, u32[]{:S(2)}) copy-start(bf16[800,800]{1,0:T(8,128)(2,1)} %param.9) | copy-start | bytes 3840004
  4.3 4.4 %copy-start.5 = (f32[1,2]{1,0:T(1,128)S(1)}, f32[1,2]{1,0:T(1,128)}, u32[]{:S(2)}) copy-start(f32[1,2]{1,0:T(1,128)} %param.11) | copy-start | bytes 28
  4.3 4.4 %copy-start.4 = (s32[1,4,162]{2,1,0:T(4,128)S(1)}, s32[1,4,162]{2,1,0:T(4,128)}, u32[]{:S(2)}) copy-start(s32[1,4,162]{2,1,0:T(4,128)} %param.14) | copy-start | bytes 7780
  4.3 4.6 %copy-start.2 = (s32[1,2,729]{2,1,0:T(2,128)S(1)}, s32[1,2,729]{2,1,0:T(2,128)}, u32[]{:S(2)}) copy-start(s32[1,2,729]{2,1,0:T(2,128)} %param.13) | copy-start | bytes 17500
  4.3 4.8 %copy-start.3 = (f32[1,1408]{1,0:T(1,128)S(1)}, f32[1,1408]{1,0:T(1,128)}, u32[]{:S(2)}) copy-start(f32[1,1408]{1,0:T(1,128)} %param.12) | copy-start | bytes 16900
  4.3 12.7 %all-to-all-start = ((bf16[352,4,200]{0,2,1:T(8,128)(2,1)}), bf16[352,4,200]{0,2,1:T(8,128)(2,1)S(1)}, u32[]{:S(2)}, u32[]{:S(2)}) async-start(bf16[352,4,200]{0,2,1:T(8,128)(2,1)} %bitcast.3), calls=%async_computation | async-start | bytes 1228800 | tf_op jit(solution)/shard_map/all_to_all | solution.py:62
  18.5 7.2 %collective-permute-start = (bf16[192,200]{0,1:T(8,128)(2,1)S(1)}, bf16[192,200]{0,1:T(8,128)(2,1)S(1)}, u32[]{:S(2)}, u32[]{:S(2)}) collective-permute-start(bf16[192,200]{0,1:T(8,128)(2,1)S(1)} %get-tuple-element.15), channel_id=1, source_target_pairs={{0,1},{1,0},{2,3},{3,2},{4,5},{5,4},{6,7},{7,6},{8,9},{9,8},{10,11... | collective-permute-start | bytes 230408 | tf_op jit(solution)/shard_map/ppermute | solution.py:24
  20.2 6.0 %collective-permute-start.1 = (bf16[192,200]{0,1:T(8,128)(2,1)S(1)}, bf16[192,200]{0,1:T(8,128)(2,1)S(1)}, u32[]{:S(2)}, u32[]{:S(2)}) collective-permute-start(bf16[192,200]{0,1:T(8,128)(2,1)S(1)} %get-tuple-element.16), channel_id=1, source_target_pairs={{1,2},{2,1},{3,4},{4,3},{5,6},{6,5},{9,10},{10,9},{11,12},{12,11},... | collective-permute-start | bytes 230408 | tf_op jit(solution)/shard_map/ppermute | solution.py:24
  25.7 1.3 %copy-start.1 = (bf16[729,729]{1,0:T(8,128)(2,1)S(1)}, bf16[729,729]{1,0:T(8,128)(2,1)}, u32[]{:S(2)}) copy-start(bf16[729,729]{1,0:T(8,128)(2,1)} %param.10) | copy-start | bytes 3188650
  28.9 5.5 %collective-permute-start.2 = (bf16[192,200]{0,1:T(8,128)(2,1)S(1)}, bf16[192,200]{0,1:T(8,128)(2,1)S(1)}, u32[]{:S(2)}, u32[]{:S(2)}) collective-permute-start(bf16[192,200]{0,1:T(8,128)(2,1)S(1)} %get-tuple-element.13), channel_id=1, source_target_pairs={{0,1},{1,0},{2,3},{3,2},{4,5},{5,4},{6,7},{7,6},{8,9},{9,8},{10,11... | collective-permute-start | bytes 230408 | tf_op jit(solution)/shard_map/ppermute | solution.py:24
  29.0 6.0 %collective-permute-start.3 = (bf16[192,200]{0,1:T(8,128)(2,1)S(1)}, bf16[192,200]{0,1:T(8,128)(2,1)S(1)}, u32[]{:S(2)}, u32[]{:S(2)}) collective-permute-start(bf16[192,200]{0,1:T(8,128)(2,1)S(1)} %get-tuple-element.14), channel_id=1, source_target_pairs={{1,2},{2,1},{3,4},{4,3},{5,6},{6,5},{9,10},{10,9},{11,12},{12,11},... | collective-permute-start | bytes 230408 | tf_op jit(solution)/shard_map/ppermute | solution.py:24
  36.5 6.4 %collective-permute-start.4 = (bf16[192,200]{0,1:T(8,128)(2,1)S(1)}, bf16[192,200]{0,1:T(8,128)(2,1)S(1)}, u32[]{:S(2)}, u32[]{:S(2)}) collective-permute-start(bf16[192,200]{0,1:T(8,128)(2,1)S(1)} %get-tuple-element.11), channel_id=1, source_target_pairs={{0,1},{1,0},{2,3},{3,2},{4,5},{5,4},{6,7},{7,6},{8,9},{9,8},{10,11... | collective-permute-start | bytes 230408 | tf_op jit(solution)/shard_map/ppermute | solution.py:24
  36.5 6.3 %collective-permute-start.5 = (bf16[192,200]{0,1:T(8,128)(2,1)S(1)}, bf16[192,200]{0,1:T(8,128)(2,1)S(1)}, u32[]{:S(2)}, u32[]{:S(2)}) collective-permute-start(bf16[192,200]{0,1:T(8,128)(2,1)S(1)} %get-tuple-element.12), channel_id=1, source_target_pairs={{1,2},{2,1},{3,4},{4,3},{5,6},{6,5},{9,10},{10,9},{11,12},{12,11},... | collective-permute-start | bytes 230408 | tf_op jit(solution)/shard_map/ppermute | solution.py:24
  45.6 5.6 %collective-permute-start.6 = (bf16[192,200]{0,1:T(8,128)(2,1)S(1)}, bf16[192,200]{0,1:T(8,128)(2,1)S(1)}, u32[]{:S(2)}, u32[]{:S(2)}) collective-permute-start(bf16[192,200]{0,1:T(8,128)(2,1)S(1)} %get-tuple-element.9), channel_id=1, source_target_pairs={{0,1},{1,0},{2,3},{3,2},{4,5},{5,4},{6,7},{7,6},{8,9},{9,8},{10,11... | collective-permute-start | bytes 230408 | tf_op jit(solution)/shard_map/ppermute | solution.py:24
  45.7 6.1 %collective-permute-start.7 = (bf16[192,200]{0,1:T(8,128)(2,1)S(1)}, bf16[192,200]{0,1:T(8,128)(2,1)S(1)}, u32[]{:S(2)}, u32[]{:S(2)}) collective-permute-start(bf16[192,200]{0,1:T(8,128)(2,1)S(1)} %get-tuple-element.10), channel_id=1, source_target_pairs={{1,2},{2,1},{3,4},{4,3},{5,6},{6,5},{9,10},{10,9},{11,12},{12,11},... | collective-permute-start | bytes 230408 | tf_op jit(solution)/shard_map/ppermute | solution.py:24
  53.3 6.2 %collective-permute-start.8 = (bf16[192,200]{0,1:T(8,128)(2,1)S(1)}, bf16[192,200]{0,1:T(8,128)(2,1)S(1)}, u32[]{:S(2)}, u32[]{:S(2)}) collective-permute-start(bf16[192,200]{0,1:T(8,128)(2,1)S(1)} %get-tuple-element.7), channel_id=1, source_target_pairs={{0,1},{1,0},{2,3},{3,2},{4,5},{5,4},{6,7},{7,6},{8,9},{9,8},{10,11... | collective-permute-start | bytes 230408 | tf_op jit(solution)/shard_map/ppermute | solution.py:24
  53.4 6.2 %collective-permute-start.9 = (bf16[192,200]{0,1:T(8,128)(2,1)S(1)}, bf16[192,200]{0,1:T(8,128)(2,1)S(1)}, u32[]{:S(2)}, u32[]{:S(2)}) collective-permute-start(bf16[192,200]{0,1:T(8,128)(2,1)S(1)} %get-tuple-element.8), channel_id=1, source_target_pairs={{1,2},{2,1},{3,4},{4,3},{5,6},{6,5},{9,10},{10,9},{11,12},{12,11},... | collective-permute-start | bytes 230408 | tf_op jit(solution)/shard_map/ppermute | solution.py:24
  62.3 6.0 %collective-permute-start.10 = (bf16[192,200]{0,1:T(8,128)(2,1)S(1)}, bf16[192,200]{0,1:T(8,128)(2,1)S(1)}, u32[]{:S(2)}, u32[]{:S(2)}) collective-permute-start(bf16[192,200]{0,1:T(8,128)(2,1)S(1)} %get-tuple-element.5), channel_id=1, source_target_pairs={{0,1},{1,0},{2,3},{3,2},{4,5},{5,4},{6,7},{7,6},{8,9},{9,8},{10,11... | collective-permute-start | bytes 230408 | tf_op jit(solution)/shard_map/ppermute | solution.py:24
  62.4 6.2 %collective-permute-start.11 = (bf16[192,200]{0,1:T(8,128)(2,1)S(1)}, bf16[192,200]{0,1:T(8,128)(2,1)S(1)}, u32[]{:S(2)}, u32[]{:S(2)}) collective-permute-start(bf16[192,200]{0,1:T(8,128)(2,1)S(1)} %get-tuple-element.6), channel_id=1, source_target_pairs={{1,2},{2,1},{3,4},{4,3},{5,6},{6,5},{9,10},{10,9},{11,12},{12,11},... | collective-permute-start | bytes 230408 | tf_op jit(solution)/shard_map/ppermute | solution.py:24
where the time goes:
time: 70.6 us; the launch traced here: 70.2 us
  starting transfers between devices  28.6 us (41%)
  matrix products  27.8 us (39%)
  waiting for transfers between devices  9.62 us (14%)
  local copies, waits for them, and re-layouts  2.45 us (3%)
  between operations  1.25 us (2%)
    dot_general x25, matrix products, dot(): lax.dot_general(a, b, (contract, ((), ())), preferred_element_type=jnp.fl...  27.8 us
    ppermute x12, starting transfers between devices, swap(): return lax.ppermute(value, 'dom', pairs)  24.2 us
    all_to_all x1, waiting for transfers between devices, shards(): lax.all_to_all(rotated, 'band', split_axis=1, concat_axis=0, tiled=True)  7.94 us
    all_to_all x1, starting transfers between devices, shards(): lax.all_to_all(rotated, 'band', split_axis=1, concat_axis=0, tiled=True)  4.41 us
    ppermute x12, waiting for transfers between devices, swap(): return lax.ppermute(value, 'dom', pairs)  1.67 us
  transfers between devices with their start and end apart: 13, of which 5 were waited for; matrix products, arithmetic and copies ran while one was open for 19% of the time, Pallas kernels for 0%

commit v1 on v0

v1 whole, which is shorter than its diff:
```python
import functools

import jax
import jax.numpy as jnp
from jax import lax
from jax.experimental import pallas as pl
from jax.experimental.pallas import tpu as pltpu
from jax.sharding import PartitionSpec as P

DEGREE = 8
FILTER_STEPS = 3
FACE_NODES = 81

OFFSETS = (1, 8, -8, -1)
CENTER = 5.0
HALF_WIDTH = 5.0
BF16 = jnp.bfloat16
F32 = jnp.float32
VMEM = pl.BlockSpec(memory_space=pltpu.VMEM)
SMEM = pl.BlockSpec(memory_space=pltpu.SMEM)


def round_up(value, multiple):
    return -(-value // multiple) * multiple


def swap(value, first):
    domains = lax.axis_size("dom")
    pairs = []
    for low in range(first, domains - 1, 2):
        pairs += [(low, low + 1), (low + 1, low)]
    return lax.ppermute(value, "dom", pairs)


def shift(value, by):
    domains = lax.axis_size("dom")
    pairs = [(i, i + by) for i in range(domains) if 0 <= i + by < domains]
    return lax.ppermute(value, "dom", pairs)


def far_groups(domains):
    return [g for g, offset in enumerate(OFFSETS) if abs(offset) > 1 and abs(offset) < domains]


def exchange(blocks, to_owner):
    far = far_groups(lax.axis_size("dom"))
    out = [swap(blocks[0], 0), swap(blocks[1], 1)]
    for block, group in zip(blocks[2:], far):
        out.append(shift(block, OFFSETS[group] if to_owner else -OFFSETS[group]))
    return out


def call(kernel, out_shape, args, flops, scalars=0, scratch=()):
    outs = out_shape if isinstance(out_shape, (tuple, list)) else (out_shape,)
    size = sum(a.size * a.dtype.itemsize for a in list(args) + list(outs))
    return pl.pallas_call(
        kernel,
        out_shape=out_shape,
        in_specs=[SMEM] * scalars + [VMEM] * (len(args) - scalars),
        out_specs=jax.tree.map(lambda _: VMEM, out_shape),
        scratch_shapes=list(scratch),
        cost_estimate=pl.CostEstimate(flops=flops, bytes_accessed=size, transcendentals=0),
        compiler_params=pltpu.CompilerParams(vmem_limit_bytes=24 << 20),
    )(*args)


def shape(dims, dtype):
    return jax.ShapeDtypeStruct(dims, dtype)


def mm(a, b):
    return jnp.dot(a, b, preferred_element_type=F32)


def mm_nt(a, b):
    return lax.dot_general(a, b, (((1,), (1,)), ((), ())), preferred_element_type=F32)


def rows_hot(index, first, count):
    rows = lax.broadcasted_iota(jnp.int32, (count, index.shape[1]), 0) + first
    return (rows == index).astype(BF16)


def steps(total, size):
    return [(i, min(size, total - i)) for i in range(0, total, size)]


def rotate_kernel(scalars, piece, rotation, out):
    width = out.shape[1]
    rotated = lax.dot_general(
        rotation[...], piece[...], (((0,), (0,)), ((), ())), preferred_element_type=F32
    )
    rows = lax.broadcasted_iota(jnp.int32, rotated.shape, 1) + scalars[0]
    rotated = jnp.where(rows < scalars[1], rotated, 0.0)
    for group in range(out.shape[0]):
        out[group] = rotated[group * width : (group + 1) * width, :].astype(BF16)


def couple_kernel(capacity, weight, node_row, stiffness, to_ghost, to_own, *locals_):
    nodes = stiffness.shape[0]
    blocks, slots = to_own.shape[:2]
    for block in range(blocks):
        local = locals_[block]
        for cell in range(weight.shape[0]):
            picks = rows_hot(node_row[:, cell * nodes : (cell + 1) * nodes], capacity + block * slots, slots)
            product = mm(picks, stiffness[...]) * weight[cell]
            local[:, cell * nodes : (cell + 1) * nodes] = product.astype(BF16)
        for other in range(blocks):
            picks = rows_hot(node_row[...], capacity + other * slots, slots)
            to_ghost[block, other] = mm_nt(local[...], picks).astype(BF16)
    for i, n in steps(capacity, 256):
        picks = rows_hot(node_row[...], i, n)
        for block in range(blocks):
            to_own[block, :, i : i + n] = mm_nt(locals_[block][...], picks).astype(BF16)


def pick_rows(send_row, values, outs):
    for block, out in enumerate(outs):
        picks = rows_hot(send_row[block : block + 1, :], 0, values.shape[1])
        out[...] = mm(values[...], picks).astype(BF16)


def join_kernel(send_row, pieces, values, *outs):
    values[...] = jnp.concatenate([pieces[p] for p in range(pieces.shape[0])], axis=1)
    pick_rows(send_row, values, outs)


def cells_kernel(weight, node_row, stiffness, values, product, terms, local):
    capacity = values.shape[1]
    nodes = stiffness.shape[0]
    blocks, _, slots = terms.shape
    for cell in range(weight.shape[0]):
        first = cell * nodes
        for i, n in steps(nodes, 256):
            picks = rows_hot(node_row[:, first + i : first + i + n], 0, capacity)
            local[:, i : i + n] = mm(values[...], picks).astype(BF16)
        result = mm(local[...], stiffness[...]) * weight[cell]
        product[:, first : first + nodes] = result.astype(BF16)
    for block in range(blocks):
        terms[block] = mm_nt(product[...], rows_hot(node_row[...], capacity + block * slots, slots))


def ghost_kernel(terms, to_ghost, *refs):
    blocks = terms.shape[0]
    arrived, outs = refs[:blocks], refs[blocks:]
    for block in range(blocks):
        total = terms[block]
        for other in range(blocks):
            total = total + mm(arrived[other][...], to_ghost[other, block])
        outs[block][...] = total.astype(BF16)


def own_kernel(node_row, product, to_own, *refs):
    arrived, out = refs[:-1], refs[-1]
    for i, n in steps(out.shape[1], 256):
        total = mm_nt(product[...], rows_hot(node_row[...], i, n))
        for block, ghost in enumerate(arrived):
            total = total + mm(ghost[...], to_own[block, :, i : i + n])
        out[:, i : i + n] = total


def update_kernel(blocks, first_step, last_step, send_row, potential, total, values, *refs):
    refs = list(refs)
    previous = None if first_step else refs.pop(0)
    arrived, out, picked = refs[:blocks], refs[blocks], refs[blocks + 1 :]
    for i, n in steps(out.shape[1], 256):
        at = slice(i, i + n)
        applied = total[:, at]
        for block in range(blocks):
            applied = applied + mm_nt(arrived[block][...], rows_hot(send_row[block : block + 1, :], i, n))
        shifted = applied + (potential[:, at] - CENTER) * values[:, at].astype(F32)
        if first_step:
            following = shifted * (1.0 / HALF_WIDTH)
        else:
            following = shifted * (2.0 / HALF_WIDTH) - previous[:, at].astype(F32)
        out[:, at] = following.astype(BF16)
    if not last_step:
        pick_rows(send_row, out, picked)


def shards(
    orbitals, rotation, cell_stiffness, cell_scale, potential, cell_nodes, send_rows, domain_rows
):
    domains = lax.axis_size("dom")
    bands = lax.axis_size("band")
    domain = lax.axis_index("dom")
    row_piece = orbitals[0]
    piece_rows, columns = row_piece.shape
    own_rows = domain_rows[0]
    width = columns // bands
    first_row = lax.axis_index("band") * piece_rows
    rotated = call(
        rotate_kernel,
        shape((bands, width, piece_rows), BF16),
        (jnp.stack([first_row, own_rows]).astype(jnp.int32), row_piece.T, rotation),
        2 * piece_rows * columns * columns,
        scalars=1,
    )
    pieces = lax.all_to_all(rotated, "band", split_axis=0, concat_axis=0, tiled=True)

    capacity = potential.shape[1]
    cells, nodes = cell_nodes.shape[1:]
    slots = send_rows.shape[2]
    nodes_pad = round_up(nodes, 256)
    slots_pad = round_up(slots, 16)
    far = far_groups(domains)
    blocks = 2 + len(far)
    ghosts = blocks * slots_pad
    even = domain % 2 == 0
    send_lists = [
        jnp.where(even, send_rows[0, 3], send_rows[0, 0]),
        jnp.where(even, send_rows[0, 0], send_rows[0, 3]),
    ] + [send_rows[0, g] for g in far]
    send_row = jnp.pad(
        jnp.stack(send_lists), ((0, 0), (0, slots_pad - slots)), constant_values=capacity
    )
    group = (cell_nodes[0] - capacity) // slots
    slot = (cell_nodes[0] - capacity) % slots
    block = jnp.where((group == 0) == even, 0, 1)
    for pos, g in enumerate(far):
        block = jnp.where(group == g, 2 + pos, block)
    ghost_index = capacity + block * slots_pad + slot
    node_list = jnp.where(cell_nodes[0] < capacity, cell_nodes[0], ghost_index)
    node_list = jnp.pad(
        node_list, ((0, 0), (0, nodes_pad - nodes)), constant_values=capacity + ghosts
    ).reshape(-1)
    node_row = node_list[None, :]
    stiffness = jnp.pad(cell_stiffness, ((0, nodes_pad - nodes), (0, nodes_pad - nodes)))

    cell_total = (own_rows - FACE_NODES) // (DEGREE * FACE_NODES)
    cell_live = jnp.arange(cell_scale.shape[1], dtype=jnp.int32) < cell_total
    weight = jnp.where(cell_live, cell_scale[0], jnp.zeros_like(cell_scale[0]))

    local_rows = cells * nodes_pad
    cell_flops = 2 * local_rows * nodes_pad
    to_ghost, to_own = call(
        functools.partial(couple_kernel, capacity),
        (
            shape((blocks, blocks, slots_pad, slots_pad), BF16),
            shape((blocks, slots_pad, capacity), BF16),
        ),
        (weight, node_row, stiffness),
        (cell_flops + 2 * local_rows * (ghosts + capacity)) * ghosts,
        scalars=1,
        scratch=[pltpu.VMEM((slots_pad, local_rows), BF16)] * blocks,
    )
    block_shapes = (shape((width, slots_pad), BF16),) * blocks
    current, *picked = call(
        join_kernel,
        (shape((width, capacity), BF16),) + block_shapes,
        (send_row, pieces),
        2 * ghosts * capacity * width,
    )
    previous = None
    for filter_step in range(FILTER_STEPS):
        last = filter_step == FILTER_STEPS - 1
        arrived = exchange(picked, False)
        product, terms = call(
            cells_kernel,
            (shape((width, local_rows), BF16), shape((blocks, width, slots_pad), F32)),
            (weight, node_row, stiffness, current),
            (cell_flops + 2 * local_rows * (capacity + ghosts)) * width,
            scalars=1,
            scratch=[pltpu.VMEM((width, nodes_pad), BF16)],
        )
        sums = call(
            ghost_kernel, block_shapes, (terms, to_ghost, *arrived), 2 * ghosts * ghosts * width
        )
        returned = exchange(sums, True)
        total = call(
            own_kernel,
            shape((width, capacity), F32),
            (node_row, product, to_own, *arrived),
            2 * capacity * (local_rows + ghosts) * width,
        )
        operands = [send_row, potential, total, current]
        if previous is not None:
            operands.append(previous)
        following, *picked = call(
            functools.partial(update_kernel, blocks, previous is None, last),
            (shape((width, capacity), BF16),) + (() if last else block_shapes),
            (*operands, *returned),
            4 * capacity * ghosts * width,
        )
        previous, current = current, following
    return current.T[None]


def solution(mesh):
    return jax.shard_map(
        shards,
        mesh=mesh,
        in_specs=(
            P("dom", "band", None),
            P(),
            P(),
            P("dom", None),
            P("dom", None),
            P("dom", None, None),
            P("dom", None, None),
            P("dom"),
        ),
        out_specs=P("dom", None, "band"),
        check_vma=False,
    )
```

time: 70.6 us -> 63.6 us (0.901)
  matrix products: 27.8 us -> 0 us
  Pallas kernels: 0 us -> 27 us
  waiting for transfers between devices: 9.62 us -> 4.42 us
  starting transfers between devices: 28.6 us -> 27.6 us
    dot_general x25 -> x0, matrix products: 27.8 us -> none  [dot(): lax.dot_general(a, b, (contract, ((), ())), preferred_element_type=jnp.fl...]
    pallas_call x0 -> x15, Pallas kernels: none -> 27 us  [call(): pl.pallas_call(kernel, out_shape=out_shape, in_specs=[SMEM] * scalars + [...]
    all_to_all x1, waiting for transfers between devices: 7.94 us -> 2.48 us  [shards(): lax.all_to_all(rotated, 'band', split_axis=0, concat_axis=0, tiled=True)]
    unnamed x12 -> x16, local copies, waits for them, and re-layouts: 0.62 us -> 3 us
    ppermute x12, starting transfers between devices: 24.2 us -> 23.2 us  [swap(): return lax.ppermute(value, 'dom', pairs)]
  transfers between devices with their start and end apart: 13 -> 13, of which waited for: 5 -> 4; matrix products, arithmetic and copies ran while one was open for 19% -> 0% of each run, Pallas kernels for 0% -> 31%
where the time goes in v1:
time: 63.6 us; the launch traced here: 63.2 us
  starting transfers between devices  27.6 us (43%)
  Pallas kernels  27 us (42%)
  waiting for transfers between devices  4.42 us (7%)
  local copies, waits for them, and re-layouts  3.11 us (5%)
  between operations  1 us (2%)
    pallas_call x15, Pallas kernels, call(): pl.pallas_call(kernel, out_shape=out_shape, in_specs=[SMEM] * scalars + [...  27 us
    ppermute x12, starting transfers between devices, swap(): return lax.ppermute(value, 'dom', pairs)  23.2 us
    all_to_all x1, starting transfers between devices, shards(): lax.all_to_all(rotated, 'band', split_axis=0, concat_axis=0, tiled=True)  4.4 us
    unnamed x16, local copies, waits for them, and re-layouts  3 us
    all_to_all x1, waiting for transfers between devices, shards(): lax.all_to_all(rotated, 'band', split_axis=0, concat_axis=0, tiled=True)  2.48 us
    ppermute x12, waiting for transfers between devices, swap(): return lax.ppermute(value, 'dom', pairs)  1.94 us
  transfers between devices with their start and end apart: 13, of which 4 were waited for; matrix products, arithmetic and copies ran while one was open for 0% of the time, Pallas kernels for 31%

profile of v1, /device:TPU:1, one launch (start us, length us, event | category | flops | bytes accessed | tf_op | source)
XLA Modules:
  0.0 63.2 jit_solution(7465926474876325304)
XLA Ops:
  0.7 0.1 pad_add_fusion.1.scalars
  0.7 1.4 %copy-done = bf16[800,800]{1,0:T(8,128)(2,1)S(1)} copy-done((bf16[800,800]{1,0:T(8,128)(2,1)S(1)}, bf16[800,800]{1,0:T(8,128)(2,1)}, u32[]{:S(2)}) %copy-start) | copy-done | bytes 1280024
  2.1 1.1 %copy-done.1 = bf16[1,352,800]{1,2,0:T(8,128)(2,1)S(1)} copy-done((bf16[1,352,800]{1,2,0:T(8,128)(2,1)S(1)}, bf16[1,352,800]{1,2,0:T(8,128)(2,1)}, u32[]{:S(2)}) %copy-start.1) | copy-done | bytes 563224
  3.2 2.4 %shard_map.82 = bf16[4,200,352]{2,1,0:T(8,128)(2,1)} custom-call(s32[2]{0:T(128)S(1)} %pad_add_fusion.1.scalars, bf16[800,352]{1,0:T(8,128)(2,1)S(1)} %bitcast.24, bf16[800,800]{1,0:T(8,128)(2,1)S(1)} %copy-done), custom_call_target="tpu_custom_call" | custom-call | flops 450560000 | bytes 2406408 | tf_op jit(solution)/shard_map/pallas_call | solution.py:56
  5.5 4.4 %all-to-all-start = ((bf16[4,200,352]{2,1,0:T(8,128)(2,1)}), bf16[4,200,352]{2,1,0:T(8,128)(2,1)S(1)}, u32[]{:S(2)}, u32[]{:S(2)}) async-start(bf16[4,200,352]{2,1,0:T(8,128)(2,1)} %shard_map.82), calls=%async_computation | async-start | bytes 1228800 | tf_op jit(solution)/shard_map/all_to_all | solution.py:199
  10.1 0.0 copy-start.6
  10.1 0.1 pad.14.stiffness
  10.2 0.5 copy-done.6
  10.8 5.0 %shard_map.85 = (bf16[2,2,176,176]{3,2,1,0:T(8,128)(2,1)S(1)}, bf16[2,176,1408]{2,1,0:T(8,128)(2,1)S(1)}) custom-call(f32[2]{0:T(128)S(1)} %compare_select_fusion.2.weight, s32[1,1536]{1,0:T(1,128)S(1)} %bitcast.25, bf16[768,768]{1,0:T(8,128)(2,1)S(1)} %pad.14.stiffness), custom_call_target="tpu_custom_call" | custom-call | flops 2733637632 | bytes 2424840 | tf_op jit(solution)/shard_map/pallas_call | solution.py:56
  15.8 2.5 %all-to-all-done.pieces = bf16[4,200,352]{2,1,0:T(8,128)(2,1)S(1)} async-done(((bf16[4,200,352]{2,1,0:T(8,128)(2,1)}), bf16[4,200,352]{2,1,0:T(8,128)(2,1)S(1)}, u32[]{:S(2)}, u32[]{:S(2)}) %all-to-all-start) | async-done | bytes 563232 | tf_op jit(solution)/shard_map/all_to_all | solution.py:199
  18.3 0.5 shard_map.83
  18.8 1.7 %collective-permute-start = (bf16[200,176]{1,0:T(8,128)(2,1)S(1)}, bf16[200,176]{1,0:T(8,128)(2,1)S(1)}, u32[]{:S(2)}, u32[]{:S(2)}) collective-permute-start(bf16[200,176]{1,0:T(8,128)(2,1)S(1)} %get-tuple-element.31), channel_id=1, source_target_pairs={{0,1},{1,0},{2,3},{3,2},{4,5},{5,4},{6,7},{7,6},{8,9},{9,8},{10,11... | collective-permute-start | bytes 211208 | tf_op jit(solution)/shard_map/ppermute | solution.py:32
  20.5 3.1 %collective-permute-start.1 = (bf16[200,176]{1,0:T(8,128)(2,1)S(1)}, bf16[200,176]{1,0:T(8,128)(2,1)S(1)}, u32[]{:S(2)}, u32[]{:S(2)}) collective-permute-start(bf16[200,176]{1,0:T(8,128)(2,1)S(1)} %get-tuple-element.32), channel_id=1, source_target_pairs={{1,2},{2,1},{3,4},{4,3},{5,6},{6,5},{9,10},{10,9},{11,12},{12,11},... | collective-permute-start | bytes 211208 | tf_op jit(solution)/shard_map/ppermute | solution.py:32
  23.6 3.0 %shard_map.84 = (bf16[200,1536]{1,0:T(8,128)(2,1)S(1)}, f32[2,200,176]{2,1,0:T(8,128)S(1)}) custom-call(f32[2]{0:T(128)S(1)} %compare_select_fusion.2.weight, s32[1,1536]{1,0:T(1,128)S(1)} %bitcast.26, bf16[768,768]{1,0:T(8,128)(2,1)S(1)} %pad.14.stiffness, bf16[200,1408]{1,0:T(8,128)(2,1)S(1)} %get-tuple-element.28.values.refs_0_), custom_call_target="tpu_custom_call" | custom-call | flops 1553203200 | bytes 2645000 | tf_op jit(solution)/shard_map/pallas_call | solution.py:56
  26.6 0.0 collective-permute-done.refs_0_
  26.6 0.0 collective-permute-done.1.refs_1_
  26.6 0.3 shard_map.87
  26.9 0.1 collective-permute-start.2
  27.0 3.6 %collective-permute-start.3 = (bf16[200,176]{1,0:T(8,128)(2,1)S(1)}, bf16[200,176]{1,0:T(8,128)(2,1)S(1)}, u32[]{:S(2)}, u32[]{:S(2)}) collective-permute-start(bf16[200,176]{1,0:T(8,128)(2,1)S(1)} %get-tuple-element.36), channel_id=1, source_target_pairs={{1,2},{2,1},{3,4},{4,3},{5,6},{6,5},{9,10},{10,9},{11,12},{12,11},... | collective-permute-start | bytes 211208 | tf_op jit(solution)/shard_map/ppermute | solution.py:32
  30.5 0.0 copy-start.2
  30.6 1.8 %shard_map.86.total = f32[200,1408]{1,0:T(8,128)S(1)} custom-call(s32[1,1536]{1,0:T(1,128)S(1)} %bitcast.27, bf16[200,1536]{1,0:T(8,128)(2,1)S(1)} %get-tuple-element.29.product, bf16[2,176,1408]{2,1,0:T(8,128)(2,1)S(1)} %get-tuple-element.30.to_own, bf16[200,176]{1,0:T(8,128)(2,1)S(1)} %collective-permute-done.refs_0_, ...), custom_call_target="tpu_custom_call" | custom-call | flops 1063321600 | bytes 2878976 | tf_op jit(solution)/shard_map/pallas_call | solution.py:56
  32.4 0.0 collective-permute-done.2.refs_0_
  32.4 0.6 collective-permute-done.3.refs_1_
  32.9 1.1 %shard_map.88 = (bf16[200,1408]{1,0:T(8,128)(2,1)S(1)}, bf16[200,176]{1,0:T(8,128)(2,1)S(1)}, bf16[200,176]{1,0:T(8,128)(2,1)S(1)}) custom-call(s32[2,176]{1,0:T(2,128)S(1)} %pad.12.send_row, f32[1,1408]{1,0:T(1,128)S(1)} %copy-done.2, f32[200,1408]{1,0:T(8,128)S(1)} %shard_map.86.total, bf16[200,1408]{1,0:T(8,128)(2,1)S(1)} %get-tuple-element.28.values.refs_0_, ...), custom_call_target="tpu_custom_call" | custom-call | flops 396492800 | bytes 2541440 | tf_op jit(solution)/shard_map/pallas_call | solution.py:56
  34.1 0.1 collective-permute-start.4
  34.2 3.7 %collective-permute-start.5 = (bf16[200,176]{1,0:T(8,128)(2,1)S(1)}, bf16[200,176]{1,0:T(8,128)(2,1)S(1)}, u32[]{:S(2)}, u32[]{:S(2)}) collective-permute-start(bf16[200,176]{1,0:T(8,128)(2,1)S(1)} %get-tuple-element.40), channel_id=1, source_target_pairs={{1,2},{2,1},{3,4},{4,3},{5,6},{6,5},{9,10},{10,9},{11,12},{12,11},... | collective-permute-start | bytes 211208 | tf_op jit(solution)/shard_map/ppermute | solution.py:32
  37.8 3.0 %shard_map.89 = (bf16[200,1536]{1,0:T(8,128)(2,1)S(1)}, f32[2,200,176]{2,1,0:T(8,128)S(1)}) custom-call(f32[2]{0:T(128)S(1)} %compare_select_fusion.2.weight, s32[1,1536]{1,0:T(1,128)S(1)} %bitcast.28, bf16[768,768]{1,0:T(8,128)(2,1)S(1)} %pad.14.stiffness, bf16[200,1408]{1,0:T(8,128)(2,1)S(1)} %get-tuple-element.37.values.refs_0_), custom_call_target="tpu_custom_call" | custom-call | flops 1553203200 | bytes 2645000 | tf_op jit(solution)/shard_map/pallas_call | solution.py:56
  40.8 0.0 collective-permute-done.4.refs_0_
  40.8 0.0 collective-permute-done.5.refs_1_
  40.8 0.3 shard_map.91
  41.1 0.1 collective-permute-start.6
  41.2 3.8 %collective-permute-start.7 = (bf16[200,176]{1,0:T(8,128)(2,1)S(1)}, bf16[200,176]{1,0:T(8,128)(2,1)S(1)}, u32[]{:S(2)}, u32[]{:S(2)}) collective-permute-start(bf16[200,176]{1,0:T(8,128)(2,1)S(1)} %get-tuple-element.43), channel_id=1, source_target_pairs={{1,2},{2,1},{3,4},{4,3},{5,6},{6,5},{9,10},{10,9},{11,12},{12,11},... | collective-permute-start | bytes 211208 | tf_op jit(solution)/shard_map/ppermute | solution.py:32
  44.9 1.8 %shard_map.90.total = f32[200,1408]{1,0:T(8,128)S(1)} custom-call(s32[1,1536]{1,0:T(1,128)S(1)} %bitcast.29, bf16[200,1536]{1,0:T(8,128)(2,1)S(1)} %get-tuple-element.38.product, bf16[2,176,1408]{2,1,0:T(8,128)(2,1)S(1)} %get-tuple-element.30.to_own, bf16[200,176]{1,0:T(8,128)(2,1)S(1)} %collective-permute-done.4.refs_0_, ...), custom_call_target="tpu_custom_call" | custom-call | flops 1063321600 | bytes 2878976 | tf_op jit(solution)/shard_map/pallas_call | solution.py:56
  46.8 0.0 collective-permute-done.6.refs_1_
  46.8 0.6 collective-permute-done.7.refs_2_
  47.3 1.2 %shard_map.92 = (bf16[200,1408]{1,0:T(8,128)(2,1)S(1)}, bf16[200,176]{1,0:T(8,128)(2,1)S(1)}, bf16[200,176]{1,0:T(8,128)(2,1)S(1)}) custom-call(s32[2,176]{1,0:T(2,128)S(1)} %pad.12.send_row, f32[1,1408]{1,0:T(1,128)S(1)} %copy-done.2, f32[200,1408]{1,0:T(8,128)S(1)} %shard_map.90.total, bf16[200,1408]{1,0:T(8,128)(2,1)S(1)} %get-tuple-element.37.values.refs_0_, ...), custom_call_target="tpu_custom_call" | custom-call | flops 396492800 | bytes 3104640 | tf_op jit(solution)/shard_map/pallas_call | solution.py:56
  48.5 0.1 collective-permute-start.8
  48.6 3.7 %collective-permute-start.9 = (bf16[200,176]{1,0:T(8,128)(2,1)S(1)}, bf16[200,176]{1,0:T(8,128)(2,1)S(1)}, u32[]{:S(2)}, u32[]{:S(2)}) collective-permute-start(bf16[200,176]{1,0:T(8,128)(2,1)S(1)} %get-tuple-element.47), channel_id=1, source_target_pairs={{1,2},{2,1},{3,4},{4,3},{5,6},{6,5},{9,10},{10,9},{11,12},{12,11},... | collective-permute-start | bytes 211208 | tf_op jit(solution)/shard_map/ppermute | solution.py:32
  52.3 3.0 %shard_map.93 = (bf16[200,1536]{1,0:T(8,128)(2,1)S(1)}, f32[2,200,176]{2,1,0:T(8,128)S(1)}) custom-call(f32[2]{0:T(128)S(1)} %compare_select_fusion.2.weight, s32[1,1536]{1,0:T(1,128)S(1)} %bitcast.30, bf16[768,768]{1,0:T(8,128)(2,1)S(1)} %pad.14.stiffness, bf16[200,1408]{1,0:T(8,128)(2,1)S(1)} %get-tuple-element.44.values), custom_call_target="tpu_custom_call" | custom-call | flops 1553203200 | bytes 2645000 | tf_op jit(solution)/shard_map/pallas_call | solution.py:56
  55.3 0.0 collective-permute-done.8.refs_0_
  55.3 0.0 collective-permute-done.9.refs_1_
  55.3 0.3 shard_map.95
  55.6 0.1 collective-permute-start.10
  55.6 3.3 %collective-permute-start.11 = (bf16[200,176]{1,0:T(8,128)(2,1)S(1)}, bf16[200,176]{1,0:T(8,128)(2,1)S(1)}, u32[]{:S(2)}, u32[]{:S(2)}) collective-permute-start(bf16[200,176]{1,0:T(8,128)(2,1)S(1)} %get-tuple-element.50), channel_id=1, source_target_pairs={{1,2},{2,1},{3,4},{4,3},{5,6},{6,5},{9,10},{10,9},{11,12},{12,11},... | collective-permute-start | bytes 211208 | tf_op jit(solution)/shard_map/ppermute | solution.py:32
  59.0 1.8 %shard_map.94.total = f32[200,1408]{1,0:T(8,128)S(1)} custom-call(s32[1,1536]{1,0:T(1,128)S(1)} %bitcast.31, bf16[200,1536]{1,0:T(8,128)(2,1)S(1)} %get-tuple-element.45.product, bf16[2,176,1408]{2,1,0:T(8,128)(2,1)S(1)} %get-tuple-element.30.to_own, bf16[200,176]{1,0:T(8,128)(2,1)S(1)} %collective-permute-done.8.refs_0_, ...), custom_call_target="tpu_custom_call" | custom-call | flops 1063321600 | bytes 2878976 | tf_op jit(solution)/shard_map/pallas_call | solution.py:56
  60.8 0.0 collective-permute-done.10.refs_1_
  60.8 0.8 %collective-permute-done.11.refs_2_ = bf16[200,176]{1,0:T(8,128)(2,1)S(1)} collective-permute-done((bf16[200,176]{1,0:T(8,128)(2,1)S(1)}, bf16[200,176]{1,0:T(8,128)(2,1)S(1)}, u32[]{:S(2)}, u32[]{:S(2)}) %collective-permute-start.11) | collective-permute-done | bytes 70432 | tf_op jit(solution)/shard_map/ppermute | solution.py:32
  61.6 1.6 %shard_map.96 = bf16[200,1408]{1,0:T(8,128)(2,1)} custom-call(s32[2,176]{1,0:T(2,128)S(1)} %pad.12.send_row, f32[1,1408]{1,0:T(1,128)S(1)} %copy-done.2, f32[200,1408]{1,0:T(8,128)S(1)} %shard_map.94.total, bf16[200,1408]{1,0:T(8,128)(2,1)S(1)} %get-tuple-element.44.values, bf16[200,1408]{1,0:T(8,128)(2,1)S(1)} %get-tuple-element.37.values.refs_0_, ...), custom_call_target="tpu_custom_call" | custom-call | flops 396492800 | bytes 2963840 | tf_op jit(solution)/shard_map/pallas_call | solution.py:56
  (16 shorter events, 0.1 us)
Async XLA Ops:
  0.7 1.4 %copy-start = (bf16[800,800]{1,0:T(8,128)(2,1)S(1)}, bf16[800,800]{1,0:T(8,128)(2,1)}, u32[]{:S(2)}) copy-start(bf16[800,800]{1,0:T(8,128)(2,1)} %rotation.1) | copy-start | bytes 3840004
  2.1 1.1 %copy-start.1 = (bf16[1,352,800]{1,2,0:T(8,128)(2,1)S(1)}, bf16[1,352,800]{1,2,0:T(8,128)(2,1)}, u32[]{:S(2)}) copy-start(bf16[1,352,800]{1,2,0:T(8,128)(2,1)} %param.8) | copy-start | bytes 1689604
  5.5 4.4 %copy-start.5 = (s32[1,4,162]{2,1,0:T(4,128)S(1)}, s32[1,4,162]{2,1,0:T(4,128)}, u32[]{:S(2)}) copy-start(s32[1,4,162]{2,1,0:T(4,128)} %param.14) | copy-start | bytes 7780
  5.5 4.4 %copy-start.4 = (s32[1,2,729]{2,1,0:T(2,128)S(1)}, s32[1,2,729]{2,1,0:T(2,128)}, u32[]{:S(2)}) copy-start(s32[1,2,729]{2,1,0:T(2,128)} %param.13) | copy-start | bytes 17500
  5.5 4.5 %copy-start.3 = (bf16[729,729]{1,0:T(8,128)(2,1)S(1)}, bf16[729,729]{1,0:T(8,128)(2,1)}, u32[]{:S(2)}) copy-start(bf16[729,729]{1,0:T(8,128)(2,1)} %param.10) | copy-start | bytes 3188650
  5.5 12.7 %all-to-all-start = ((bf16[4,200,352]{2,1,0:T(8,128)(2,1)}), bf16[4,200,352]{2,1,0:T(8,128)(2,1)S(1)}, u32[]{:S(2)}, u32[]{:S(2)}) async-start(bf16[4,200,352]{2,1,0:T(8,128)(2,1)} %shard_map.82), calls=%async_computation | async-start | bytes 1228800 | tf_op jit(solution)/shard_map/all_to_all | solution.py:199
  10.1 0.7 %copy-start.6 = (f32[1,2]{1,0:T(1,128)S(1)}, f32[1,2]{1,0:T(1,128)}, u32[]{:S(2)}) copy-start(f32[1,2]{1,0:T(1,128)} %param.11) | copy-start | bytes 28
  18.8 7.8 %collective-permute-start = (bf16[200,176]{1,0:T(8,128)(2,1)S(1)}, bf16[200,176]{1,0:T(8,128)(2,1)S(1)}, u32[]{:S(2)}, u32[]{:S(2)}) collective-permute-start(bf16[200,176]{1,0:T(8,128)(2,1)S(1)} %get-tuple-element.31), channel_id=1, source_target_pairs={{0,1},{1,0},{2,3},{3,2},{4,5},{5,4},{6,7},{7,6},{8,9},{9,8},{10,11... | collective-permute-start | bytes 211208 | tf_op jit(solution)/shard_map/ppermute | solution.py:32
  20.5 6.1 %collective-permute-start.1 = (bf16[200,176]{1,0:T(8,128)(2,1)S(1)}, bf16[200,176]{1,0:T(8,128)(2,1)S(1)}, u32[]{:S(2)}, u32[]{:S(2)}) collective-permute-start(bf16[200,176]{1,0:T(8,128)(2,1)S(1)} %get-tuple-element.32), channel_id=1, source_target_pairs={{1,2},{2,1},{3,4},{4,3},{5,6},{6,5},{9,10},{10,9},{11,12},{12,11},... | collective-permute-start | bytes 211208 | tf_op jit(solution)/shard_map/ppermute | solution.py:32
  26.9 5.5 %collective-permute-start.2 = (bf16[200,176]{1,0:T(8,128)(2,1)S(1)}, bf16[200,176]{1,0:T(8,128)(2,1)S(1)}, u32[]{:S(2)}, u32[]{:S(2)}) collective-permute-start(bf16[200,176]{1,0:T(8,128)(2,1)S(1)} %get-tuple-element.35), channel_id=1, source_target_pairs={{0,1},{1,0},{2,3},{3,2},{4,5},{5,4},{6,7},{7,6},{8,9},{9,8},{10,11... | collective-permute-start | bytes 211208 | tf_op jit(solution)/shard_map/ppermute | solution.py:32
  27.0 6.0 %collective-permute-start.3 = (bf16[200,176]{1,0:T(8,128)(2,1)S(1)}, bf16[200,176]{1,0:T(8,128)(2,1)S(1)}, u32[]{:S(2)}, u32[]{:S(2)}) collective-permute-start(bf16[200,176]{1,0:T(8,128)(2,1)S(1)} %get-tuple-element.36), channel_id=1, source_target_pairs={{1,2},{2,1},{3,4},{4,3},{5,6},{6,5},{9,10},{10,9},{11,12},{12,11},... | collective-permute-start | bytes 211208 | tf_op jit(solution)/shard_map/ppermute | solution.py:32
  30.5 2.4 %copy-start.2 = (f32[1,1408]{1,0:T(1,128)S(1)}, f32[1,1408]{1,0:T(1,128)}, u32[]{:S(2)}) copy-start(f32[1,1408]{1,0:T(1,128)} %potential.5) | copy-start | bytes 16900
  34.1 6.7 %collective-permute-start.4 = (bf16[200,176]{1,0:T(8,128)(2,1)S(1)}, bf16[200,176]{1,0:T(8,128)(2,1)S(1)}, u32[]{:S(2)}, u32[]{:S(2)}) collective-permute-start(bf16[200,176]{1,0:T(8,128)(2,1)S(1)} %get-tuple-element.39), channel_id=1, source_target_pairs={{0,1},{1,0},{2,3},{3,2},{4,5},{5,4},{6,7},{7,6},{8,9},{9,8},{10,11... | collective-permute-start | bytes 211208 | tf_op jit(solution)/shard_map/ppermute | solution.py:32
  34.2 6.7 %collective-permute-start.5 = (bf16[200,176]{1,0:T(8,128)(2,1)S(1)}, bf16[200,176]{1,0:T(8,128)(2,1)S(1)}, u32[]{:S(2)}, u32[]{:S(2)}) collective-permute-start(bf16[200,176]{1,0:T(8,128)(2,1)S(1)} %get-tuple-element.40), channel_id=1, source_target_pairs={{1,2},{2,1},{3,4},{4,3},{5,6},{6,5},{9,10},{10,9},{11,12},{12,11},... | collective-permute-start | bytes 211208 | tf_op jit(solution)/shard_map/ppermute | solution.py:32
  41.1 5.7 %collective-permute-start.6 = (bf16[200,176]{1,0:T(8,128)(2,1)S(1)}, bf16[200,176]{1,0:T(8,128)(2,1)S(1)}, u32[]{:S(2)}, u32[]{:S(2)}) collective-permute-start(bf16[200,176]{1,0:T(8,128)(2,1)S(1)} %get-tuple-element.42), channel_id=1, source_target_pairs={{0,1},{1,0},{2,3},{3,2},{4,5},{5,4},{6,7},{7,6},{8,9},{9,8},{10,11... | collective-permute-start | bytes 211208 | tf_op jit(solution)/shard_map/ppermute | solution.py:32
  41.2 6.2 %collective-permute-start.7 = (bf16[200,176]{1,0:T(8,128)(2,1)S(1)}, bf16[200,176]{1,0:T(8,128)(2,1)S(1)}, u32[]{:S(2)}, u32[]{:S(2)}) collective-permute-start(bf16[200,176]{1,0:T(8,128)(2,1)S(1)} %get-tuple-element.43), channel_id=1, source_target_pairs={{1,2},{2,1},{3,4},{4,3},{5,6},{6,5},{9,10},{10,9},{11,12},{12,11},... | collective-permute-start | bytes 211208 | tf_op jit(solution)/shard_map/ppermute | solution.py:32
  48.5 6.7 %collective-permute-start.8 = (bf16[200,176]{1,0:T(8,128)(2,1)S(1)}, bf16[200,176]{1,0:T(8,128)(2,1)S(1)}, u32[]{:S(2)}, u32[]{:S(2)}) collective-permute-start(bf16[200,176]{1,0:T(8,128)(2,1)S(1)} %get-tuple-element.46), channel_id=1, source_target_pairs={{0,1},{1,0},{2,3},{3,2},{4,5},{5,4},{6,7},{7,6},{8,9},{9,8},{10,11... | collective-permute-start | bytes 211208 | tf_op jit(solution)/shard_map/ppermute | solution.py:32
  48.6 6.7 %collective-permute-start.9 = (bf16[200,176]{1,0:T(8,128)(2,1)S(1)}, bf16[200,176]{1,0:T(8,128)(2,1)S(1)}, u32[]{:S(2)}, u32[]{:S(2)}) collective-permute-start(bf16[200,176]{1,0:T(8,128)(2,1)S(1)} %get-tuple-element.47), channel_id=1, source_target_pairs={{1,2},{2,1},{3,4},{4,3},{5,6},{6,5},{9,10},{10,9},{11,12},{12,11},... | collective-permute-start | bytes 211208 | tf_op jit(solution)/shard_map/ppermute | solution.py:32
  55.6 5.3 %collective-permute-start.10 = (bf16[200,176]{1,0:T(8,128)(2,1)S(1)}, bf16[200,176]{1,0:T(8,128)(2,1)S(1)}, u32[]{:S(2)}, u32[]{:S(2)}) collective-permute-start(bf16[200,176]{1,0:T(8,128)(2,1)S(1)} %get-tuple-element.49), channel_id=1, source_target_pairs={{0,1},{1,0},{2,3},{3,2},{4,5},{5,4},{6,7},{7,6},{8,9},{9,8},{10,11... | collective-permute-start | bytes 211208 | tf_op jit(solution)/shard_map/ppermute | solution.py:32
  55.6 6.0 %collective-permute-start.11 = (bf16[200,176]{1,0:T(8,128)(2,1)S(1)}, bf16[200,176]{1,0:T(8,128)(2,1)S(1)}, u32[]{:S(2)}, u32[]{:S(2)}) collective-permute-start(bf16[200,176]{1,0:T(8,128)(2,1)S(1)} %get-tuple-element.50), channel_id=1, source_target_pairs={{1,2},{2,1},{3,4},{4,3},{5,6},{6,5},{9,10},{10,9},{11,12},{12,11},... | collective-permute-start | bytes 211208 | tf_op jit(solution)/shard_map/ppermute | solution.py:32

commit v2 on v1

v2 whole, which is shorter than its diff:
```python
import functools

import jax
import jax.numpy as jnp
from jax import lax
from jax.experimental import pallas as pl
from jax.experimental.pallas import tpu as pltpu
from jax.sharding import PartitionSpec as P

DEGREE = 8
FILTER_STEPS = 3
FACE_NODES = 81

OFFSETS = (1, 8, -8, -1)
CENTER = 5.0
HALF_WIDTH = 5.0
BF16 = jnp.bfloat16
F32 = jnp.float32
VMEM = pl.BlockSpec(memory_space=pltpu.VMEM)
ANY = pl.BlockSpec(memory_space=pl.ANY)
LANES = 128
ROTATE_VMEM = 56 << 20
HEAD = 768


def round_up(value, multiple):
    return -(-value // multiple) * multiple


def swap(value, first):
    domains = lax.axis_size("dom")
    pairs = []
    for low in range(first, domains - 1, 2):
        pairs += [(low, low + 1), (low + 1, low)]
    return lax.ppermute(value, "dom", pairs)


def shift(value, by):
    domains = lax.axis_size("dom")
    pairs = [(i, i + by) for i in range(domains) if 0 <= i + by < domains]
    return lax.ppermute(value, "dom", pairs)


def far_groups(domains):
    return [g for g, offset in enumerate(OFFSETS) if abs(offset) > 1 and abs(offset) < domains]


def exchange(blocks, to_owner):
    out = [swap(blocks[0], 1)]
    for block, group in zip(blocks[1:], far_groups(lax.axis_size("dom"))):
        out.append(shift(block, OFFSETS[group] if to_owner else -OFFSETS[group]))
    return out


def call(kernel, out_shape, args, flops, scratch=(), in_specs=None, vmem=24 << 20):
    outs = out_shape if isinstance(out_shape, (tuple, list)) else (out_shape,)
    size = sum(a.size * a.dtype.itemsize for a in list(args) + list(outs))
    return pl.pallas_call(
        kernel,
        out_shape=out_shape,
        in_specs=in_specs or [VMEM] * len(args),
        out_specs=jax.tree.map(lambda _: VMEM, out_shape),
        scratch_shapes=list(scratch),
        cost_estimate=pl.CostEstimate(flops=flops, bytes_accessed=size, transcendentals=0),
        compiler_params=pltpu.CompilerParams(vmem_limit_bytes=vmem),
    )(*args)


def shape(dims, dtype):
    return jax.ShapeDtypeStruct(dims, dtype)


def mm(a, b):
    return jnp.dot(a, b, preferred_element_type=F32)


def mm_nt(a, b):
    return lax.dot_general(a, b, (((1,), (1,)), ((), ())), preferred_element_type=F32)


def rows_hot(index, first, count):
    rows = lax.broadcasted_iota(jnp.int32, (count, index.shape[1]), 0) + first
    return (rows == index).astype(BF16)


def steps(total, size):
    return [(i, min(size, total - i)) for i in range(0, total, size)]


def rotate_kernel(piece, rotation, *refs):
    outs, (piece_held, rotation_held, groups, sems) = refs[:-4], refs[-4:]
    copies = (
        pltpu.make_async_copy(rotation, rotation_held, sems.at[0]),
        pltpu.make_async_copy(piece, piece_held, sems.at[1]),
    )
    for copy in copies:
        copy.start()
    for copy in copies:
        copy.wait()
    rotated = lax.dot_general(
        rotation_held[...], piece_held[...], (((0,), (0,)), ((), ())), preferred_element_type=F32
    )
    width = groups.shape[1]
    for group in range(groups.shape[0]):
        groups[group] = rotated[group * width : (group + 1) * width, :].astype(BF16)
    mine = lax.axis_index("band")
    for k, out in enumerate(outs):
        out[...] = groups[mine ^ k]


def columns_hot(index, capacity, hot):
    turned = jnp.broadcast_to(index, (LANES, index.shape[1])).T
    for i, n in steps(capacity, LANES):
        lanes = lax.broadcasted_iota(jnp.int32, (turned.shape[0], n), 1) + i
        hot[:, i : i + n] = (turned[:, :n] == lanes).astype(BF16)


def couple_kernel(capacity, weight, node_row, stiffness, to_ghost, to_own, scatter, local):
    nodes = stiffness.shape[0]
    ghosts = to_own.shape[0]
    slots = to_ghost.shape[2]
    for i, n in steps(node_row.shape[1], nodes):
        picks = rows_hot(node_row[:, i : i + n], capacity, ghosts)
        local[:, i : i + n] = (mm(picks, stiffness[...]) * weight[:, i : i + n]).astype(BF16)
    columns_hot(node_row[...], capacity, scatter)
    for block in range(to_ghost.shape[0]):
        picks = rows_hot(node_row[...], capacity + block * slots, slots)
        to_ghost[block] = mm_nt(local[...], picks).astype(BF16)
    for i, n in steps(capacity, 256):
        to_own[:, i : i + n] = mm(local[...], scatter[:, i : i + n]).astype(BF16)


def pick_rows(send_row, block, values, out):
    picks = rows_hot(send_row[block : block + 1, :], 0, values.shape[1])
    out[...] = mm(values[...], picks).astype(BF16)


def join_kernel(send_row, keep, after, *refs):
    bands = refs[-1].shape[0]
    pieces, (values, near_picked, held) = refs[:bands], refs[bands:]
    mine = lax.axis_index("band")
    for k, piece in enumerate(pieces):
        held[mine ^ k] = piece[...]
    joined = jnp.concatenate([held[p] for p in range(bands)], axis=1)
    values[...] = jnp.where(keep[...] > 0, joined.astype(F32), 0.0).astype(BF16)
    pick_rows(send_row, 0, values, near_picked)


def terms_kernel(send_row, to_own, values, terms, *picked):
    slots = terms.shape[2]
    for block, out in enumerate(picked):
        pick_rows(send_row, block + 1, values, out)
    for block in range(terms.shape[0]):
        terms[block] = mm_nt(values[...], to_own[block * slots : (block + 1) * slots, :])


def cells_kernel(first_step, weight, node_row, stiffness, scatter, potential, values, after, *refs):
    refs = list(refs)
    previous = None if first_step else refs.pop(0)
    product, head, *locals_ = refs
    capacity = values.shape[1]
    nodes = stiffness.shape[0]
    parts = steps(product.shape[1], nodes)
    for (i, n), local in zip(parts, locals_):
        local[...] = mm(values[...], rows_hot(node_row[:, i : i + n], 0, capacity)).astype(BF16)
    for (i, n), local in zip(parts, locals_):
        product[:, i : i + n] = (mm(local[...], stiffness[...]) * weight[:, i : i + n]).astype(BF16)
    for i, n in steps(head.shape[1], 256):
        at = slice(i, i + n)
        sums = mm(product[...], scatter[:, at])
        head[:, at] = own_columns(first_step, at, sums, potential, values, previous)


def ghost_sum(block, terms, to_ghost, arrived):
    slots = terms.shape[2]
    total = terms[block]
    for other, values in arrived:
        total = total + mm(values, to_ghost[block, other * slots : (other + 1) * slots, :])
    return total.astype(BF16)


def ghost_kernel(terms, to_ghost, *refs):
    blocks = terms.shape[0]
    arrived = [(other, refs[other][...]) for other in range(blocks)]
    for block in range(blocks):
        refs[blocks + block][...] = ghost_sum(block, terms, to_ghost, arrived)


def parcel_kernel(terms, to_ghost, near_ghosts, far_picked, parcel):
    width, slots = far_picked.shape
    sums = ghost_sum(1, terms, to_ghost, [(0, near_ghosts[...])])
    parcel[:width, :] = jnp.concatenate([far_picked[...], sums], axis=1)
    if parcel.shape[0] > width:
        parcel[width:, :] = jnp.zeros((parcel.shape[0] - width, 2 * slots), BF16)
        first = parcel.shape[0] - slots
        parcel[first:, :slots] = to_ghost[1, slots : 2 * slots, :]


def near_kernel(terms, to_ghost, near_ghosts, parcel, after, out):
    width, slots = out.shape
    arrived = [(0, near_ghosts[...]), (1, parcel[:width, :slots])]
    out[...] = ghost_sum(0, terms, to_ghost, arrived)


def scale_of(first_step):
    return (1.0 if first_step else 2.0) / HALF_WIDTH


def own_columns(first_step, at, sums, potential, values, previous):
    shifted = sums + (potential[:, at] - CENTER) * values[:, at].astype(F32)
    result = shifted * scale_of(first_step)
    return result if first_step else result - previous[:, at].astype(F32)


def own_kernel(first_step, product, scatter, to_own, potential, values, head, *refs):
    refs = list(refs)
    previous = None if first_step else refs.pop(0)
    arrived, out = refs[:-1], refs[-1]
    ghosts = jnp.concatenate([ghost[...] for ghost in arrived], axis=1)
    for i, n in steps(out.shape[1], 256):
        at = slice(i, i + n)
        sums = mm(ghosts, to_own[:, at])
        if i < head.shape[1]:
            out[:, at] = head[:, at] + sums * scale_of(first_step)
        else:
            sums = sums + mm(product[...], scatter[:, at])
            out[:, at] = own_columns(first_step, at, sums, potential, values, previous)


def paired_own_kernel(
    first_step, product, scatter, to_own, potential, values, head, send_row, near_ghosts, far_picked, parcel, first_parcel, *refs
):
    previous, out = (None if first_step else refs[0]), refs[-1]
    width, slots = far_picked.shape
    ghosts = jnp.concatenate([near_ghosts[...], parcel[:width, :slots]], axis=1)
    coupling = first_parcel[first_parcel.shape[0] - slots :, :slots]
    returned = parcel[:width, slots:].astype(F32) + mm(far_picked[...], coupling)
    returned = returned.astype(BF16)
    for i, n in steps(out.shape[1], 256):
        at = slice(i, i + n)
        sums = mm(ghosts, to_own[:, at]) + mm_nt(returned, rows_hot(send_row[1:2, :], i, n))
        if i < head.shape[1]:
            out[:, at] = head[:, at] + sums * scale_of(first_step)
        else:
            sums = sums + mm(product[...], scatter[:, at])
            out[:, at] = own_columns(first_step, at, sums, potential, values, previous)


def update_kernel(blocks, first_step, last_step, send_row, total, *refs):
    arrived, out, picked = refs[:blocks], refs[blocks], refs[blocks + 1 :]
    for i, n in steps(out.shape[1], 256):
        at = slice(i, i + n)
        added = 0.0
        for block in range(blocks):
            added = added + mm_nt(arrived[block][...], rows_hot(send_row[block : block + 1, :], i, n))
        out[:, at] = (total[:, at] + added * scale_of(first_step)).astype(BF16)
    if not last_step:
        pick_rows(send_row, 0, out, picked[0])


def shards(
    orbitals, rotation, cell_stiffness, cell_scale, potential, cell_nodes, send_rows, domain_rows
):
    domains = lax.axis_size("dom")
    bands = lax.axis_size("band")
    domain = lax.axis_index("dom")
    row_piece = orbitals[0]
    piece_rows, columns = row_piece.shape
    own_rows = domain_rows[0]
    width = columns // bands
    piece_shapes = (shape((width, piece_rows), BF16),) * bands
    pieces = list(call(
        rotate_kernel,
        piece_shapes,
        (row_piece.T, rotation),
        2 * piece_rows * columns * columns,
        scratch=[
            pltpu.VMEM((columns, piece_rows), BF16),
            pltpu.VMEM((columns, columns), BF16),
            pltpu.VMEM((bands, width, piece_rows), BF16),
            pltpu.SemaphoreType.DMA((2,)),
        ],
        in_specs=[ANY, ANY],
        vmem=ROTATE_VMEM,
    ))
    for k in reversed(range(1, bands)):
        pieces[k] = lax.ppermute(pieces[k], "band", [(i, i ^ k) for i in range(bands)])

    capacity = potential.shape[1]
    cells, nodes = cell_nodes.shape[1:]
    slots = send_rows.shape[2]
    nodes_pad = round_up(nodes, 256)
    slots_pad = round_up(slots, 16)
    far = far_groups(domains)
    blocks = 2 + len(far)
    ghosts = blocks * slots_pad
    even = domain % 2 == 0
    send_lists = [
        jnp.where(even, send_rows[0, 3], send_rows[0, 0]),
        jnp.where(even, send_rows[0, 0], send_rows[0, 3]),
    ] + [send_rows[0, g] for g in far]
    send_row = jnp.pad(
        jnp.stack(send_lists), ((0, 0), (0, slots_pad - slots)), constant_values=capacity
    )
    group = (cell_nodes[0] - capacity) // slots
    slot = (cell_nodes[0] - capacity) % slots
    block = jnp.where((group == 0) == even, 0, 1)
    for pos, g in enumerate(far):
        block = jnp.where(group == g, 2 + pos, block)
    ghost_index = capacity + block * slots_pad + slot
    node_list = jnp.where(cell_nodes[0] < capacity, cell_nodes[0], ghost_index)
    node_list = jnp.pad(
        node_list, ((0, 0), (0, nodes_pad - nodes)), constant_values=capacity + ghosts
    ).reshape(-1)
    node_row = node_list[None, :]
    stiffness = jnp.pad(cell_stiffness, ((0, nodes_pad - nodes), (0, nodes_pad - nodes)))

    cell_total = (own_rows - FACE_NODES) // (DEGREE * FACE_NODES)
    cell_live = jnp.arange(cell_scale.shape[1], dtype=jnp.int32) < cell_total
    weight = jnp.where(cell_live, cell_scale[0], jnp.zeros_like(cell_scale[0]))
    weight = jnp.repeat(weight, nodes_pad)[None, :]

    local_rows = cells * nodes_pad
    cell_flops = 2 * local_rows * nodes_pad
    to_ghost, to_own, scatter = call(
        functools.partial(couple_kernel, capacity),
        (
            shape((blocks, ghosts, slots_pad), BF16),
            shape((ghosts, capacity), BF16),
            shape((local_rows, capacity), BF16),
        ),
        (weight, node_row, stiffness),
        (cell_flops + 2 * local_rows * (ghosts + capacity)) * ghosts,
        scratch=[pltpu.VMEM((ghosts, local_rows), BF16)],
    )
    block_shape = shape((width, slots_pad), BF16)
    keep = (jnp.arange(capacity, dtype=jnp.int32) < own_rows).astype(jnp.int32)[None, :]
    current, near_picked = call(
        join_kernel,
        (shape((width, capacity), BF16), block_shape),
        (send_row, keep, to_ghost, *pieces),
        2 * slots_pad * capacity * width,
        scratch=[pltpu.VMEM((bands, width, piece_rows), BF16)],
        in_specs=[VMEM, VMEM, ANY] + [VMEM] * bands,
    )
    head_columns = min(HEAD, capacity)
    previous = None
    parcel_rows = round_up(width, 16) + slots_pad
    first_parcel = None
    for filter_step in range(FILTER_STEPS):
        first, last = filter_step == 0, filter_step == FILTER_STEPS - 1
        near = swap(near_picked, 0)
        terms, *picked = call(
            terms_kernel,
            (shape((blocks, width, slots_pad), F32),) + (block_shape,) * (blocks - 1),
            (send_row, to_own, current),
            4 * ghosts * capacity * width,
        )
        if far:
            arrived = [near, *exchange(picked, False)]
            ready = terms
        else:
            parcel = call(
                parcel_kernel,
                shape((parcel_rows if first else width, 2 * slots_pad), BF16),
                (terms, to_ghost, near, picked[0]),
                2 * slots_pad * slots_pad * width,
            )
            ready = parcel
            parcel = swap(parcel, 1)
            first_parcel = parcel if first else first_parcel
        history = () if first else (previous,)
        product, head = call(
            functools.partial(cells_kernel, first),
            (shape((width, local_rows), BF16), shape((width, head_columns), F32)),
            (weight, node_row, stiffness, scatter, potential, current, ready, *history),
            (cell_flops + 2 * local_rows * (capacity + head_columns)) * width,
            scratch=[pltpu.VMEM((width, nodes_pad), BF16)] * cells,
            in_specs=[VMEM] * 6 + [ANY] + [VMEM] * len(history),
        )
        own_flops = 2 * ((capacity - head_columns) * local_rows + capacity * ghosts) * width
        own_operands = (product, scatter, to_own, potential, current, head)
        if far:
            sums = call(
                ghost_kernel,
                (block_shape,) * blocks,
                (terms, to_ghost, *arrived),
                2 * ghosts * ghosts * width,
            )
            returned = [swap(sums[0], 0), *exchange(sums[1:], True)]
            total = call(
                functools.partial(own_kernel, first),
                shape((width, capacity), F32),
                (*own_operands, *history, *arrived),
                own_flops,
            )
        else:
            sums = call(
                near_kernel,
                block_shape,
                (terms, to_ghost, near, parcel, head),
                2 * ghosts * slots_pad * width,
                in_specs=[VMEM] * 4 + [ANY],
            )
            returned = [swap(sums, 0)]
            total = call(
                functools.partial(paired_own_kernel, first),
                shape((width, capacity), F32),
                (*own_operands, send_row, near, picked[0], parcel, first_parcel, *history),
                own_flops,
            )
        following, *near_next = call(
            functools.partial(update_kernel, len(returned), first, last),
            (shape((width, capacity), BF16),) + (() if last else (block_shape,)),
            (send_row, total, *returned),
            2 * capacity * (ghosts + slots_pad * len(returned)) * width,
        )
        previous, current = current, following
        near_picked = near_next[0] if near_next else None
    return current.T[None]


def solution(mesh):
    return jax.shard_map(
        shards,
        mesh=mesh,
        in_specs=(
            P("dom", "band", None),
            P(),
            P(),
            P("dom", None),
            P("dom", None),
            P("dom", None, None),
            P("dom", None, None),
            P("dom"),
        ),
        out_specs=P("dom", None, "band"),
        check_vma=False,
    )
```

time: 63.6 us -> 50.8 us (0.80)
  starting transfers between devices: 27.6 us -> 16.9 us
  local copies, waits for them, and re-layouts: 3.11 us -> 0.23 us
  waiting for transfers between devices: 4.42 us -> 6.25 us
  Pallas kernels: 27 us -> 25.7 us
    ppermute x12 -> x9, starting transfers between devices: 23.2 us -> 13.6 us  [swap(): return lax.ppermute(value, 'dom', pairs)]
    all_to_all x1 -> x0, starting transfers between devices: 4.4 us -> none  [shards(): lax.all_to_all(rotated, 'band', split_axis=0, concat_axis=0, tiled=True)]
    ppermute x0 -> x3, starting transfers between devices: none -> 3.37 us  [shards(): lax.ppermute(pieces[k], 'band', [(i, i ^ k) for i in range(bands)])]
    unnamed x16, local copies, waits for them, and re-layouts: 3 us -> 0.12 us
    all_to_all x1 -> x0, waiting for transfers between devices: 2.48 us -> none  [shards(): lax.all_to_all(rotated, 'band', split_axis=0, concat_axis=0, tiled=True)]
    ppermute x12 -> x9, waiting for transfers between devices: 1.94 us -> 4.14 us  [swap(): return lax.ppermute(value, 'dom', pairs)]
    ppermute x0 -> x3, waiting for transfers between devices: none -> 2.11 us  [shards(): lax.ppermute(pieces[k], 'band', [(i, i ^ k) for i in range(bands)])]
    pallas_call x15 -> x21, Pallas kernels: 27 us -> 25.7 us  [call(): pl.pallas_call(kernel, out_shape=out_shape, in_specs=in_specs or [VMEM] *...]
  transfers between devices with their start and end apart: 13 -> 12, of which waited for: 4 -> 7; matrix products, arithmetic and copies ran while one was open for 0% -> 1% of each run, Pallas kernels for 31% -> 35%
where the time goes in v2:
time: 50.8 us; the launch traced here: 50.2 us
  Pallas kernels  25.7 us (51%)
  starting transfers between devices  16.9 us (33%)
  waiting for transfers between devices  6.25 us (12%)
  between operations  1.04 us (2%)
    pallas_call x21, Pallas kernels, call(): pl.pallas_call(kernel, out_shape=out_shape, in_specs=in_specs or [VMEM] *...  25.7 us
    ppermute x9, starting transfers between devices, swap(): return lax.ppermute(value, 'dom', pairs)  13.6 us
    ppermute x9, waiting for transfers between devices, swap(): return lax.ppermute(value, 'dom', pairs)  4.14 us
    ppermute x3, starting transfers between devices, shards(): lax.ppermute(pieces[k], 'band', [(i, i ^ k) for i in range(bands)])  3.37 us
    ppermute x3, waiting for transfers between devices, shards(): lax.ppermute(pieces[k], 'band', [(i, i ^ k) for i in range(bands)])  2.11 us
  transfers between devices with their start and end apart: 12, of which 7 were waited for; matrix products, arithmetic and copies ran while one was open for 1% of the time, Pallas kernels for 35%

profile of v2, /device:TPU:1, one launch (start us, length us, event | category | flops | bytes accessed | tf_op | source)
XLA Modules:
  0.0 50.2 jit_solution(6054628529553900750)
XLA Ops:
  0.0 3.5 %shard_map.83 = (bf16[200,352]{1,0:T(8,128)(2,1)}, bf16[200,352]{1,0:T(8,128)(2,1)}, bf16[200,352]{1,0:T(8,128)(2,1)}, bf16[200,352]{1,0:T(8,128)(2,1)}) custom-call(bf16[800,352]{1,0:T(8,128)(2,1)} %bitcast.36, bf16[800,800]{1,0:T(8,128)(2,1)} %rotation.1), custom_call_target="tpu_custom_call" | custom-call | flops 450560000 | bytes 2406400 | tf_op jit(solution)/shard_map/pallas_call | solution.py:58
  3.5 2.1 %collective-permute-start = (bf16[200,352]{1,0:T(8,128)(2,1)}, bf16[200,352]{1,0:T(8,128)(2,1)S(1)}, u32[]{:S(2)}, u32[]{:S(2)}) collective-permute-start(bf16[200,352]{1,0:T(8,128)(2,1)} %get-tuple-element.33), channel_id=1, source_target_pairs={{0,8},{8,0},{16,24},{24,16},{1,9},{9,1},{17,25},{25,17},{2,10},{10... | collective-permute-start | bytes 422408 | tf_op jit(solution)/shard_map/ppermute | solution.py:287
  5.6 1.2 %collective-permute-start.1 = (bf16[200,352]{1,0:T(8,128)(2,1)}, bf16[200,352]{1,0:T(8,128)(2,1)S(1)}, u32[]{:S(2)}, u32[]{:S(2)}) collective-permute-start(bf16[200,352]{1,0:T(8,128)(2,1)} %get-tuple-element.34), channel_id=1, source_target_pairs={{0,16},{8,24},{16,0},{24,8},{1,17},{9,25},{17,1},{25,9},{2,18},{10... | collective-permute-start | bytes 422408 | tf_op jit(solution)/shard_map/ppermute | solution.py:287
  6.9 0.0 collective-permute-start.2
  7.7 0.1 broadcast_bitcast_fusion
  7.8 0.1 pad.14.stiffness
  7.9 0.0 copy-start
  7.9 4.0 %shard_map.82 = (bf16[2,352,176]{2,1,0:T(8,128)(2,1)S(1)}, bf16[352,1408]{1,0:T(8,128)(2,1)S(1)}, bf16[1536,1408]{1,0:T(8,128)(2,1)S(1)}) custom-call(f32[1,1536]{1,0:T(1,128)S(1)} %bitcast.32, s32[1,1536]{1,0:T(1,128)S(1)} %bitcast.28, bf16[768,768]{1,0:T(8,128)(2,1)S(1)} %pad.14.stiffness), custom_call_target="tpu_custom_call" | custom-call | flops 2733637632 | bytes 6756352 | tf_op jit(solution)/shard_map/pallas_call | solution.py:58
  11.9 0.0 collective-permute-done.refs_1_
  11.9 0.0 collective-permute-done.1.refs_2_
  12.0 2.1 %collective-permute-done.2.refs_3_ = bf16[200,352]{1,0:T(8,128)(2,1)S(1)} collective-permute-done((bf16[200,352]{1,0:T(8,128)(2,1)}, bf16[200,352]{1,0:T(8,128)(2,1)S(1)}, u32[]{:S(2)}, u32[]{:S(2)}) %collective-permute-start.2) | collective-permute-done | bytes 140832 | tf_op jit(solution)/shard_map/ppermute | solution.py:287
  14.1 0.5 %shard_map.84 = (bf16[200,1408]{1,0:T(8,128)(2,1)S(1)}, bf16[200,176]{1,0:T(8,128)(2,1)S(1)}) custom-call(s32[2,176]{1,0:T(2,128)S(1)} %pad.12.send_row, s32[1,1408]{1,0:T(1,128)S(1)} %compare_convert_fusion.keep, bf16[2,352,176]{2,1,0:T(8,128)(2,1)S(1)} %get-tuple-element.31.after.to_ghost, bf16[200,352]{1,0:T(8,128)(2,1)S(1)} %copy-done, ...), custom_call_target="tpu_custom_call" | custom-call | flops 99123200 | bytes 1451648 | tf_op jit(solution)/shard_map/pallas_call | solution.py:58
  14.6 1.5 %collective-permute-start.3 = (bf16[200,176]{1,0:T(8,128)(2,1)S(1)}, bf16[200,176]{1,0:T(8,128)(2,1)S(1)}, u32[]{:S(2)}, u32[]{:S(2)}) collective-permute-start(bf16[200,176]{1,0:T(8,128)(2,1)S(1)} %get-tuple-element.39), channel_id=1, source_target_pairs={{0,1},{1,0},{2,3},{3,2},{4,5},{5,4},{6,7},{7,6},{8,9},{9,8},{10,11... | collective-permute-start | bytes 211208 | tf_op jit(solution)/shard_map/ppermute | solution.py:35
  16.1 0.7 %shard_map.85 = (f32[2,200,176]{2,1,0:T(8,128)S(1)}, bf16[200,176]{1,0:T(8,128)(2,1)S(1)}) custom-call(s32[2,176]{1,0:T(2,128)S(1)} %pad.12.send_row, bf16[352,1408]{1,0:T(8,128)(2,1)S(1)} %get-tuple-element.37.to_own, bf16[200,1408]{1,0:T(8,128)(2,1)S(1)} %get-tuple-element.36.values.refs_0_), custom_call_target="tpu_custom_call" | custom-call | flops 396492800 | bytes 1907840 | tf_op jit(solution)/shard_map/pallas_call | solution.py:58
  16.8 0.3 collective-permute-done.3.near_ghosts
  17.1 0.2 shard_map.86.after
  17.3 3.4 %collective-permute-start.4 = (bf16[384,352]{1,0:T(8,128)(2,1)S(1)}, bf16[384,352]{1,0:T(8,128)(2,1)S(1)}, u32[]{:S(2)}, u32[]{:S(2)}) collective-permute-start(bf16[384,352]{1,0:T(8,128)(2,1)S(1)} %shard_map.86.after), channel_id=1, source_target_pairs={{1,2},{2,1},{3,4},{4,3},{5,6},{6,5},{9,10},{10,9},{11,12},{12,11},... | collective-permute-start | bytes 811016 | tf_op jit(solution)/shard_map/ppermute | solution.py:35
  20.8 2.4 %shard_map.87 = (bf16[200,1536]{1,0:T(8,128)(2,1)S(1)}, f32[200,768]{1,0:T(8,128)S(1)}) custom-call(f32[1,1536]{1,0:T(1,128)S(1)} %bitcast.33, s32[1,1536]{1,0:T(1,128)S(1)} %bitcast.29, bf16[768,768]{1,0:T(8,128)(2,1)S(1)} %pad.14.stiffness, bf16[1536,1408]{1,0:T(8,128)(2,1)S(1)} %get-tuple-element.30.scatter, f32[1,1408]{1,0:T(1,128)S(1)} %copy-done.1, ...), custom_call_target="tpu_custom_call" | custom-call | flops 1808793600 | bytes 7585280 | tf_op jit(solution)/shard_map/pallas_call | solution.py:58
  23.1 2.2 %collective-permute-done.4.parcel.first_parcel = bf16[384,352]{1,0:T(8,128)(2,1)S(1)} collective-permute-done((bf16[384,352]{1,0:T(8,128)(2,1)S(1)}, bf16[384,352]{1,0:T(8,128)(2,1)S(1)}, u32[]{:S(2)}, u32[]{:S(2)}) %collective-permute-start.4) | collective-permute-done | bytes 270368 | tf_op jit(solution)/shard_map/ppermute | solution.py:35
  25.4 0.2 shard_map.89
  25.6 0.1 collective-permute-start.5
  25.7 1.5 %shard_map.88.total = f32[200,1408]{1,0:T(8,128)S(1)} custom-call(bf16[200,1536]{1,0:T(8,128)(2,1)S(1)} %get-tuple-element.41.product, bf16[1536,1408]{1,0:T(8,128)(2,1)S(1)} %get-tuple-element.30.scatter, bf16[352,1408]{1,0:T(8,128)(2,1)S(1)} %get-tuple-element.37.to_own, f32[1,1408]{1,0:T(1,128)S(1)} %copy-done.1, ...), custom_call_target="tpu_custom_call" | custom-call | flops 591462400 | bytes 8923520 | tf_op jit(solution)/shard_map/pallas_call | solution.py:58
  27.2 0.0 collective-permute-done.5.refs_0_
  27.2 0.7 %shard_map.90 = (bf16[200,1408]{1,0:T(8,128)(2,1)S(1)}, bf16[200,176]{1,0:T(8,128)(2,1)S(1)}) custom-call(s32[2,176]{1,0:T(2,128)S(1)} %pad.12.send_row, f32[200,1408]{1,0:T(8,128)S(1)} %shard_map.88.total, bf16[200,176]{1,0:T(8,128)(2,1)S(1)} %collective-permute-done.5.refs_0_), custom_call_target="tpu_custom_call" | custom-call | flops 297369600 | bytes 1831808 | tf_op jit(solution)/shard_map/pallas_call | solution.py:58
  27.9 0.6 %collective-permute-start.6 = (bf16[200,176]{1,0:T(8,128)(2,1)S(1)}, bf16[200,176]{1,0:T(8,128)(2,1)S(1)}, u32[]{:S(2)}, u32[]{:S(2)}) collective-permute-start(bf16[200,176]{1,0:T(8,128)(2,1)S(1)} %get-tuple-element.45), channel_id=1, source_target_pairs={{0,1},{1,0},{2,3},{3,2},{4,5},{5,4},{6,7},{7,6},{8,9},{9,8},{10,11... | collective-permute-start | bytes 211208 | tf_op jit(solution)/shard_map/ppermute | solution.py:35
  28.5 0.7 %shard_map.91 = (f32[2,200,176]{2,1,0:T(8,128)S(1)}, bf16[200,176]{1,0:T(8,128)(2,1)S(1)}) custom-call(s32[2,176]{1,0:T(2,128)S(1)} %pad.12.send_row, bf16[352,1408]{1,0:T(8,128)(2,1)S(1)} %get-tuple-element.37.to_own, bf16[200,1408]{1,0:T(8,128)(2,1)S(1)} %get-tuple-element.43.values.refs_0_), custom_call_target="tpu_custom_call" | custom-call | flops 396492800 | bytes 1907840 | tf_op jit(solution)/shard_map/pallas_call | solution.py:58
  29.2 0.3 collective-permute-done.6.near_ghosts
  29.4 0.2 shard_map.92.after
  29.7 3.6 %collective-permute-start.7 = (bf16[200,352]{1,0:T(8,128)(2,1)S(1)}, bf16[200,352]{1,0:T(8,128)(2,1)S(1)}, u32[]{:S(2)}, u32[]{:S(2)}) collective-permute-start(bf16[200,352]{1,0:T(8,128)(2,1)S(1)} %shard_map.92.after), channel_id=1, source_target_pairs={{1,2},{2,1},{3,4},{4,3},{5,6},{6,5},{9,10},{10,9},{11,12},{12,11},... | collective-permute-start | bytes 422408 | tf_op jit(solution)/shard_map/ppermute | solution.py:35
  33.3 2.4 %shard_map.93 = (bf16[200,1536]{1,0:T(8,128)(2,1)S(1)}, f32[200,768]{1,0:T(8,128)S(1)}) custom-call(f32[1,1536]{1,0:T(1,128)S(1)} %bitcast.34, s32[1,1536]{1,0:T(1,128)S(1)} %bitcast.30, bf16[768,768]{1,0:T(8,128)(2,1)S(1)} %pad.14.stiffness, bf16[1536,1408]{1,0:T(8,128)(2,1)S(1)} %get-tuple-element.30.scatter, f32[1,1408]{1,0:T(1,128)S(1)} %copy-done.1, ...), custom_call_target="tpu_custom_call" | custom-call | flops 1808793600 | bytes 8018944 | tf_op jit(solution)/shard_map/pallas_call | solution.py:58
  35.7 0.5 %collective-permute-done.7.parcel = bf16[200,352]{1,0:T(8,128)(2,1)S(1)} collective-permute-done((bf16[200,352]{1,0:T(8,128)(2,1)S(1)}, bf16[200,352]{1,0:T(8,128)(2,1)S(1)}, u32[]{:S(2)}, u32[]{:S(2)}) %collective-permute-start.7) | collective-permute-done | bytes 140832 | tf_op jit(solution)/shard_map/ppermute | solution.py:35
  36.2 0.2 shard_map.95
  36.4 0.1 collective-permute-start.8
  36.5 1.6 %shard_map.94.total = f32[200,1408]{1,0:T(8,128)S(1)} custom-call(bf16[200,1536]{1,0:T(8,128)(2,1)S(1)} %get-tuple-element.47.product, bf16[1536,1408]{1,0:T(8,128)(2,1)S(1)} %get-tuple-element.30.scatter, bf16[352,1408]{1,0:T(8,128)(2,1)S(1)} %get-tuple-element.37.to_own, f32[1,1408]{1,0:T(1,128)S(1)} %copy-done.1, ...), custom_call_target="tpu_custom_call" | custom-call | flops 591462400 | bytes 9357184 | tf_op jit(solution)/shard_map/pallas_call | solution.py:58
  38.1 0.0 collective-permute-done.8.refs_0_
  38.1 0.7 %shard_map.96 = (bf16[200,1408]{1,0:T(8,128)(2,1)S(1)}, bf16[200,176]{1,0:T(8,128)(2,1)S(1)}) custom-call(s32[2,176]{1,0:T(2,128)S(1)} %pad.12.send_row, f32[200,1408]{1,0:T(8,128)S(1)} %shard_map.94.total, bf16[200,176]{1,0:T(8,128)(2,1)S(1)} %collective-permute-done.8.refs_0_), custom_call_target="tpu_custom_call" | custom-call | flops 297369600 | bytes 1831808 | tf_op jit(solution)/shard_map/pallas_call | solution.py:58
  38.8 0.6 %collective-permute-start.9 = (bf16[200,176]{1,0:T(8,128)(2,1)S(1)}, bf16[200,176]{1,0:T(8,128)(2,1)S(1)}, u32[]{:S(2)}, u32[]{:S(2)}) collective-permute-start(bf16[200,176]{1,0:T(8,128)(2,1)S(1)} %get-tuple-element.51), channel_id=1, source_target_pairs={{0,1},{1,0},{2,3},{3,2},{4,5},{5,4},{6,7},{7,6},{8,9},{9,8},{10,11... | collective-permute-start | bytes 211208 | tf_op jit(solution)/shard_map/ppermute | solution.py:35
  39.4 0.7 %shard_map.97 = (f32[2,200,176]{2,1,0:T(8,128)S(1)}, bf16[200,176]{1,0:T(8,128)(2,1)S(1)}) custom-call(s32[2,176]{1,0:T(2,128)S(1)} %pad.12.send_row, bf16[352,1408]{1,0:T(8,128)(2,1)S(1)} %get-tuple-element.37.to_own, bf16[200,1408]{1,0:T(8,128)(2,1)S(1)} %get-tuple-element.49.values), custom_call_target="tpu_custom_call" | custom-call | flops 396492800 | bytes 1907840 | tf_op jit(solution)/shard_map/pallas_call | solution.py:58
  40.1 0.3 collective-permute-done.9.near_ghosts
  40.3 0.2 shard_map.98.after
  40.6 3.6 %collective-permute-start.10 = (bf16[200,352]{1,0:T(8,128)(2,1)S(1)}, bf16[200,352]{1,0:T(8,128)(2,1)S(1)}, u32[]{:S(2)}, u32[]{:S(2)}) collective-permute-start(bf16[200,352]{1,0:T(8,128)(2,1)S(1)} %shard_map.98.after), channel_id=1, source_target_pairs={{1,2},{2,1},{3,4},{4,3},{5,6},{6,5},{9,10},{10,9},{11,12},{12,11},... | collective-permute-start | bytes 422408 | tf_op jit(solution)/shard_map/ppermute | solution.py:35
  44.2 2.3 %shard_map.99 = (bf16[200,1536]{1,0:T(8,128)(2,1)S(1)}, f32[200,768]{1,0:T(8,128)S(1)}) custom-call(f32[1,1536]{1,0:T(1,128)S(1)} %bitcast.35, s32[1,1536]{1,0:T(1,128)S(1)} %bitcast.31, bf16[768,768]{1,0:T(8,128)(2,1)S(1)} %pad.14.stiffness, bf16[1536,1408]{1,0:T(8,128)(2,1)S(1)} %get-tuple-element.30.scatter, f32[1,1408]{1,0:T(1,128)S(1)} %copy-done.1, ...), custom_call_target="tpu_custom_call" | custom-call | flops 1808793600 | bytes 8018944 | tf_op jit(solution)/shard_map/pallas_call | solution.py:58
  46.6 0.6 %collective-permute-done.10.parcel = bf16[200,352]{1,0:T(8,128)(2,1)S(1)} collective-permute-done((bf16[200,352]{1,0:T(8,128)(2,1)S(1)}, bf16[200,352]{1,0:T(8,128)(2,1)S(1)}, u32[]{:S(2)}, u32[]{:S(2)}) %collective-permute-start.10) | collective-permute-done | bytes 140832 | tf_op jit(solution)/shard_map/ppermute | solution.py:35
  47.1 0.2 shard_map.101
  47.3 0.1 collective-permute-start.11
  47.4 1.5 %shard_map.100.total = f32[200,1408]{1,0:T(8,128)S(1)} custom-call(bf16[200,1536]{1,0:T(8,128)(2,1)S(1)} %get-tuple-element.53.product, bf16[1536,1408]{1,0:T(8,128)(2,1)S(1)} %get-tuple-element.30.scatter, bf16[352,1408]{1,0:T(8,128)(2,1)S(1)} %get-tuple-element.37.to_own, f32[1,1408]{1,0:T(1,128)S(1)} %copy-done.1, ...), custom_call_target="tpu_custom_call" | custom-call | flops 591462400 | bytes 9357184 | tf_op jit(solution)/shard_map/pallas_call | solution.py:58
  48.9 0.0 collective-permute-done.11.refs_0_
  49.0 1.2 %shard_map.102 = bf16[200,1408]{1,0:T(8,128)(2,1)} custom-call(s32[2,176]{1,0:T(2,128)S(1)} %pad.12.send_row, f32[200,1408]{1,0:T(8,128)S(1)} %shard_map.100.total, bf16[200,176]{1,0:T(8,128)(2,1)S(1)} %collective-permute-done.11.refs_0_), custom_call_target="tpu_custom_call" | custom-call | flops 297369600 | bytes 1761408 | tf_op jit(solution)/shard_map/pallas_call | solution.py:58
  (20 shorter events, 0.1 us)
Async XLA Ops:
  0.0 7.6 %copy-start.4 = (s32[1,4,162]{2,1,0:T(4,128)S(1)}, s32[1,4,162]{2,1,0:T(4,128)}, u32[]{:S(2)}) copy-start(s32[1,4,162]{2,1,0:T(4,128)} %param.14) | copy-start | bytes 7780
  0.0 7.6 %copy-start.3 = (s32[1,2,729]{2,1,0:T(2,128)S(1)}, s32[1,2,729]{2,1,0:T(2,128)}, u32[]{:S(2)}) copy-start(s32[1,2,729]{2,1,0:T(2,128)} %param.13) | copy-start | bytes 17500
  0.0 7.7 %copy-start.5 = (f32[1,2]{1,0:T(1,128)S(1)}, f32[1,2]{1,0:T(1,128)}, u32[]{:S(2)}) copy-start(f32[1,2]{1,0:T(1,128)} %param.11) | copy-start | bytes 28
  0.0 7.8 %copy-start.2 = (bf16[729,729]{1,0:T(8,128)(2,1)S(1)}, bf16[729,729]{1,0:T(8,128)(2,1)}, u32[]{:S(2)}) copy-start(bf16[729,729]{1,0:T(8,128)(2,1)} %param.10) | copy-start | bytes 3188650
  3.5 8.4 %collective-permute-start = (bf16[200,352]{1,0:T(8,128)(2,1)}, bf16[200,352]{1,0:T(8,128)(2,1)S(1)}, u32[]{:S(2)}, u32[]{:S(2)}) collective-permute-start(bf16[200,352]{1,0:T(8,128)(2,1)} %get-tuple-element.33), channel_id=1, source_target_pairs={{0,8},{8,0},{16,24},{24,16},{1,9},{9,1},{17,25},{25,17},{2,10},{10... | collective-permute-start | bytes 422408 | tf_op jit(solution)/shard_map/ppermute | solution.py:287
  5.6 6.3 %collective-permute-start.1 = (bf16[200,352]{1,0:T(8,128)(2,1)}, bf16[200,352]{1,0:T(8,128)(2,1)S(1)}, u32[]{:S(2)}, u32[]{:S(2)}) collective-permute-start(bf16[200,352]{1,0:T(8,128)(2,1)} %get-tuple-element.34), channel_id=1, source_target_pairs={{0,16},{8,24},{16,0},{24,8},{1,17},{9,25},{17,1},{25,9},{2,18},{10... | collective-permute-start | bytes 422408 | tf_op jit(solution)/shard_map/ppermute | solution.py:287
  6.9 7.2 %collective-permute-start.2 = (bf16[200,352]{1,0:T(8,128)(2,1)}, bf16[200,352]{1,0:T(8,128)(2,1)S(1)}, u32[]{:S(2)}, u32[]{:S(2)}) collective-permute-start(bf16[200,352]{1,0:T(8,128)(2,1)} %get-tuple-element.35), channel_id=1, source_target_pairs={{0,24},{8,16},{16,8},{24,0},{1,25},{9,17},{17,9},{25,1},{2,26},{10... | collective-permute-start | bytes 422408 | tf_op jit(solution)/shard_map/ppermute | solution.py:287
  7.9 6.1 %copy-start = (bf16[200,352]{1,0:T(8,128)(2,1)S(1)}, bf16[200,352]{1,0:T(8,128)(2,1)}, u32[]{:S(2)}) copy-start(bf16[200,352]{1,0:T(8,128)(2,1)} %get-tuple-element.32.refs_0_) | copy-start | bytes 422404
  14.6 2.5 %collective-permute-start.3 = (bf16[200,176]{1,0:T(8,128)(2,1)S(1)}, bf16[200,176]{1,0:T(8,128)(2,1)S(1)}, u32[]{:S(2)}, u32[]{:S(2)}) collective-permute-start(bf16[200,176]{1,0:T(8,128)(2,1)S(1)} %get-tuple-element.39), channel_id=1, source_target_pairs={{0,1},{1,0},{2,3},{3,2},{4,5},{5,4},{6,7},{7,6},{8,9},{9,8},{10,11... | collective-permute-start | bytes 211208 | tf_op jit(solution)/shard_map/ppermute | solution.py:35
  16.1 4.7 %copy-start.1 = (f32[1,1408]{1,0:T(1,128)S(1)}, f32[1,1408]{1,0:T(1,128)}, u32[]{:S(2)}) copy-start(f32[1,1408]{1,0:T(1,128)} %potential.11) | copy-start | bytes 16900
  17.3 8.0 %collective-permute-start.4 = (bf16[384,352]{1,0:T(8,128)(2,1)S(1)}, bf16[384,352]{1,0:T(8,128)(2,1)S(1)}, u32[]{:S(2)}, u32[]{:S(2)}) collective-permute-start(bf16[384,352]{1,0:T(8,128)(2,1)S(1)} %shard_map.86.after), channel_id=1, source_target_pairs={{1,2},{2,1},{3,4},{4,3},{5,6},{6,5},{9,10},{10,9},{11,12},{12,11},... | collective-permute-start | bytes 811016 | tf_op jit(solution)/shard_map/ppermute | solution.py:35
  25.6 1.6 %collective-permute-start.5 = (bf16[200,176]{1,0:T(8,128)(2,1)S(1)}, bf16[200,176]{1,0:T(8,128)(2,1)S(1)}, u32[]{:S(2)}, u32[]{:S(2)}) collective-permute-start(bf16[200,176]{1,0:T(8,128)(2,1)S(1)} %shard_map.89), channel_id=1, source_target_pairs={{0,1},{1,0},{2,3},{3,2},{4,5},{5,4},{6,7},{7,6},{8,9},{9,8},{10,11... | collective-permute-start | bytes 211208 | tf_op jit(solution)/shard_map/ppermute | solution.py:35
  27.9 1.5 %collective-permute-start.6 = (bf16[200,176]{1,0:T(8,128)(2,1)S(1)}, bf16[200,176]{1,0:T(8,128)(2,1)S(1)}, u32[]{:S(2)}, u32[]{:S(2)}) collective-permute-start(bf16[200,176]{1,0:T(8,128)(2,1)S(1)} %get-tuple-element.45), channel_id=1, source_target_pairs={{0,1},{1,0},{2,3},{3,2},{4,5},{5,4},{6,7},{7,6},{8,9},{9,8},{10,11... | collective-permute-start | bytes 211208 | tf_op jit(solution)/shard_map/ppermute | solution.py:35
  29.7 6.5 %collective-permute-start.7 = (bf16[200,352]{1,0:T(8,128)(2,1)S(1)}, bf16[200,352]{1,0:T(8,128)(2,1)S(1)}, u32[]{:S(2)}, u32[]{:S(2)}) collective-permute-start(bf16[200,352]{1,0:T(8,128)(2,1)S(1)} %shard_map.92.after), channel_id=1, source_target_pairs={{1,2},{2,1},{3,4},{4,3},{5,6},{6,5},{9,10},{10,9},{11,12},{12,11},... | collective-permute-start | bytes 422408 | tf_op jit(solution)/shard_map/ppermute | solution.py:35
  36.4 1.6 %collective-permute-start.8 = (bf16[200,176]{1,0:T(8,128)(2,1)S(1)}, bf16[200,176]{1,0:T(8,128)(2,1)S(1)}, u32[]{:S(2)}, u32[]{:S(2)}) collective-permute-start(bf16[200,176]{1,0:T(8,128)(2,1)S(1)} %shard_map.95), channel_id=1, source_target_pairs={{0,1},{1,0},{2,3},{3,2},{4,5},{5,4},{6,7},{7,6},{8,9},{9,8},{10,11... | collective-permute-start | bytes 211208 | tf_op jit(solution)/shard_map/ppermute | solution.py:35
  38.8 1.5 %collective-permute-start.9 = (bf16[200,176]{1,0:T(8,128)(2,1)S(1)}, bf16[200,176]{1,0:T(8,128)(2,1)S(1)}, u32[]{:S(2)}, u32[]{:S(2)}) collective-permute-start(bf16[200,176]{1,0:T(8,128)(2,1)S(1)} %get-tuple-element.51), channel_id=1, source_target_pairs={{0,1},{1,0},{2,3},{3,2},{4,5},{5,4},{6,7},{7,6},{8,9},{9,8},{10,11... | collective-permute-start | bytes 211208 | tf_op jit(solution)/shard_map/ppermute | solution.py:35
  40.6 6.5 %collective-permute-start.10 = (bf16[200,352]{1,0:T(8,128)(2,1)S(1)}, bf16[200,352]{1,0:T(8,128)(2,1)S(1)}, u32[]{:S(2)}, u32[]{:S(2)}) collective-permute-start(bf16[200,352]{1,0:T(8,128)(2,1)S(1)} %shard_map.98.after), channel_id=1, source_target_pairs={{1,2},{2,1},{3,4},{4,3},{5,6},{6,5},{9,10},{10,9},{11,12},{12,11},... | collective-permute-start | bytes 422408 | tf_op jit(solution)/shard_map/ppermute | solution.py:35
  47.3 1.6 %collective-permute-start.11 = (bf16[200,176]{1,0:T(8,128)(2,1)S(1)}, bf16[200,176]{1,0:T(8,128)(2,1)S(1)}, u32[]{:S(2)}, u32[]{:S(2)}) collective-permute-start(bf16[200,176]{1,0:T(8,128)(2,1)S(1)} %shard_map.101), channel_id=1, source_target_pairs={{0,1},{1,0},{2,3},{3,2},{4,5},{5,4},{6,7},{7,6},{8,9},{9,8},{10,11... | collective-permute-start | bytes 211208 | tf_op jit(solution)/shard_map/ppermute | solution.py:35

commit v3 on v2

--- a/solution.py
+++ b/solution.py
@@ -20,7 +20,6 @@
 ANY = pl.BlockSpec(memory_space=pl.ANY)
 LANES = 128
 ROTATE_VMEM = 56 << 20
-HEAD = 768
 
 
 def round_up(value, multiple):
@@ -52,14 +51,14 @@
     return out
 
 
-def call(kernel, out_shape, args, flops, scratch=(), in_specs=None, vmem=24 << 20):
+def call(kernel, out_shape, args, flops, scratch=(), in_specs=None, out_specs=None, vmem=24 << 20):
     outs = out_shape if isinstance(out_shape, (tuple, list)) else (out_shape,)
     size = sum(a.size * a.dtype.itemsize for a in list(args) + list(outs))
     return pl.pallas_call(
         kernel,
         out_shape=out_shape,
         in_specs=in_specs or [VMEM] * len(args),
-        out_specs=jax.tree.map(lambda _: VMEM, out_shape),
+        out_specs=out_specs or jax.tree.map(lambda _: VMEM, out_shape),
         scratch_shapes=list(scratch),
         cost_estimate=pl.CostEstimate(flops=flops, bytes_accessed=size, transcendentals=0),
         compiler_params=pltpu.CompilerParams(vmem_limit_bytes=vmem),
@@ -115,7 +114,7 @@
         hot[:, i : i + n] = (turned[:, :n] == lanes).astype(BF16)
 
 
-def couple_kernel(capacity, weight, node_row, stiffness, to_ghost, to_own, scatter, local):
+def couple_kernel(capacity, weight, node_row, send_row, stiffness, to_ghost, to_own, scatter, spread, local):
     nodes = stiffness.shape[0]
     ghosts = to_own.shape[0]
     slots = to_ghost.shape[2]
@@ -123,6 +122,8 @@
         picks = rows_hot(node_row[:, i : i + n], capacity, ghosts)
         local[:, i : i + n] = (mm(picks, stiffness[...]) * weight[:, i : i + n]).astype(BF16)
     columns_hot(node_row[...], capacity, scatter)
+    for block in range(to_ghost.shape[0]):
+        columns_hot(send_row[block : block + 1, :], capacity, spread.at[block])
     for block in range(to_ghost.shape[0]):
         picks = rows_hot(node_row[...], capacity + block * slots, slots)
         to_ghost[block] = mm_nt(local[...], picks).astype(BF16)
@@ -157,7 +158,7 @@
 def cells_kernel(first_step, weight, node_row, stiffness, scatter, potential, values, after, *refs):
     refs = list(refs)
     previous = None if first_step else refs.pop(0)
-    product, head, *locals_ = refs
+    out, product, *locals_ = refs
     capacity = values.shape[1]
     nodes = stiffness.shape[0]
     parts = steps(product.shape[1], nodes)
@@ -165,10 +166,12 @@
         local[...] = mm(values[...], rows_hot(node_row[:, i : i + n], 0, capacity)).astype(BF16)
     for (i, n), local in zip(parts, locals_):
         product[:, i : i + n] = (mm(local[...], stiffness[...]) * weight[:, i : i + n]).astype(BF16)
-    for i, n in steps(head.shape[1], 256):
+    for i, n in steps(capacity, 256):
         at = slice(i, i + n)
         sums = mm(product[...], scatter[:, at])
-        head[:, at] = own_columns(first_step, at, sums, potential, values, previous)
+        shifted = sums + (potential[:, at] - CENTER) * values[:, at].astype(F32)
+        result = shifted * scale_of(first_step)
+        out[:, at] = result if first_step else result - previous[:, at].astype(F32)
 
 
 def ghost_sum(block, terms, to_ghost, arrived):
@@ -186,14 +189,20 @@
         refs[blocks + block][...] = ghost_sum(block, terms, to_ghost, arrived)
 
 
+def coupling_rows(slots):
+    return round_up(-(-slots // 2), 16)
+
+
 def parcel_kernel(terms, to_ghost, near_ghosts, far_picked, parcel):
     width, slots = far_picked.shape
     sums = ghost_sum(1, terms, to_ghost, [(0, near_ghosts[...])])
     parcel[:width, :] = jnp.concatenate([far_picked[...], sums], axis=1)
     if parcel.shape[0] > width:
+        half = coupling_rows(slots)
+        first = parcel.shape[0] - half
         parcel[width:, :] = jnp.zeros((parcel.shape[0] - width, 2 * slots), BF16)
-        first = parcel.shape[0] - slots
-        parcel[first:, :slots] = to_ghost[1, slots : 2 * slots, :]
+        parcel[first:, :slots] = to_ghost[1, slots : slots + half, :]
+        parcel[first : first + slots - half, slots:] = to_ghost[1, slots + half : 2 * slots, :]
 
 
 def near_kernel(terms, to_ghost, near_ghosts, parcel, after, out):
@@ -206,56 +215,56 @@
     return (1.0 if first_step else 2.0) / HALF_WIDTH
 
 
-def own_columns(first_step, at, sums, potential, values, previous):
-    shifted = sums + (potential[:, at] - CENTER) * values[:, at].astype(F32)
-    result = shifted * scale_of(first_step)
-    return result if first_step else result - previous[:, at].astype(F32)
-
-
-def own_kernel(first_step, product, scatter, to_own, potential, values, head, *refs):
-    refs = list(refs)
-    previous = None if first_step else refs.pop(0)
+def own_kernel(first_step, to_own, head, *refs):
     arrived, out = refs[:-1], refs[-1]
     ghosts = jnp.concatenate([ghost[...] for ghost in arrived], axis=1)
     for i, n in steps(out.shape[1], 256):
         at = slice(i, i + n)
-        sums = mm(ghosts, to_own[:, at])
-        if i < head.shape[1]:
-            out[:, at] = head[:, at] + sums * scale_of(first_step)
-        else:
-            sums = sums + mm(product[...], scatter[:, at])
-            out[:, at] = own_columns(first_step, at, sums, potential, values, previous)
+        out[:, at] = head[:, at] + mm(ghosts, to_own[:, at]) * scale_of(first_step)
 
 
 def paired_own_kernel(
-    first_step, product, scatter, to_own, potential, values, head, send_row, near_ghosts, far_picked, parcel, first_parcel, *refs
+    first_step, to_own, head, spread, near_ghosts, far_picked, parcel, first_parcel, out
 ):
-    previous, out = (None if first_step else refs[0]), refs[-1]
     width, slots = far_picked.shape
     ghosts = jnp.concatenate([near_ghosts[...], parcel[:width, :slots]], axis=1)
-    coupling = first_parcel[first_parcel.shape[0] - slots :, :slots]
+    half = coupling_rows(slots)
+    start = first_parcel.shape[0] - half
+    coupling = jnp.concatenate(
+        [first_parcel[start:, :slots], first_parcel[start : start + slots - half, slots:]], axis=0
+    )
     returned = parcel[:width, slots:].astype(F32) + mm(far_picked[...], coupling)
     returned = returned.astype(BF16)
     for i, n in steps(out.shape[1], 256):
         at = slice(i, i + n)
-        sums = mm(ghosts, to_own[:, at]) + mm_nt(returned, rows_hot(send_row[1:2, :], i, n))
-        if i < head.shape[1]:
-            out[:, at] = head[:, at] + sums * scale_of(first_step)
-        else:
-            sums = sums + mm(product[...], scatter[:, at])
-            out[:, at] = own_columns(first_step, at, sums, potential, values, previous)
-
-
-def update_kernel(blocks, first_step, last_step, send_row, total, *refs):
-    arrived, out, picked = refs[:blocks], refs[blocks], refs[blocks + 1 :]
+        sums = mm(ghosts, to_own[:, at]) + mm(returned, spread[1, :, at])
+        out[:, at] = head[:, at] + sums * scale_of(first_step)
+
+
+def updated_columns(first_step, spread, i, n, total, arrived):
+    sums = 0.0
+    for block, ghost in enumerate(arrived):
+        sums = sums + mm(ghost[...], spread[block, :, i : i + n])
+    return (total[:, i : i + n] + sums * scale_of(first_step)).astype(BF16)
+
+
+def update_kernel(blocks, first_step, spread, send_row, total, *refs):
+    arrived, (out, near_picked) = refs[:blocks], refs[blocks:]
     for i, n in steps(out.shape[1], 256):
-        at = slice(i, i + n)
-        added = 0.0
-        for block in range(blocks):
-            added = added + mm_nt(arrived[block][...], rows_hot(send_row[block : block + 1, :], i, n))
-        out[:, at] = (total[:, at] + added * scale_of(first_step)).astype(BF16)
-    if not last_step:
-        pick_rows(send_row, 0, out, picked[0])
+        out[:, i : i + n] = updated_columns(first_step, spread, i, n, total, arrived)
+    near_picked[...] = mm_nt(out[...], spread[0]).astype(BF16)
+
+
+def last_kernel(blocks, first_step, spread, total, *refs):
+    arrived, (out, held, sems) = refs[:blocks], refs[blocks:]
+    copies = []
+    for part, (i, n) in enumerate(steps(out.shape[1], 256)):
+        held[:, i : i + n] = updated_columns(first_step, spread, i, n, total, arrived)
+        at = pl.ds(i, n)
+        copies.append(pltpu.make_async_copy(held.at[:, at], out.at[:, at], sems.at[part]))
+        copies[-1].start()
+    for copy in copies:
+        copy.wait()
 
 
 def shards(
@@ -322,14 +331,15 @@
 
     local_rows = cells * nodes_pad
     cell_flops = 2 * local_rows * nodes_pad
-    to_ghost, to_own, scatter = call(
+    to_ghost, to_own, scatter, spread = call(
         functools.partial(couple_kernel, capacity),
         (
             shape((blocks, ghosts, slots_pad), BF16),
             shape((ghosts, capacity), BF16),
             shape((local_rows, capacity), BF16),
+            shape((blocks, slots_pad, capacity), BF16),
         ),
-        (weight, node_row, stiffness),
+        (weight, node_row, send_row, stiffness),
         (cell_flops + 2 * local_rows * (ghosts + capacity)) * ghosts,
         scratch=[pltpu.VMEM((ghosts, local_rows), BF16)],
     )
@@ -343,9 +353,8 @@
         scratch=[pltpu.VMEM((bands, width, piece_rows), BF16)],
         in_specs=[VMEM, VMEM, ANY] + [VMEM] * bands,
     )
-    head_columns = min(HEAD, capacity)
     previous = None
-    parcel_rows = round_up(width, 16) + slots_pad
+    parcel_rows = round_up(width, 16) + coupling_rows(slots_pad)
     first_parcel = None
     for filter_step in range(FILTER_STEPS):
         first, last = filter_step == 0, filter_step == FILTER_STEPS - 1
@@ -370,16 +379,15 @@
             parcel = swap(parcel, 1)
             first_parcel = parcel if first else first_parcel
         history = () if first else (previous,)
-        product, head = call(
+        head = call(
             functools.partial(cells_kernel, first),
-            (shape((width, local_rows), BF16), shape((width, head_columns), F32)),
+            shape((width, capacity), F32),
             (weight, node_row, stiffness, scatter, potential, current, ready, *history),
-            (cell_flops + 2 * local_rows * (capacity + head_columns)) * width,
-            scratch=[pltpu.VMEM((width, nodes_pad), BF16)] * cells,
+            (cell_flops + 4 * local_rows * capacity) * width,
+            scratch=[pltpu.VMEM((width, local_rows), BF16)] + [pltpu.VMEM((width, nodes_pad), BF16)] * cells,
             in_specs=[VMEM] * 6 + [ANY] + [VMEM] * len(history),
         )
-        own_flops = 2 * ((capacity - head_columns) * local_rows + capacity * ghosts) * width
-        own_operands = (product, scatter, to_own, potential, current, head)
+        own_flops = 2 * capacity * ghosts * width
         if far:
             sums = call(
                 ghost_kernel,
@@ -391,7 +399,7 @@
             total = call(
                 functools.partial(own_kernel, first),
                 shape((width, capacity), F32),
-                (*own_operands, *history, *arrived),
+                (to_own, head, *arrived),
                 own_flops,
             )
         else:
@@ -406,17 +414,30 @@
             total = call(
                 functools.partial(paired_own_kernel, first),
                 shape((width, capacity), F32),
-                (*own_operands, send_row, near, picked[0], parcel, first_parcel, *history),
+                (to_own, head, spread, near, picked[0], parcel, first_parcel),
                 own_flops,
             )
-        following, *near_next = call(
-            functools.partial(update_kernel, len(returned), first, last),
-            (shape((width, capacity), BF16),) + (() if last else (block_shape,)),
-            (send_row, total, *returned),
-            2 * capacity * (ghosts + slots_pad * len(returned)) * width,
-        )
-        previous, current = current, following
-        near_picked = near_next[0] if near_next else None
+        update_flops = 2 * capacity * (ghosts + slots_pad * len(returned)) * width
+        if last:
+            current = call(
+                functools.partial(last_kernel, len(returned), first),
+                shape((width, capacity), BF16),
+                (spread, total, *returned),
+                update_flops,
+                scratch=[
+                    pltpu.VMEM((width, capacity), BF16),
+                    pltpu.SemaphoreType.DMA((len(steps(capacity, 256)),)),
+                ],
+                out_specs=ANY,
+            )
+        else:
+            following, near_picked = call(
+                functools.partial(update_kernel, len(returned), first),
+                (shape((width, capacity), BF16), block_shape),
+                (spread, send_row, total, *returned),
+                update_flops,
+            )
+            previous, current = current, following
     return current.T[None]
 
 

time: 50.8 us -> 48.6 us (0.957)
  waiting for transfers between devices: 6.25 us -> 5.45 us
  starting transfers between devices: 16.9 us -> 16.2 us
  Pallas kernels: 25.7 us -> 25.1 us
    ppermute x9, waiting for transfers between devices: 4.14 us -> 3.4 us  [swap(): return lax.ppermute(value, 'dom', pairs)]
    ppermute x9, starting transfers between devices: 13.6 us -> 12.9 us  [swap(): return lax.ppermute(value, 'dom', pairs)]
    pallas_call x21, Pallas kernels: 25.7 us -> 25.1 us  [call(): pl.pallas_call(kernel, out_shape=out_shape, in_specs=in_specs or [VMEM] *...]
  transfers between devices with their start and end apart: 12 -> 12, of which waited for: 7 -> 10; matrix products, arithmetic and copies ran while one was open for 1% -> 1% of each run, Pallas kernels for 35% -> 36%
where the time goes in v3:
time: 48.6 us; the launch traced here: 48.2 us
  Pallas kernels  25.1 us (52%)
  starting transfers between devices  16.2 us (33%)
  waiting for transfers between devices  5.45 us (11%)
  between operations  1.19 us (2%)
    pallas_call x21, Pallas kernels, call(): pl.pallas_call(kernel, out_shape=out_shape, in_specs=in_specs or [VMEM] *...  25.1 us
    ppermute x9, starting transfers between devices, swap(): return lax.ppermute(value, 'dom', pairs)  12.9 us
    ppermute x9, waiting for transfers between devices, swap(): return lax.ppermute(value, 'dom', pairs)  3.4 us
    ppermute x3, starting transfers between devices, shards(): lax.ppermute(pieces[k], 'band', [(i, i ^ k) for i in range(bands)])  3.37 us
    ppermute x3, waiting for transfers between devices, shards(): lax.ppermute(pieces[k], 'band', [(i, i ^ k) for i in range(bands)])  2.06 us
  transfers between devices with their start and end apart: 12, of which 10 were waited for; matrix products, arithmetic and copies ran while one was open for 1% of the time, Pallas kernels for 36%

profile of v3, /device:TPU:1, one launch (start us, length us, event | category | flops | bytes accessed | tf_op | source)
XLA Modules:
  0.0 48.2 jit_solution(16790065129895999173)
XLA Ops:
  0.0 3.5 %shard_map.83 = (bf16[200,352]{1,0:T(8,128)(2,1)}, bf16[200,352]{1,0:T(8,128)(2,1)}, bf16[200,352]{1,0:T(8,128)(2,1)}, bf16[200,352]{1,0:T(8,128)(2,1)}) custom-call(bf16[800,352]{1,0:T(8,128)(2,1)} %bitcast.36, bf16[800,800]{1,0:T(8,128)(2,1)} %rotation.1), custom_call_target="tpu_custom_call" | custom-call | flops 450560000 | bytes 2406400 | tf_op jit(solution)/shard_map/pallas_call | solution.py:57
  3.5 2.1 %collective-permute-start = (bf16[200,352]{1,0:T(8,128)(2,1)}, bf16[200,352]{1,0:T(8,128)(2,1)S(1)}, u32[]{:S(2)}, u32[]{:S(2)}) collective-permute-start(bf16[200,352]{1,0:T(8,128)(2,1)} %get-tuple-element.30), channel_id=1, source_target_pairs={{0,8},{8,0},{16,24},{24,16},{1,9},{9,1},{17,25},{25,17},{2,10},{10... | collective-permute-start | bytes 422408 | tf_op jit(solution)/shard_map/ppermute | solution.py:296
  5.6 1.2 %collective-permute-start.1 = (bf16[200,352]{1,0:T(8,128)(2,1)}, bf16[200,352]{1,0:T(8,128)(2,1)S(1)}, u32[]{:S(2)}, u32[]{:S(2)}) collective-permute-start(bf16[200,352]{1,0:T(8,128)(2,1)} %get-tuple-element.31), channel_id=1, source_target_pairs={{0,16},{8,24},{16,0},{24,8},{1,17},{9,25},{17,1},{25,9},{2,18},{10... | collective-permute-start | bytes 422408 | tf_op jit(solution)/shard_map/ppermute | solution.py:296
  6.9 0.0 collective-permute-start.2
  7.7 0.1 broadcast_bitcast_fusion
  7.8 0.1 pad.14.stiffness
  7.9 0.0 copy-start
  7.9 4.0 %shard_map.82 = (bf16[2,352,176]{2,1,0:T(8,128)(2,1)S(1)}, bf16[352,1408]{1,0:T(8,128)(2,1)S(1)}, bf16[1536,1408]{1,0:T(8,128)(2,1)S(1)}, bf16[2,176,1408]{2,1,0:T(8,128)(2,1)S(1)}) custom-call(f32[1,1536]{1,0:T(1,128)S(1)} %bitcast.32, s32[1,1536]{1,0:T(1,128)S(1)} %bitcast.28, s32[2,176]{1,0:T(2,128)S(1)} %pad.13.send_row, bf16[768,768]{1,0:T(8,128)(2,1)S(1)} %pad.14.stiffness), custom_call_target="tpu_custom_call" | custom-call | flops 2733637632 | bytes 7748992 | tf_op jit(solution)/shard_map/pallas_call | solution.py:57
  12.0 0.0 collective-permute-done.refs_1_
  12.0 0.0 collective-permute-done.1.refs_2_
  12.0 2.0 %collective-permute-done.2.refs_3_ = bf16[200,352]{1,0:T(8,128)(2,1)S(1)} collective-permute-done((bf16[200,352]{1,0:T(8,128)(2,1)}, bf16[200,352]{1,0:T(8,128)(2,1)S(1)}, u32[]{:S(2)}, u32[]{:S(2)}) %collective-permute-start.2) | collective-permute-done | bytes 140832 | tf_op jit(solution)/shard_map/ppermute | solution.py:296
  14.1 0.5 %shard_map.84 = (bf16[200,1408]{1,0:T(8,128)(2,1)S(1)}, bf16[200,176]{1,0:T(8,128)(2,1)S(1)}) custom-call(s32[2,176]{1,0:T(2,128)S(1)} %pad.13.send_row, s32[1,1408]{1,0:T(1,128)S(1)} %compare_convert_fusion.keep, bf16[2,352,176]{2,1,0:T(8,128)(2,1)S(1)} %get-tuple-element.28.after.to_ghost, bf16[200,352]{1,0:T(8,128)(2,1)S(1)} %copy-done, ...), custom_call_target="tpu_custom_call" | custom-call | flops 99123200 | bytes 1451648 | tf_op jit(solution)/shard_map/pallas_call | solution.py:57
  14.6 1.5 %collective-permute-start.3 = (bf16[200,176]{1,0:T(8,128)(2,1)S(1)}, bf16[200,176]{1,0:T(8,128)(2,1)S(1)}, u32[]{:S(2)}, u32[]{:S(2)}) collective-permute-start(bf16[200,176]{1,0:T(8,128)(2,1)S(1)} %get-tuple-element.35), channel_id=1, source_target_pairs={{0,1},{1,0},{2,3},{3,2},{4,5},{5,4},{6,7},{7,6},{8,9},{9,8},{10,11... | collective-permute-start | bytes 211208 | tf_op jit(solution)/shard_map/ppermute | solution.py:34
  16.1 0.7 %shard_map.85 = (f32[2,200,176]{2,1,0:T(8,128)S(1)}, bf16[200,176]{1,0:T(8,128)(2,1)S(1)}) custom-call(s32[2,176]{1,0:T(2,128)S(1)} %pad.13.send_row, bf16[352,1408]{1,0:T(8,128)(2,1)S(1)} %get-tuple-element.26.to_own, bf16[200,1408]{1,0:T(8,128)(2,1)S(1)} %get-tuple-element.33.values.refs_0_), custom_call_target="tpu_custom_call" | custom-call | flops 396492800 | bytes 1907840 | tf_op jit(solution)/shard_map/pallas_call | solution.py:57
  16.8 0.3 collective-permute-done.3.near_ghosts
  17.1 0.2 shard_map.86.after
  17.3 3.4 %collective-permute-start.4 = (bf16[304,352]{1,0:T(8,128)(2,1)S(1)}, bf16[304,352]{1,0:T(8,128)(2,1)S(1)}, u32[]{:S(2)}, u32[]{:S(2)}) collective-permute-start(bf16[304,352]{1,0:T(8,128)(2,1)S(1)} %shard_map.86.after), channel_id=1, source_target_pairs={{1,2},{2,1},{3,4},{4,3},{5,6},{6,5},{9,10},{10,9},{11,12},{12,11},... | collective-permute-start | bytes 642056 | tf_op jit(solution)/shard_map/ppermute | solution.py:34
  20.8 2.7 %shard_map.87.head.after = f32[200,1408]{1,0:T(8,128)S(1)} custom-call(f32[1,1536]{1,0:T(1,128)S(1)} %bitcast.33, s32[1,1536]{1,0:T(1,128)S(1)} %bitcast.29, bf16[768,768]{1,0:T(8,128)(2,1)S(1)} %pad.14.stiffness, bf16[1536,1408]{1,0:T(8,128)(2,1)S(1)} %get-tuple-element.27.scatter, f32[1,1408]{1,0:T(1,128)S(1)} %copy-done.1, ...), custom_call_target="tpu_custom_call" | custom-call | flops 2202009600 | bytes 7426560 | tf_op jit(solution)/shard_map/pallas_call | solution.py:57
  23.5 1.2 %collective-permute-done.4.parcel.first_parcel = bf16[304,352]{1,0:T(8,128)(2,1)S(1)} collective-permute-done((bf16[304,352]{1,0:T(8,128)(2,1)S(1)}, bf16[304,352]{1,0:T(8,128)(2,1)S(1)}, u32[]{:S(2)}, u32[]{:S(2)}) %collective-permute-start.4) | collective-permute-done | bytes 214048 | tf_op jit(solution)/shard_map/ppermute | solution.py:34
  24.7 0.2 shard_map.89
  24.9 0.1 collective-permute-start.5
  25.0 1.0 %shard_map.88.total = f32[200,1408]{1,0:T(8,128)S(1)} custom-call(bf16[352,1408]{1,0:T(8,128)(2,1)S(1)} %get-tuple-element.26.to_own, f32[200,1408]{1,0:T(8,128)S(1)} %shard_map.87.head.after, bf16[2,176,1408]{2,1,0:T(8,128)(2,1)S(1)} %get-tuple-element.25.spread, bf16[200,176]{1,0:T(8,128)(2,1)S(1)} %collective-permute-done.3.near_ghosts, ...), custom_call_target="tpu_custom_call" | custom-call | flops 198246400 | bytes 4804096 | tf_op jit(solution)/shard_map/pallas_call | solution.py:57
  26.0 0.3 collective-permute-done.5.refs_0_
  26.3 0.6 %shard_map.90 = (bf16[200,1408]{1,0:T(8,128)(2,1)S(1)}, bf16[200,176]{1,0:T(8,128)(2,1)S(1)}) custom-call(bf16[2,176,1408]{2,1,0:T(8,128)(2,1)S(1)} %get-tuple-element.25.spread, s32[2,176]{1,0:T(2,128)S(1)} %pad.13.send_row, f32[200,1408]{1,0:T(8,128)S(1)} %shard_map.88.total, bf16[200,176]{1,0:T(8,128)(2,1)S(1)} %collective-permute-done.5.refs_0_), custom_call_target="tpu_custom_call" | custom-call | flops 297369600 | bytes 2823040 | tf_op jit(solution)/shard_map/pallas_call | solution.py:57
  26.9 0.3 collective-permute-start.6
  27.2 0.7 %shard_map.91 = (f32[2,200,176]{2,1,0:T(8,128)S(1)}, bf16[200,176]{1,0:T(8,128)(2,1)S(1)}) custom-call(s32[2,176]{1,0:T(2,128)S(1)} %pad.13.send_row, bf16[352,1408]{1,0:T(8,128)(2,1)S(1)} %get-tuple-element.26.to_own, bf16[200,1408]{1,0:T(8,128)(2,1)S(1)} %get-tuple-element.37.values.refs_0_), custom_call_target="tpu_custom_call" | custom-call | flops 396492800 | bytes 1907840 | tf_op jit(solution)/shard_map/pallas_call | solution.py:57
  27.9 0.4 collective-permute-done.6.near_ghosts
  28.3 0.2 shard_map.92.after
  28.5 3.6 %collective-permute-start.7 = (bf16[200,352]{1,0:T(8,128)(2,1)S(1)}, bf16[200,352]{1,0:T(8,128)(2,1)S(1)}, u32[]{:S(2)}, u32[]{:S(2)}) collective-permute-start(bf16[200,352]{1,0:T(8,128)(2,1)S(1)} %shard_map.92.after), channel_id=1, source_target_pairs={{1,2},{2,1},{3,4},{4,3},{5,6},{6,5},{9,10},{10,9},{11,12},{12,11},... | collective-permute-start | bytes 422408 | tf_op jit(solution)/shard_map/ppermute | solution.py:34
  32.2 2.8 %shard_map.93.head.after = f32[200,1408]{1,0:T(8,128)S(1)} custom-call(f32[1,1536]{1,0:T(1,128)S(1)} %bitcast.34, s32[1,1536]{1,0:T(1,128)S(1)} %bitcast.30, bf16[768,768]{1,0:T(8,128)(2,1)S(1)} %pad.14.stiffness, bf16[1536,1408]{1,0:T(8,128)(2,1)S(1)} %get-tuple-element.27.scatter, f32[1,1408]{1,0:T(1,128)S(1)} %copy-done.1, ...), custom_call_target="tpu_custom_call" | custom-call | flops 2202009600 | bytes 7916544 | tf_op jit(solution)/shard_map/pallas_call | solution.py:57
  35.0 0.1 collective-permute-done.7.parcel
  35.1 0.2 shard_map.95
  35.3 0.1 collective-permute-start.8
  35.4 1.0 %shard_map.94.total = f32[200,1408]{1,0:T(8,128)S(1)} custom-call(bf16[352,1408]{1,0:T(8,128)(2,1)S(1)} %get-tuple-element.26.to_own, f32[200,1408]{1,0:T(8,128)S(1)} %shard_map.93.head.after, bf16[2,176,1408]{2,1,0:T(8,128)(2,1)S(1)} %get-tuple-element.25.spread, bf16[200,176]{1,0:T(8,128)(2,1)S(1)} %collective-permute-done.6.near_ghosts, ...), custom_call_target="tpu_custom_call" | custom-call | flops 198246400 | bytes 4730880 | tf_op jit(solution)/shard_map/pallas_call | solution.py:57
  36.4 0.3 collective-permute-done.8.refs_0_
  36.7 0.6 %shard_map.96 = (bf16[200,1408]{1,0:T(8,128)(2,1)S(1)}, bf16[200,176]{1,0:T(8,128)(2,1)S(1)}) custom-call(bf16[2,176,1408]{2,1,0:T(8,128)(2,1)S(1)} %get-tuple-element.25.spread, s32[2,176]{1,0:T(2,128)S(1)} %pad.13.send_row, f32[200,1408]{1,0:T(8,128)S(1)} %shard_map.94.total, bf16[200,176]{1,0:T(8,128)(2,1)S(1)} %collective-permute-done.8.refs_0_), custom_call_target="tpu_custom_call" | custom-call | flops 297369600 | bytes 2823040 | tf_op jit(solution)/shard_map/pallas_call | solution.py:57
  37.3 0.3 collective-permute-start.9
  37.6 0.7 %shard_map.97 = (f32[2,200,176]{2,1,0:T(8,128)S(1)}, bf16[200,176]{1,0:T(8,128)(2,1)S(1)}) custom-call(s32[2,176]{1,0:T(2,128)S(1)} %pad.13.send_row, bf16[352,1408]{1,0:T(8,128)(2,1)S(1)} %get-tuple-element.26.to_own, bf16[200,1408]{1,0:T(8,128)(2,1)S(1)} %get-tuple-element.41.values), custom_call_target="tpu_custom_call" | custom-call | flops 396492800 | bytes 1907840 | tf_op jit(solution)/shard_map/pallas_call | solution.py:57
  38.3 0.4 collective-permute-done.9.near_ghosts
  38.7 0.2 shard_map.98.after
  38.9 3.4 %collective-permute-start.10 = (bf16[200,352]{1,0:T(8,128)(2,1)S(1)}, bf16[200,352]{1,0:T(8,128)(2,1)S(1)}, u32[]{:S(2)}, u32[]{:S(2)}) collective-permute-start(bf16[200,352]{1,0:T(8,128)(2,1)S(1)} %shard_map.98.after), channel_id=1, source_target_pairs={{1,2},{2,1},{3,4},{4,3},{5,6},{6,5},{9,10},{10,9},{11,12},{12,11},... | collective-permute-start | bytes 422408 | tf_op jit(solution)/shard_map/ppermute | solution.py:34
  42.4 2.8 %shard_map.99.head.after = f32[200,1408]{1,0:T(8,128)S(1)} custom-call(f32[1,1536]{1,0:T(1,128)S(1)} %bitcast.35, s32[1,1536]{1,0:T(1,128)S(1)} %bitcast.31, bf16[768,768]{1,0:T(8,128)(2,1)S(1)} %pad.14.stiffness, bf16[1536,1408]{1,0:T(8,128)(2,1)S(1)} %get-tuple-element.27.scatter, f32[1,1408]{1,0:T(1,128)S(1)} %copy-done.1, ...), custom_call_target="tpu_custom_call" | custom-call | flops 2202009600 | bytes 7916544 | tf_op jit(solution)/shard_map/pallas_call | solution.py:57
  45.2 0.3 collective-permute-done.10.parcel
  45.4 0.2 shard_map.101
  45.7 0.1 collective-permute-start.11
  45.7 1.0 %shard_map.100.total = f32[200,1408]{1,0:T(8,128)S(1)} custom-call(bf16[352,1408]{1,0:T(8,128)(2,1)S(1)} %get-tuple-element.26.to_own, f32[200,1408]{1,0:T(8,128)S(1)} %shard_map.99.head.after, bf16[2,176,1408]{2,1,0:T(8,128)(2,1)S(1)} %get-tuple-element.25.spread, bf16[200,176]{1,0:T(8,128)(2,1)S(1)} %collective-permute-done.9.near_ghosts, ...), custom_call_target="tpu_custom_call" | custom-call | flops 198246400 | bytes 4730880 | tf_op jit(solution)/shard_map/pallas_call | solution.py:57
  46.8 0.3 collective-permute-done.11.refs_0_
  47.0 1.1 %shard_map.102 = bf16[200,1408]{1,0:T(8,128)(2,1)} custom-call(bf16[2,176,1408]{2,1,0:T(8,128)(2,1)S(1)} %get-tuple-element.25.spread, f32[200,1408]{1,0:T(8,128)S(1)} %shard_map.100.total, bf16[200,176]{1,0:T(8,128)(2,1)S(1)} %collective-permute-done.11.refs_0_), custom_call_target="tpu_custom_call" | custom-call | flops 297369600 | bytes 2751232 | tf_op jit(solution)/shard_map/pallas_call | solution.py:57
  (20 shorter events, 0.1 us)
Async XLA Ops:
  0.0 7.6 %copy-start.4 = (s32[1,4,162]{2,1,0:T(4,128)S(1)}, s32[1,4,162]{2,1,0:T(4,128)}, u32[]{:S(2)}) copy-start(s32[1,4,162]{2,1,0:T(4,128)} %param.14) | copy-start | bytes 7780
  0.0 7.6 %copy-start.3 = (s32[1,2,729]{2,1,0:T(2,128)S(1)}, s32[1,2,729]{2,1,0:T(2,128)}, u32[]{:S(2)}) copy-start(s32[1,2,729]{2,1,0:T(2,128)} %param.13) | copy-start | bytes 17500
  0.0 7.7 %copy-start.5 = (f32[1,2]{1,0:T(1,128)S(1)}, f32[1,2]{1,0:T(1,128)}, u32[]{:S(2)}) copy-start(f32[1,2]{1,0:T(1,128)} %param.11) | copy-start | bytes 28
  0.0 7.8 %copy-start.2 = (bf16[729,729]{1,0:T(8,128)(2,1)S(1)}, bf16[729,729]{1,0:T(8,128)(2,1)}, u32[]{:S(2)}) copy-start(bf16[729,729]{1,0:T(8,128)(2,1)} %param.10) | copy-start | bytes 3188650
  3.5 8.5 %collective-permute-start = (bf16[200,352]{1,0:T(8,128)(2,1)}, bf16[200,352]{1,0:T(8,128)(2,1)S(1)}, u32[]{:S(2)}, u32[]{:S(2)}) collective-permute-start(bf16[200,352]{1,0:T(8,128)(2,1)} %get-tuple-element.30), channel_id=1, source_target_pairs={{0,8},{8,0},{16,24},{24,16},{1,9},{9,1},{17,25},{25,17},{2,10},{10... | collective-permute-start | bytes 422408 | tf_op jit(solution)/shard_map/ppermute | solution.py:296
  5.6 6.4 %collective-permute-start.1 = (bf16[200,352]{1,0:T(8,128)(2,1)}, bf16[200,352]{1,0:T(8,128)(2,1)S(1)}, u32[]{:S(2)}, u32[]{:S(2)}) collective-permute-start(bf16[200,352]{1,0:T(8,128)(2,1)} %get-tuple-element.31), channel_id=1, source_target_pairs={{0,16},{8,24},{16,0},{24,8},{1,17},{9,25},{17,1},{25,9},{2,18},{10... | collective-permute-start | bytes 422408 | tf_op jit(solution)/shard_map/ppermute | solution.py:296
  6.9 7.2 %collective-permute-start.2 = (bf16[200,352]{1,0:T(8,128)(2,1)}, bf16[200,352]{1,0:T(8,128)(2,1)S(1)}, u32[]{:S(2)}, u32[]{:S(2)}) collective-permute-start(bf16[200,352]{1,0:T(8,128)(2,1)} %get-tuple-element.32), channel_id=1, source_target_pairs={{0,24},{8,16},{16,8},{24,0},{1,25},{9,17},{17,9},{25,1},{2,26},{10... | collective-permute-start | bytes 422408 | tf_op jit(solution)/shard_map/ppermute | solution.py:296
  7.9 6.1 %copy-start = (bf16[200,352]{1,0:T(8,128)(2,1)S(1)}, bf16[200,352]{1,0:T(8,128)(2,1)}, u32[]{:S(2)}) copy-start(bf16[200,352]{1,0:T(8,128)(2,1)} %get-tuple-element.29.refs_0_) | copy-start | bytes 422404
  14.6 2.5 %collective-permute-start.3 = (bf16[200,176]{1,0:T(8,128)(2,1)S(1)}, bf16[200,176]{1,0:T(8,128)(2,1)S(1)}, u32[]{:S(2)}, u32[]{:S(2)}) collective-permute-start(bf16[200,176]{1,0:T(8,128)(2,1)S(1)} %get-tuple-element.35), channel_id=1, source_target_pairs={{0,1},{1,0},{2,3},{3,2},{4,5},{5,4},{6,7},{7,6},{8,9},{9,8},{10,11... | collective-permute-start | bytes 211208 | tf_op jit(solution)/shard_map/ppermute | solution.py:34
  16.1 4.7 %copy-start.1 = (f32[1,1408]{1,0:T(1,128)S(1)}, f32[1,1408]{1,0:T(1,128)}, u32[]{:S(2)}) copy-start(f32[1,1408]{1,0:T(1,128)} %potential.5) | copy-start | bytes 16900
  17.3 7.4 %collective-permute-start.4 = (bf16[304,352]{1,0:T(8,128)(2,1)S(1)}, bf16[304,352]{1,0:T(8,128)(2,1)S(1)}, u32[]{:S(2)}, u32[]{:S(2)}) collective-permute-start(bf16[304,352]{1,0:T(8,128)(2,1)S(1)} %shard_map.86.after), channel_id=1, source_target_pairs={{1,2},{2,1},{3,4},{4,3},{5,6},{6,5},{9,10},{10,9},{11,12},{12,11},... | collective-permute-start | bytes 642056 | tf_op jit(solution)/shard_map/ppermute | solution.py:34
  24.9 1.4 %collective-permute-start.5 = (bf16[200,176]{1,0:T(8,128)(2,1)S(1)}, bf16[200,176]{1,0:T(8,128)(2,1)S(1)}, u32[]{:S(2)}, u32[]{:S(2)}) collective-permute-start(bf16[200,176]{1,0:T(8,128)(2,1)S(1)} %shard_map.89), channel_id=1, source_target_pairs={{0,1},{1,0},{2,3},{3,2},{4,5},{5,4},{6,7},{7,6},{8,9},{9,8},{10,11... | collective-permute-start | bytes 211208 | tf_op jit(solution)/shard_map/ppermute | solution.py:34
  26.9 1.4 %collective-permute-start.6 = (bf16[200,176]{1,0:T(8,128)(2,1)S(1)}, bf16[200,176]{1,0:T(8,128)(2,1)S(1)}, u32[]{:S(2)}, u32[]{:S(2)}) collective-permute-start(bf16[200,176]{1,0:T(8,128)(2,1)S(1)} %get-tuple-element.39), channel_id=1, source_target_pairs={{0,1},{1,0},{2,3},{3,2},{4,5},{5,4},{6,7},{7,6},{8,9},{9,8},{10,11... | collective-permute-start | bytes 211208 | tf_op jit(solution)/shard_map/ppermute | solution.py:34
  28.5 6.5 %collective-permute-start.7 = (bf16[200,352]{1,0:T(8,128)(2,1)S(1)}, bf16[200,352]{1,0:T(8,128)(2,1)S(1)}, u32[]{:S(2)}, u32[]{:S(2)}) collective-permute-start(bf16[200,352]{1,0:T(8,128)(2,1)S(1)} %shard_map.92.after), channel_id=1, source_target_pairs={{1,2},{2,1},{3,4},{4,3},{5,6},{6,5},{9,10},{10,9},{11,12},{12,11},... | collective-permute-start | bytes 422408 | tf_op jit(solution)/shard_map/ppermute | solution.py:34
  35.3 1.4 %collective-permute-start.8 = (bf16[200,176]{1,0:T(8,128)(2,1)S(1)}, bf16[200,176]{1,0:T(8,128)(2,1)S(1)}, u32[]{:S(2)}, u32[]{:S(2)}) collective-permute-start(bf16[200,176]{1,0:T(8,128)(2,1)S(1)} %shard_map.95), channel_id=1, source_target_pairs={{0,1},{1,0},{2,3},{3,2},{4,5},{5,4},{6,7},{7,6},{8,9},{9,8},{10,11... | collective-permute-start | bytes 211208 | tf_op jit(solution)/shard_map/ppermute | solution.py:34
  37.3 1.4 %collective-permute-start.9 = (bf16[200,176]{1,0:T(8,128)(2,1)S(1)}, bf16[200,176]{1,0:T(8,128)(2,1)S(1)}, u32[]{:S(2)}, u32[]{:S(2)}) collective-permute-start(bf16[200,176]{1,0:T(8,128)(2,1)S(1)} %get-tuple-element.43), channel_id=1, source_target_pairs={{0,1},{1,0},{2,3},{3,2},{4,5},{5,4},{6,7},{7,6},{8,9},{9,8},{10,11... | collective-permute-start | bytes 211208 | tf_op jit(solution)/shard_map/ppermute | solution.py:34
  38.9 6.5 %collective-permute-start.10 = (bf16[200,352]{1,0:T(8,128)(2,1)S(1)}, bf16[200,352]{1,0:T(8,128)(2,1)S(1)}, u32[]{:S(2)}, u32[]{:S(2)}) collective-permute-start(bf16[200,352]{1,0:T(8,128)(2,1)S(1)} %shard_map.98.after), channel_id=1, source_target_pairs={{1,2},{2,1},{3,4},{4,3},{5,6},{6,5},{9,10},{10,9},{11,12},{12,11},... | collective-permute-start | bytes 422408 | tf_op jit(solution)/shard_map/ppermute | solution.py:34
  45.7 1.4 %collective-permute-start.11 = (bf16[200,176]{1,0:T(8,128)(2,1)S(1)}, bf16[200,176]{1,0:T(8,128)(2,1)S(1)}, u32[]{:S(2)}, u32[]{:S(2)}) collective-permute-start(bf16[200,176]{1,0:T(8,128)(2,1)S(1)} %shard_map.101), channel_id=1, source_target_pairs={{0,1},{1,0},{2,3},{3,2},{4,5},{5,4},{6,7},{7,6},{8,9},{9,8},{10,11... | collective-permute-start | bytes 211208 | tf_op jit(solution)/shard_map/ppermute | solution.py:34

commit v4 on v3

--- a/solution.py
+++ b/solution.py
@@ -19,6 +19,8 @@
 VMEM = pl.BlockSpec(memory_space=pltpu.VMEM)
 ANY = pl.BlockSpec(memory_space=pl.ANY)
 LANES = 128
+DIGIT = 64
+DIGIT_ROWS = 16
 ROTATE_VMEM = 56 << 20
 
 
@@ -51,7 +53,7 @@
     return out
 
 
-def call(kernel, out_shape, args, flops, scratch=(), in_specs=None, out_specs=None, vmem=24 << 20):
+def call(kernel, out_shape, args, flops, scratch=(), in_specs=None, out_specs=None, vmem=16 << 20):
     outs = out_shape if isinstance(out_shape, (tuple, list)) else (out_shape,)
     size = sum(a.size * a.dtype.itemsize for a in list(args) + list(outs))
     return pl.pallas_call(
@@ -114,7 +116,7 @@
         hot[:, i : i + n] = (turned[:, :n] == lanes).astype(BF16)
 
 
-def couple_kernel(capacity, weight, node_row, send_row, stiffness, to_ghost, to_own, scatter, spread, local):
+def couple_kernel(capacity, weight, node_row, send_row, stiffness, to_ghost, to_own, scatter, spread, to_near, far_near, local):
     nodes = stiffness.shape[0]
     ghosts = to_own.shape[0]
     slots = to_ghost.shape[2]
@@ -129,14 +131,24 @@
         to_ghost[block] = mm_nt(local[...], picks).astype(BF16)
     for i, n in steps(capacity, 256):
         to_own[:, i : i + n] = mm(local[...], scatter[:, i : i + n]).astype(BF16)
+    to_near[...] = mm_nt(to_own[...], spread[0]).astype(BF16)
+    far_near[...] = mm_nt(spread[1], spread[0]).astype(BF16)
+
+
+def same_kernel(capacity, first_near, same):
+    slots = same.shape[0]
+    digits = first_near[first_near.shape[0] - DIGIT_ROWS :, :].astype(F32)
+    rows = digits[0:1, :] * DIGIT + digits[1:2, :]
+    turned = jnp.broadcast_to(rows, (slots, slots)).T
+    same[...] = ((turned == rows) & (turned < capacity)).astype(BF16)
 
 
 def pick_rows(send_row, block, values, out):
     picks = rows_hot(send_row[block : block + 1, :], 0, values.shape[1])
-    out[...] = mm(values[...], picks).astype(BF16)
-
-
-def join_kernel(send_row, keep, after, *refs):
+    out[: values.shape[0], :] = mm(values[...], picks).astype(BF16)
+
+
+def join_kernel(send_row, keep, digits, after, *refs):
     bands = refs[-1].shape[0]
     pieces, (values, near_picked, held) = refs[:bands], refs[bands:]
     mine = lax.axis_index("band")
@@ -144,6 +156,9 @@
         held[mine ^ k] = piece[...]
     joined = jnp.concatenate([held[p] for p in range(bands)], axis=1)
     values[...] = jnp.where(keep[...] > 0, joined.astype(F32), 0.0).astype(BF16)
+    if near_picked.shape[0] > values.shape[0]:
+        near_picked[...] = jnp.zeros(near_picked.shape, BF16)
+        near_picked[near_picked.shape[0] - DIGIT_ROWS :, :] = digits[...]
     pick_rows(send_row, 0, values, near_picked)
 
 
@@ -155,10 +170,12 @@
         terms[block] = mm_nt(values[...], to_own[block * slots : (block + 1) * slots, :])
 
 
-def cells_kernel(first_step, weight, node_row, stiffness, scatter, potential, values, after, *refs):
+def cells_kernel(first_step, near_wanted, weight, node_row, stiffness, scatter, spread, potential, values, after, *refs):
     refs = list(refs)
     previous = None if first_step else refs.pop(0)
-    out, product, *locals_ = refs
+    out = refs.pop(0)
+    near_out = refs.pop(0) if near_wanted else None
+    product, *locals_ = refs
     capacity = values.shape[1]
     nodes = stiffness.shape[0]
     parts = steps(product.shape[1], nodes)
@@ -172,6 +189,8 @@
         shifted = sums + (potential[:, at] - CENTER) * values[:, at].astype(F32)
         result = shifted * scale_of(first_step)
         out[:, at] = result if first_step else result - previous[:, at].astype(F32)
+    if near_wanted:
+        near_out[...] = mm_nt(out[...].astype(BF16), spread[0])
 
 
 def ghost_sum(block, terms, to_ghost, arrived):
@@ -195,19 +214,56 @@
 
 def parcel_kernel(terms, to_ghost, near_ghosts, far_picked, parcel):
     width, slots = far_picked.shape
-    sums = ghost_sum(1, terms, to_ghost, [(0, near_ghosts[...])])
-    parcel[:width, :] = jnp.concatenate([far_picked[...], sums], axis=1)
+    sums = ghost_sum(1, terms, to_ghost, [(0, near_ghosts[:width, :])])
     if parcel.shape[0] > width:
         half = coupling_rows(slots)
         first = parcel.shape[0] - half
-        parcel[width:, :] = jnp.zeros((parcel.shape[0] - width, 2 * slots), BF16)
+        parcel[...] = jnp.zeros(parcel.shape, BF16)
         parcel[first:, :slots] = to_ghost[1, slots : slots + half, :]
         parcel[first : first + slots - half, slots:] = to_ghost[1, slots + half : 2 * slots, :]
+    parcel[:width, :] = jnp.concatenate([far_picked[...], sums], axis=1)
+
+
+def returned_sums(far_picked, parcel, first_parcel):
+    width, slots = far_picked.shape
+    half = coupling_rows(slots)
+    start = first_parcel.shape[0] - half
+    coupling = jnp.concatenate(
+        [first_parcel[start:, :slots], first_parcel[start : start + slots - half, slots:]], axis=0
+    )
+    returned = parcel[:width, slots:].astype(F32) + mm(far_picked[...], coupling)
+    return returned.astype(BF16)
+
+
+def pair_kernel(
+    first_step, terms, to_ghost, near_ghosts, far_picked, parcel, first_parcel, near_head, to_near, far_near, out
+):
+    width, slots = far_picked.shape
+    far_ghosts = parcel[:width, :slots]
+    sums = ghost_sum(0, terms, to_ghost, [(0, near_ghosts[:width, :]), (1, far_ghosts)])
+    returned = returned_sums(far_picked, parcel, first_parcel)
+    known = mm(near_ghosts[:width, :], to_near[:slots, :]) + mm(far_ghosts, to_near[slots:, :])
+    known = near_head[...] + (known + mm(returned, far_near[...])) * scale_of(first_step)
+    out[...] = jnp.concatenate([sums, known.astype(BF16)], axis=1)
+
+
+def advance_kernel(
+    first_step, spread, same, send_row, to_own, to_ghost, total, sent, arrived, values, near_ghosts, far_picked, terms, parcel
+):
+    slots = far_picked.shape[1]
+    sums = arrived[:, :slots]
+    for i, n in steps(values.shape[1], 256):
+        added = mm(sums, spread[0, :, i : i + n]) * scale_of(first_step)
+        values[:, i : i + n] = (total[:, i : i + n] + added).astype(BF16)
+    near = mm(sent[:, :slots], same[...]) * scale_of(first_step) + arrived[:, slots:].astype(F32)
+    near_ghosts[...] = near.astype(BF16)
+    terms_kernel(send_row, to_own, values, terms, far_picked)
+    parcel_kernel(terms, to_ghost, near_ghosts, far_picked, parcel)
 
 
 def near_kernel(terms, to_ghost, near_ghosts, parcel, after, out):
     width, slots = out.shape
-    arrived = [(0, near_ghosts[...]), (1, parcel[:width, :slots])]
+    arrived = [(0, near_ghosts[:width, :]), (1, parcel[:width, :slots])]
     out[...] = ghost_sum(0, terms, to_ghost, arrived)
 
 
@@ -227,14 +283,8 @@
     first_step, to_own, head, spread, near_ghosts, far_picked, parcel, first_parcel, out
 ):
     width, slots = far_picked.shape
-    ghosts = jnp.concatenate([near_ghosts[...], parcel[:width, :slots]], axis=1)
-    half = coupling_rows(slots)
-    start = first_parcel.shape[0] - half
-    coupling = jnp.concatenate(
-        [first_parcel[start:, :slots], first_parcel[start : start + slots - half, slots:]], axis=0
-    )
-    returned = parcel[:width, slots:].astype(F32) + mm(far_picked[...], coupling)
-    returned = returned.astype(BF16)
+    ghosts = jnp.concatenate([near_ghosts[:width, :], parcel[:width, :slots]], axis=1)
+    returned = returned_sums(far_picked, parcel, first_parcel)
     for i, n in steps(out.shape[1], 256):
         at = slice(i, i + n)
         sums = mm(ghosts, to_own[:, at]) + mm(returned, spread[1, :, at])
@@ -331,13 +381,15 @@
 
     local_rows = cells * nodes_pad
     cell_flops = 2 * local_rows * nodes_pad
-    to_ghost, to_own, scatter, spread = call(
+    to_ghost, to_own, scatter, spread, to_near, far_near = call(
         functools.partial(couple_kernel, capacity),
         (
             shape((blocks, ghosts, slots_pad), BF16),
             shape((ghosts, capacity), BF16),
             shape((local_rows, capacity), BF16),
             shape((blocks, slots_pad, capacity), BF16),
+            shape((ghosts, slots_pad), BF16),
+            shape((slots_pad, slots_pad), BF16),
         ),
         (weight, node_row, send_row, stiffness),
         (cell_flops + 2 * local_rows * (ghosts + capacity)) * ghosts,
@@ -345,47 +397,60 @@
     )
     block_shape = shape((width, slots_pad), BF16)
     keep = (jnp.arange(capacity, dtype=jnp.int32) < own_rows).astype(jnp.int32)[None, :]
+    near_rows = width if far else round_up(width, 16) + DIGIT_ROWS
+    digits = jnp.pad(
+        jnp.stack([send_row[0] // DIGIT, send_row[0] % DIGIT]), ((0, DIGIT_ROWS - 2), (0, 0))
+    ).astype(BF16)
     current, near_picked = call(
         join_kernel,
-        (shape((width, capacity), BF16), block_shape),
-        (send_row, keep, to_ghost, *pieces),
+        (shape((width, capacity), BF16), shape((near_rows, slots_pad), BF16)),
+        (send_row, keep, digits, to_ghost, *pieces),
         2 * slots_pad * capacity * width,
         scratch=[pltpu.VMEM((bands, width, piece_rows), BF16)],
-        in_specs=[VMEM, VMEM, ANY] + [VMEM] * bands,
+        in_specs=[VMEM, VMEM, VMEM, ANY] + [VMEM] * bands,
     )
     previous = None
     parcel_rows = round_up(width, 16) + coupling_rows(slots_pad)
-    first_parcel = None
+    terms_shape = shape((blocks, width, slots_pad), F32)
+    terms_flops = 4 * ghosts * capacity * width
     for filter_step in range(FILTER_STEPS):
         first, last = filter_step == 0, filter_step == FILTER_STEPS - 1
-        near = swap(near_picked, 0)
-        terms, *picked = call(
-            terms_kernel,
-            (shape((blocks, width, slots_pad), F32),) + (block_shape,) * (blocks - 1),
-            (send_row, to_own, current),
-            4 * ghosts * capacity * width,
-        )
+        if first or far:
+            near = swap(near_picked, 0)
+            terms, *picked = call(
+                terms_kernel,
+                (terms_shape,) + (block_shape,) * (blocks - 1),
+                (send_row, to_own, current),
+                terms_flops,
+            )
         if far:
             arrived = [near, *exchange(picked, False)]
             ready = terms
         else:
-            parcel = call(
-                parcel_kernel,
-                shape((parcel_rows if first else width, 2 * slots_pad), BF16),
-                (terms, to_ghost, near, picked[0]),
-                2 * slots_pad * slots_pad * width,
-            )
-            ready = parcel
-            parcel = swap(parcel, 1)
+            if first:
+                same = call(
+                    functools.partial(same_kernel, capacity),
+                    shape((slots_pad, slots_pad), BF16),
+                    (near,),
+                    slots_pad * slots_pad,
+                )
+                ready = call(
+                    parcel_kernel,
+                    shape((parcel_rows, 2 * slots_pad), BF16),
+                    (terms, to_ghost, near, picked[0]),
+                    2 * slots_pad * slots_pad * width,
+                )
+            parcel = swap(ready, 1)
             first_parcel = parcel if first else first_parcel
         history = () if first else (previous,)
-        head = call(
-            functools.partial(cells_kernel, first),
-            shape((width, capacity), F32),
-            (weight, node_row, stiffness, scatter, potential, current, ready, *history),
+        near_wanted = not far and not last
+        head, *near_head = call(
+            functools.partial(cells_kernel, first, near_wanted),
+            (shape((width, capacity), F32),) + (shape((width, slots_pad), F32),) * near_wanted,
+            (weight, node_row, stiffness, scatter, spread, potential, current, ready, *history),
             (cell_flops + 4 * local_rows * capacity) * width,
             scratch=[pltpu.VMEM((width, local_rows), BF16)] + [pltpu.VMEM((width, nodes_pad), BF16)] * cells,
-            in_specs=[VMEM] * 6 + [ANY] + [VMEM] * len(history),
+            in_specs=[VMEM] * 7 + [ANY] + [VMEM] * len(history),
         )
         own_flops = 2 * capacity * ghosts * width
         if far:
@@ -403,14 +468,22 @@
                 own_flops,
             )
         else:
-            sums = call(
-                near_kernel,
-                block_shape,
-                (terms, to_ghost, near, parcel, head),
-                2 * ghosts * slots_pad * width,
-                in_specs=[VMEM] * 4 + [ANY],
-            )
-            returned = [swap(sums, 0)]
+            if last:
+                sent = call(
+                    near_kernel,
+                    block_shape,
+                    (terms, to_ghost, near, parcel, head),
+                    2 * ghosts * slots_pad * width,
+                    in_specs=[VMEM] * 4 + [ANY],
+                )
+            else:
+                sent = call(
+                    functools.partial(pair_kernel, first),
+                    shape((width, 2 * slots_pad), BF16),
+                    (terms, to_ghost, near, picked[0], parcel, first_parcel, *near_head, to_near, far_near),
+                    6 * ghosts * slots_pad * width,
+                )
+            returned = [swap(sent, 0)]
             total = call(
                 functools.partial(paired_own_kernel, first),
                 shape((width, capacity), F32),
@@ -430,6 +503,21 @@
                 ],
                 out_specs=ANY,
             )
+        elif not far:
+            following, near, far_picked, terms, ready = call(
+                functools.partial(advance_kernel, first),
+                (
+                    shape((width, capacity), BF16),
+                    block_shape,
+                    block_shape,
+                    terms_shape,
+                    shape((width, 2 * slots_pad), BF16),
+                ),
+                (spread, same, send_row, to_own, to_ghost, total, sent, *returned),
+                update_flops + terms_flops,
+            )
+            picked = [far_picked]
+            previous, current = current, following
         else:
             following, near_picked = call(
                 functools.partial(update_kernel, len(returned), first),

time: 48.6 us -> 47.5 us (0.977)
  waiting for transfers between devices: 5.45 us -> 4.01 us
  Pallas kernels: 25.1 us -> 26.2 us
  starting transfers between devices: 16.2 us -> 15.4 us
    pallas_call x21 -> x18, Pallas kernels: 25.1 us -> 26.2 us  [call(): pl.pallas_call(kernel, out_shape=out_shape, in_specs=in_specs or [VMEM] *...]
    ppermute x9 -> x7, waiting for transfers between devices: 3.4 us -> 2.41 us  [swap(): return lax.ppermute(value, 'dom', pairs)]
    ppermute x9 -> x7, starting transfers between devices: 12.9 us -> 12.1 us  [swap(): return lax.ppermute(value, 'dom', pairs)]
  transfers between devices with their start and end apart: 12 -> 10, of which waited for: 10 -> 7; matrix products, arithmetic and copies ran while one was open for 1% -> 1% of each run, Pallas kernels for 36% -> 36%
where the time goes in v4:
time: 47.5 us; the launch traced here: 47.2 us
  Pallas kernels  26.2 us (55%)
  starting transfers between devices  15.4 us (32%)
  waiting for transfers between devices  4.01 us (8%)
  between operations  1.17 us (2%)
    pallas_call x18, Pallas kernels, call(): pl.pallas_call(kernel, out_shape=out_shape, in_specs=in_specs or [VMEM] *...  26.2 us
    ppermute x7, starting transfers between devices, swap(): return lax.ppermute(value, 'dom', pairs)  12.1 us
    ppermute x3, starting transfers between devices, shards(): lax.ppermute(pieces[k], 'band', [(i, i ^ k) for i in range(bands)])  3.37 us
    ppermute x7, waiting for transfers between devices, swap(): return lax.ppermute(value, 'dom', pairs)  2.41 us
    ppermute x3, waiting for transfers between devices, shards(): lax.ppermute(pieces[k], 'band', [(i, i ^ k) for i in range(bands)])  1.61 us
  transfers between devices with their start and end apart: 10, of which 7 were waited for; matrix products, arithmetic and copies ran while one was open for 1% of the time, Pallas kernels for 36%

profile of v4, /device:TPU:1, one launch (start us, length us, event | category | flops | bytes accessed | tf_op | source)
XLA Modules:
  0.0 47.2 jit_solution(10022694031743622109)
XLA Ops:
  0.0 0.0 copy-start.2
  0.0 3.5 %shard_map.83 = (bf16[200,352]{1,0:T(8,128)(2,1)}, bf16[200,352]{1,0:T(8,128)(2,1)}, bf16[200,352]{1,0:T(8,128)(2,1)}, bf16[200,352]{1,0:T(8,128)(2,1)}) custom-call(bf16[800,352]{1,0:T(8,128)(2,1)} %bitcast.36, bf16[800,800]{1,0:T(8,128)(2,1)} %rotation.1), custom_call_target="tpu_custom_call" | custom-call | flops 450560000 | bytes 2406400 | tf_op jit(solution)/shard_map/pallas_call | solution.py:59
  3.5 2.1 %collective-permute-start = (bf16[200,352]{1,0:T(8,128)(2,1)}, bf16[200,352]{1,0:T(8,128)(2,1)S(1)}, u32[]{:S(2)}, u32[]{:S(2)}) collective-permute-start(bf16[200,352]{1,0:T(8,128)(2,1)} %get-tuple-element.38), channel_id=1, source_target_pairs={{0,8},{8,0},{16,24},{24,16},{1,9},{9,1},{17,25},{25,17},{2,10},{10... | collective-permute-start | bytes 422408 | tf_op jit(solution)/shard_map/ppermute | solution.py:346
  5.6 1.2 %collective-permute-start.1 = (bf16[200,352]{1,0:T(8,128)(2,1)}, bf16[200,352]{1,0:T(8,128)(2,1)S(1)}, u32[]{:S(2)}, u32[]{:S(2)}) collective-permute-start(bf16[200,352]{1,0:T(8,128)(2,1)} %get-tuple-element.39), channel_id=1, source_target_pairs={{0,16},{8,24},{16,0},{24,8},{1,17},{9,25},{17,1},{25,9},{2,18},{10... | collective-permute-start | bytes 422408 | tf_op jit(solution)/shard_map/ppermute | solution.py:346
  6.9 0.0 collective-permute-start.2
  7.6 0.0 copy-done.4
  7.6 0.0 copy-done.3
  7.7 0.0 copy-done.5
  7.8 0.1 broadcast_bitcast_fusion
  7.8 0.0 copy-done.2
  7.9 0.1 pad.19.stiffness
  8.0 0.0 copy-start
  8.0 4.4 %shard_map.82 = (bf16[2,352,176]{2,1,0:T(8,128)(2,1)S(1)}, bf16[352,1408]{1,0:T(8,128)(2,1)S(1)}, bf16[1536,1408]{1,0:T(8,128)(2,1)S(1)}, bf16[2,176,1408]{2,1,0...) custom-call(f32[1,1536]{1,0:T(1,128)S(1)} %bitcast.32, s32[1,1536]{1,0:T(1,128)S(1)} %bitcast.28, ...), custom_call_target="tpu_custom_call" | custom-call | flops 2733637632 | bytes 7934848 | tf_op jit(solution)/shard_map/pallas_call | solution.py:59
  12.4 0.0 collective-permute-done.refs_1_
  12.4 0.0 collective-permute-done.1.refs_2_
  12.4 1.6 %collective-permute-done.2.refs_3_ = bf16[200,352]{1,0:T(8,128)(2,1)S(1)} collective-permute-done((bf16[200,352]{1,0:T(8,128)(2,1)}, bf16[200,352]{1,0:T(8,128)(2,1)S(1)}, u32[]{:S(2)}, u32[]{:S(2)}) %collective-permute-start.2) | collective-permute-done | bytes 140832 | tf_op jit(solution)/shard_map/ppermute | solution.py:346
  14.1 0.0 copy-done
  14.1 0.5 %shard_map.84 = (bf16[200,1408]{1,0:T(8,128)(2,1)S(1)}, bf16[224,176]{1,0:T(8,128)(2,1)S(1)}) custom-call(s32[2,176]{1,0:T(2,128)S(1)} %pad.18.send_row, s32[1,1408]{1,0:T(1,128)S(1)} %compare_convert_fusion.keep, bf16[16,176]{1,0:T(8,128)(2,1)S(1)} %fusion.2.digits, bf16[2,352,176]{2,1,0:T(8,128)(2,1)S(1)} %get-tuple-element.36.after.to_ghost, ...), custom_call_target="tpu_custom_call" | custom-call | flops 99123200 | bytes 1465728 | tf_op jit(solution)/shard_map/pallas_call | solution.py:59
  14.6 1.5 %collective-permute-start.3 = (bf16[224,176]{1,0:T(8,128)(2,1)S(1)}, bf16[224,176]{1,0:T(8,128)(2,1)S(1)}, u32[]{:S(2)}, u32[]{:S(2)}) collective-permute-start(bf16[224,176]{1,0:T(8,128)(2,1)S(1)} %get-tuple-element.41), channel_id=1, source_target_pairs={{0,1},{1,0},{2,3},{3,2},{4,5},{5,4},{6,7},{7,6},{8,9},{9,8},{10,11... | collective-permute-start | bytes 236552 | tf_op jit(solution)/shard_map/ppermute | solution.py:36
  16.1 0.7 %shard_map.86 = (f32[2,200,176]{2,1,0:T(8,128)S(1)}, bf16[200,176]{1,0:T(8,128)(2,1)S(1)}) custom-call(s32[2,176]{1,0:T(2,128)S(1)} %pad.18.send_row, bf16[352,1408]{1,0:T(8,128)(2,1)S(1)} %get-tuple-element.34.to_own, bf16[200,1408]{1,0:T(8,128)(2,1)S(1)} %get-tuple-element.42.values.refs_0_), custom_call_target="tpu_custom_call" | custom-call | flops 396492800 | bytes 1907840 | tf_op jit(solution)/shard_map/pallas_call | solution.py:59
  16.8 0.3 collective-permute-done.3.first_near.near_ghosts
  17.1 0.2 shard_map.87.after
  17.3 3.5 %collective-permute-start.4 = (bf16[304,352]{1,0:T(8,128)(2,1)S(1)}, bf16[304,352]{1,0:T(8,128)(2,1)S(1)}, u32[]{:S(2)}, u32[]{:S(2)}) collective-permute-start(bf16[304,352]{1,0:T(8,128)(2,1)S(1)} %shard_map.87.after), channel_id=1, source_target_pairs={{1,2},{2,1},{3,4},{4,3},{5,6},{6,5},{9,10},{10,9},{11,12},{12,11},... | collective-permute-start | bytes 642056 | tf_op jit(solution)/shard_map/ppermute | solution.py:36
  20.8 0.0 copy-done.1
  20.8 3.1 %shard_map.88 = (f32[200,1408]{1,0:T(8,128)S(1)}, f32[200,176]{1,0:T(8,128)S(1)}) custom-call(f32[1,1536]{1,0:T(1,128)S(1)} %bitcast.33, s32[1,1536]{1,0:T(1,128)S(1)} %bitcast.29, bf16[768,768]{1,0:T(8,128)(2,1)S(1)} %pad.19.stiffness, bf16[1536,1408]{1,0:T(8,128)(2,1)S(1)} %get-tuple-element.35.scatter, ...), custom_call_target="tpu_custom_call" | custom-call | flops 2202009600 | bytes 8558592 | tf_op jit(solution)/shard_map/pallas_call | solution.py:59
  23.9 0.9 %collective-permute-done.4.parcel.first_parcel = bf16[304,352]{1,0:T(8,128)(2,1)S(1)} collective-permute-done((bf16[304,352]{1,0:T(8,128)(2,1)S(1)}, bf16[304,352]{1,0:T(8,128)(2,1)S(1)}, u32[]{:S(2)}, u32[]{:S(2)}) %collective-permute-start.4) | collective-permute-done | bytes 214048 | tf_op jit(solution)/shard_map/ppermute | solution.py:36
  24.7 0.7 %shard_map.90.sent = bf16[200,352]{1,0:T(8,128)(2,1)S(1)} custom-call(f32[2,200,176]{2,1,0:T(8,128)S(1)} %get-tuple-element.43.terms, bf16[2,352,176]{2,1,0:T(8,128)(2,1)S(1)} %get-tuple-element.36.after.to_ghost, bf16[224,176]{1,0:T(8,128)(2,1)S(1)} %collective-permute-done.3.first_near.near_ghosts, bf16[200,176]{1,0:T(8,128)(2,1)S(1)} %get-tuple-element.44.far_picked, ...), custom_call_target="tpu_custom_call" | custom-call | flops 74342400 | bytes 1574144 | tf_op jit(solution)/shard_map/pallas_call | solution.py:59
  25.4 0.1 collective-permute-start.5
  25.5 0.1 shard_map.85.same
  25.6 1.0 %shard_map.89.total = f32[200,1408]{1,0:T(8,128)S(1)} custom-call(bf16[352,1408]{1,0:T(8,128)(2,1)S(1)} %get-tuple-element.34.to_own, f32[200,1408]{1,0:T(8,128)S(1)} %get-tuple-element.45.head, bf16[2,176,1408]{2,1,0:T(8,128)(2,1)S(1)} %get-tuple-element.33.spread, bf16[224,176]{1,0:T(8,128)(2,1)S(1)} %collective-permute-done.3.first_near.near_ghosts, ...), custom_call_target="tpu_custom_call" | custom-call | flops 198246400 | bytes 4812544 | tf_op jit(solution)/shard_map/pallas_call | solution.py:59
  26.6 0.2 collective-permute-done.5.arrived
  26.8 1.1 %shard_map.91 = (bf16[200,1408]{1,0:T(8,128)(2,1)S(1)}, bf16[200,176]{1,0:T(8,128)(2,1)S(1)}, bf16[200,176]{1,0:T(8,128)(2,1)S(1)}, f32[2,200,176]{2,1,0:T(8,128)S(1)}, bf16[200,352]{1,0:T(8,128)(2,1)S(1)}) custom-call(bf16[2,176,1408]{2,1,0:T(8,128)(2,1)S(1)} %get-tuple-element.33.spread, bf16[176,176]{1,0:T(8,128)(2,1)S(1)} %shard_map.85.same, ...), custom_call_target="tpu_custom_call" | custom-call | flops 693862400 | bytes 4828032 | tf_op jit(solution)/shard_map/pallas_call | solution.py:59
  27.9 3.6 %collective-permute-start.6 = (bf16[200,352]{1,0:T(8,128)(2,1)S(1)}, bf16[200,352]{1,0:T(8,128)(2,1)S(1)}, u32[]{:S(2)}, u32[]{:S(2)}) collective-permute-start(bf16[200,352]{1,0:T(8,128)(2,1)S(1)} %get-tuple-element.50.after), channel_id=1, source_target_pairs={{1,2},{2,1},{3,4},{4,3},{5,6},{6,5},{9,10},{10,9},{11,12},{12,11},... | collective-permute-start | bytes 422408 | tf_op jit(solution)/shard_map/ppermute | solution.py:36
  31.5 3.1 %shard_map.92 = (f32[200,1408]{1,0:T(8,128)S(1)}, f32[200,176]{1,0:T(8,128)S(1)}) custom-call(f32[1,1536]{1,0:T(1,128)S(1)} %bitcast.34, s32[1,1536]{1,0:T(1,128)S(1)} %bitcast.30, bf16[768,768]{1,0:T(8,128)(2,1)S(1)} %pad.19.stiffness, bf16[1536,1408]{1,0:T(8,128)(2,1)S(1)} %get-tuple-element.35.scatter, ...), custom_call_target="tpu_custom_call" | custom-call | flops 2202009600 | bytes 9048576 | tf_op jit(solution)/shard_map/pallas_call | solution.py:59
  34.6 0.0 collective-permute-done.6.parcel
  34.6 0.7 %shard_map.94.sent = bf16[200,352]{1,0:T(8,128)(2,1)S(1)} custom-call(f32[2,200,176]{2,1,0:T(8,128)S(1)} %get-tuple-element.54.terms, bf16[2,352,176]{2,1,0:T(8,128)(2,1)S(1)} %get-tuple-element.36.after.to_ghost, bf16[200,176]{1,0:T(8,128)(2,1)S(1)} %get-tuple-element.52.near_ghosts, bf16[200,176]{1,0:T(8,128)(2,1)S(1)} %get-tuple-element.53.far_picked, ...), custom_call_target="tpu_custom_call" | custom-call | flops 74342400 | bytes 1492480 | tf_op jit(solution)/shard_map/pallas_call | solution.py:59
  35.3 0.1 collective-permute-start.7
  35.4 1.0 %shard_map.93.total = f32[200,1408]{1,0:T(8,128)S(1)} custom-call(bf16[352,1408]{1,0:T(8,128)(2,1)S(1)} %get-tuple-element.34.to_own, f32[200,1408]{1,0:T(8,128)S(1)} %get-tuple-element.51.head, bf16[2,176,1408]{2,1,0:T(8,128)(2,1)S(1)} %get-tuple-element.33.spread, bf16[200,176]{1,0:T(8,128)(2,1)S(1)} %get-tuple-element.52.near_ghosts, ...), custom_call_target="tpu_custom_call" | custom-call | flops 198246400 | bytes 4730880 | tf_op jit(solution)/shard_map/pallas_call | solution.py:59
  36.4 0.3 collective-permute-done.7.arrived
  36.7 1.1 %shard_map.95 = (bf16[200,1408]{1,0:T(8,128)(2,1)S(1)}, bf16[200,176]{1,0:T(8,128)(2,1)S(1)}, bf16[200,176]{1,0:T(8,128)(2,1)S(1)}, f32[2,200,176]{2,1,0:T(8,128)S(1)}, bf16[200,352]{1,0:T(8,128)(2,1)S(1)}) custom-call(bf16[2,176,1408]{2,1,0:T(8,128)(2,1)S(1)} %get-tuple-element.33.spread, bf16[176,176]{1,0:T(8,128)(2,1)S(1)} %shard_map.85.same, ...), custom_call_target="tpu_custom_call" | custom-call | flops 693862400 | bytes 4828032 | tf_op jit(solution)/shard_map/pallas_call | solution.py:59
  37.8 3.2 %collective-permute-start.8 = (bf16[200,352]{1,0:T(8,128)(2,1)S(1)}, bf16[200,352]{1,0:T(8,128)(2,1)S(1)}, u32[]{:S(2)}, u32[]{:S(2)}) collective-permute-start(bf16[200,352]{1,0:T(8,128)(2,1)S(1)} %get-tuple-element.57.after), channel_id=1, source_target_pairs={{1,2},{2,1},{3,4},{4,3},{5,6},{6,5},{9,10},{10,9},{11,12},{12,11},... | collective-permute-start | bytes 422408 | tf_op jit(solution)/shard_map/ppermute | solution.py:36
  41.1 2.8 %shard_map.96.head.after = f32[200,1408]{1,0:T(8,128)S(1)} custom-call(f32[1,1536]{1,0:T(1,128)S(1)} %bitcast.35, s32[1,1536]{1,0:T(1,128)S(1)} %bitcast.31, bf16[768,768]{1,0:T(8,128)(2,1)S(1)} %pad.19.stiffness, bf16[1536,1408]{1,0:T(8,128)(2,1)S(1)} %get-tuple-element.35.scatter, bf16[2,176,1408]{2,1,0:T(8,128)(2,1)S(1)} %get-tuple-element.33.spread, ...), custom_call_target="tpu_custom_call" | custom-call | flops 2202009600 | bytes 8907776 | tf_op jit(solution)/shard_map/pallas_call | solution.py:59
  43.9 0.5 collective-permute-done.8.parcel
  44.4 0.2 shard_map.98
  44.6 0.1 collective-permute-start.9
  44.6 1.0 %shard_map.97.total = f32[200,1408]{1,0:T(8,128)S(1)} custom-call(bf16[352,1408]{1,0:T(8,128)(2,1)S(1)} %get-tuple-element.34.to_own, f32[200,1408]{1,0:T(8,128)S(1)} %shard_map.96.head.after, bf16[2,176,1408]{2,1,0:T(8,128)(2,1)S(1)} %get-tuple-element.33.spread, bf16[200,176]{1,0:T(8,128)(2,1)S(1)} %get-tuple-element.58.near_ghosts, ...), custom_call_target="tpu_custom_call" | custom-call | flops 198246400 | bytes 4730880 | tf_op jit(solution)/shard_map/pallas_call | solution.py:59
  45.7 0.3 collective-permute-done.9.refs_0_
  45.9 1.1 %shard_map.99 = bf16[200,1408]{1,0:T(8,128)(2,1)} custom-call(bf16[2,176,1408]{2,1,0:T(8,128)(2,1)S(1)} %get-tuple-element.33.spread, f32[200,1408]{1,0:T(8,128)S(1)} %shard_map.97.total, bf16[200,176]{1,0:T(8,128)(2,1)S(1)} %collective-permute-done.9.refs_0_), custom_call_target="tpu_custom_call" | custom-call | flops 297369600 | bytes 2751232 | tf_op jit(solution)/shard_map/pallas_call | solution.py:59
  (16 shorter events, 0.1 us)
Async XLA Ops:
  0.0 7.6 %copy-start.4 = (s32[1,4,162]{2,1,0:T(4,128)S(1)}, s32[1,4,162]{2,1,0:T(4,128)}, u32[]{:S(2)}) copy-start(s32[1,4,162]{2,1,0:T(4,128)} %param.14) | copy-start | bytes 7780
  0.0 7.6 %copy-start.3 = (s32[1,2,729]{2,1,0:T(2,128)S(1)}, s32[1,2,729]{2,1,0:T(2,128)}, u32[]{:S(2)}) copy-start(s32[1,2,729]{2,1,0:T(2,128)} %param.13) | copy-start | bytes 17500
  0.0 7.7 %copy-start.5 = (f32[1,2]{1,0:T(1,128)S(1)}, f32[1,2]{1,0:T(1,128)}, u32[]{:S(2)}) copy-start(f32[1,2]{1,0:T(1,128)} %param.11) | copy-start | bytes 28
  0.0 7.8 %copy-start.2 = (bf16[729,729]{1,0:T(8,128)(2,1)S(1)}, bf16[729,729]{1,0:T(8,128)(2,1)}, u32[]{:S(2)}) copy-start(bf16[729,729]{1,0:T(8,128)(2,1)} %param.10) | copy-start | bytes 3188650
  3.5 8.9 %collective-permute-start = (bf16[200,352]{1,0:T(8,128)(2,1)}, bf16[200,352]{1,0:T(8,128)(2,1)S(1)}, u32[]{:S(2)}, u32[]{:S(2)}) collective-permute-start(bf16[200,352]{1,0:T(8,128)(2,1)} %get-tuple-element.38), channel_id=1, source_target_pairs={{0,8},{8,0},{16,24},{24,16},{1,9},{9,1},{17,25},{25,17},{2,10},{10... | collective-permute-start | bytes 422408 | tf_op jit(solution)/shard_map/ppermute | solution.py:346
  5.6 6.8 %collective-permute-start.1 = (bf16[200,352]{1,0:T(8,128)(2,1)}, bf16[200,352]{1,0:T(8,128)(2,1)S(1)}, u32[]{:S(2)}, u32[]{:S(2)}) collective-permute-start(bf16[200,352]{1,0:T(8,128)(2,1)} %get-tuple-element.39), channel_id=1, source_target_pairs={{0,16},{8,24},{16,0},{24,8},{1,17},{9,25},{17,1},{25,9},{2,18},{10... | collective-permute-start | bytes 422408 | tf_op jit(solution)/shard_map/ppermute | solution.py:346
  6.9 7.2 %collective-permute-start.2 = (bf16[200,352]{1,0:T(8,128)(2,1)}, bf16[200,352]{1,0:T(8,128)(2,1)S(1)}, u32[]{:S(2)}, u32[]{:S(2)}) collective-permute-start(bf16[200,352]{1,0:T(8,128)(2,1)} %get-tuple-element.40), channel_id=1, source_target_pairs={{0,24},{8,16},{16,8},{24,0},{1,25},{9,17},{17,9},{25,1},{2,26},{10... | collective-permute-start | bytes 422408 | tf_op jit(solution)/shard_map/ppermute | solution.py:346
  8.0 6.1 %copy-start = (bf16[200,352]{1,0:T(8,128)(2,1)S(1)}, bf16[200,352]{1,0:T(8,128)(2,1)}, u32[]{:S(2)}) copy-start(bf16[200,352]{1,0:T(8,128)(2,1)} %get-tuple-element.37.refs_0_) | copy-start | bytes 422404
  14.6 2.5 %collective-permute-start.3 = (bf16[224,176]{1,0:T(8,128)(2,1)S(1)}, bf16[224,176]{1,0:T(8,128)(2,1)S(1)}, u32[]{:S(2)}, u32[]{:S(2)}) collective-permute-start(bf16[224,176]{1,0:T(8,128)(2,1)S(1)} %get-tuple-element.41), channel_id=1, source_target_pairs={{0,1},{1,0},{2,3},{3,2},{4,5},{5,4},{6,7},{7,6},{8,9},{9,8},{10,11... | collective-permute-start | bytes 236552 | tf_op jit(solution)/shard_map/ppermute | solution.py:36
  16.1 4.7 %copy-start.1 = (f32[1,1408]{1,0:T(1,128)S(1)}, f32[1,1408]{1,0:T(1,128)}, u32[]{:S(2)}) copy-start(f32[1,1408]{1,0:T(1,128)} %potential.5) | copy-start | bytes 16900
  17.3 7.4 %collective-permute-start.4 = (bf16[304,352]{1,0:T(8,128)(2,1)S(1)}, bf16[304,352]{1,0:T(8,128)(2,1)S(1)}, u32[]{:S(2)}, u32[]{:S(2)}) collective-permute-start(bf16[304,352]{1,0:T(8,128)(2,1)S(1)} %shard_map.87.after), channel_id=1, source_target_pairs={{1,2},{2,1},{3,4},{4,3},{5,6},{6,5},{9,10},{10,9},{11,12},{12,11},... | collective-permute-start | bytes 642056 | tf_op jit(solution)/shard_map/ppermute | solution.py:36
  25.4 1.4 %collective-permute-start.5 = (bf16[200,352]{1,0:T(8,128)(2,1)S(1)}, bf16[200,352]{1,0:T(8,128)(2,1)S(1)}, u32[]{:S(2)}, u32[]{:S(2)}) collective-permute-start(bf16[200,352]{1,0:T(8,128)(2,1)S(1)} %shard_map.90.sent), channel_id=1, source_target_pairs={{0,1},{1,0},{2,3},{3,2},{4,5},{5,4},{6,7},{7,6},{8,9},{9,8},{10,11... | collective-permute-start | bytes 422408 | tf_op jit(solution)/shard_map/ppermute | solution.py:36
  27.9 6.7 %collective-permute-start.6 = (bf16[200,352]{1,0:T(8,128)(2,1)S(1)}, bf16[200,352]{1,0:T(8,128)(2,1)S(1)}, u32[]{:S(2)}, u32[]{:S(2)}) collective-permute-start(bf16[200,352]{1,0:T(8,128)(2,1)S(1)} %get-tuple-element.50.after), channel_id=1, source_target_pairs={{1,2},{2,1},{3,4},{4,3},{5,6},{6,5},{9,10},{10,9},{11,12},{12,11},... | collective-permute-start | bytes 422408 | tf_op jit(solution)/shard_map/ppermute | solution.py:36
  35.3 1.4 %collective-permute-start.7 = (bf16[200,352]{1,0:T(8,128)(2,1)S(1)}, bf16[200,352]{1,0:T(8,128)(2,1)S(1)}, u32[]{:S(2)}, u32[]{:S(2)}) collective-permute-start(bf16[200,352]{1,0:T(8,128)(2,1)S(1)} %shard_map.94.sent), channel_id=1, source_target_pairs={{0,1},{1,0},{2,3},{3,2},{4,5},{5,4},{6,7},{7,6},{8,9},{9,8},{10,11... | collective-permute-start | bytes 422408 | tf_op jit(solution)/shard_map/ppermute | solution.py:36
  37.8 6.5 %collective-permute-start.8 = (bf16[200,352]{1,0:T(8,128)(2,1)S(1)}, bf16[200,352]{1,0:T(8,128)(2,1)S(1)}, u32[]{:S(2)}, u32[]{:S(2)}) collective-permute-start(bf16[200,352]{1,0:T(8,128)(2,1)S(1)} %get-tuple-element.57.after), channel_id=1, source_target_pairs={{1,2},{2,1},{3,4},{4,3},{5,6},{6,5},{9,10},{10,9},{11,12},{12,11},... | collective-permute-start | bytes 422408 | tf_op jit(solution)/shard_map/ppermute | solution.py:36
  44.6 1.4 %collective-permute-start.9 = (bf16[200,176]{1,0:T(8,128)(2,1)S(1)}, bf16[200,176]{1,0:T(8,128)(2,1)S(1)}, u32[]{:S(2)}, u32[]{:S(2)}) collective-permute-start(bf16[200,176]{1,0:T(8,128)(2,1)S(1)} %shard_map.98), channel_id=1, source_target_pairs={{0,1},{1,0},{2,3},{3,2},{4,5},{5,4},{6,7},{7,6},{8,9},{9,8},{10,11... | collective-permute-start | bytes 211208 | tf_op jit(solution)/shard_map/ppermute | solution.py:36

commit v5 on v4

--- a/solution.py
+++ b/solution.py
@@ -21,7 +21,7 @@
 LANES = 128
 DIGIT = 64
 DIGIT_ROWS = 16
-ROTATE_VMEM = 56 << 20
+ROTATE_VMEM = 53 << 20
 
 
 def round_up(value, multiple):

time: 47.5 us -> 46.5 us (0.979)
  Pallas kernels: 26.2 us -> 25.4 us
    pallas_call x18, Pallas kernels: 26.2 us -> 25.4 us  [call(): pl.pallas_call(kernel, out_shape=out_shape, in_specs=in_specs or [VMEM] *...]
  transfers between devices with their start and end apart: 10 -> 10, of which waited for: 7 -> 7; matrix products, arithmetic and copies ran while one was open for 1% -> 1% of each run, Pallas kernels for 36% -> 37%
where the time goes in v5:
time: 46.5 us; the launch traced here: 46.2 us
  Pallas kernels  25.4 us (55%)
  starting transfers between devices  15.4 us (33%)
  waiting for transfers between devices  3.81 us (8%)
  between operations  1.16 us (2%)
    pallas_call x18, Pallas kernels, call(): pl.pallas_call(kernel, out_shape=out_shape, in_specs=in_specs or [VMEM] *...  25.4 us
    ppermute x7, starting transfers between devices, swap(): return lax.ppermute(value, 'dom', pairs)  12.1 us
    ppermute x3, starting transfers between devices, shards(): lax.ppermute(pieces[k], 'band', [(i, i ^ k) for i in range(bands)])  3.37 us
    ppermute x7, waiting for transfers between devices, swap(): return lax.ppermute(value, 'dom', pairs)  2.39 us
    ppermute x3, waiting for transfers between devices, shards(): lax.ppermute(pieces[k], 'band', [(i, i ^ k) for i in range(bands)])  1.43 us
  transfers between devices with their start and end apart: 10, of which 7 were waited for; matrix products, arithmetic and copies ran while one was open for 1% of the time, Pallas kernels for 37%

profile of v5, /device:TPU:1, one launch (start us, length us, event | category | flops | bytes accessed | tf_op | source)
XLA Modules:
  0.0 46.2 jit_solution(12361671400486269522)
XLA Ops:
  0.0 0.0 copy-start.3
  0.0 0.0 copy-start.2
  0.0 0.0 copy-start.1
  0.0 2.7 %shard_map.83 = (bf16[200,352]{1,0:T(8,128)(2,1)S(1)}, bf16[200,352]{1,0:T(8,128)(2,1)S(1)}, bf16[200,352]{1,0:T(8,128)(2,1)S(1)}, bf16[200,352]{1,0:T(8,128)(2,1)S(1)}) custom-call(bf16[800,352]{1,0:T(8,128)(2,1)} %bitcast.36, bf16[800,800]{1,0:T(8,128)(2,1)} %rotation.1), custom_call_target="tpu_custom_call" | custom-call | flops 450560000 | bytes 2406400 | tf_op jit(solution)/shard_map/pallas_call | solution.py:59
  2.7 2.1 %collective-permute-start = (bf16[200,352]{1,0:T(8,128)(2,1)S(1)}, bf16[200,352]{1,0:T(8,128)(2,1)S(1)}, u32[]{:S(2)}, u32[]{:S(2)}) collective-permute-start(bf16[200,352]{1,0:T(8,128)(2,1)S(1)} %get-tuple-element.38), channel_id=1, source_target_pairs={{0,8},{8,0},{16,24},{24,16},{1,9},{9,1},{17,25},{25,17},{2,10},{10... | collective-permute-start | bytes 422408 | tf_op jit(solution)/shard_map/ppermute | solution.py:346
  4.8 1.3 %collective-permute-start.1 = (bf16[200,352]{1,0:T(8,128)(2,1)S(1)}, bf16[200,352]{1,0:T(8,128)(2,1)S(1)}, u32[]{:S(2)}, u32[]{:S(2)}) collective-permute-start(bf16[200,352]{1,0:T(8,128)(2,1)S(1)} %get-tuple-element.39), channel_id=1, source_target_pairs={{0,16},{8,24},{16,0},{24,8},{1,17},{9,25},{17,1},{25,9},{2,18},{10... | collective-permute-start | bytes 422408 | tf_op jit(solution)/shard_map/ppermute | solution.py:346
  6.1 0.0 collective-permute-start.2
  6.8 0.0 copy-done.3
  6.8 0.0 copy-done.2
  6.9 0.0 copy-done.4
  7.0 0.1 broadcast_bitcast_fusion
  7.1 0.0 copy-done.1
  7.1 0.1 pad.19.stiffness
  7.2 4.4 %shard_map.82 = (bf16[2,352,176]{2,1,0:T(8,128)(2,1)S(1)}, bf16[352,1408]{1,0:T(8,128)(2,1)S(1)}, bf16[1536,1408]{1,0:T(8,128)(2,1)S(1)}, bf16[2,176,1408]{2,1,0...) custom-call(f32[1,1536]{1,0:T(1,128)S(1)} %bitcast.32, s32[1,1536]{1,0:T(1,128)S(1)} %bitcast.28, ...), custom_call_target="tpu_custom_call" | custom-call | flops 2733637632 | bytes 7934848 | tf_op jit(solution)/shard_map/pallas_call | solution.py:59
  11.6 0.0 collective-permute-done.refs_1_
  11.6 0.0 collective-permute-done.1.refs_2_
  11.6 1.4 %collective-permute-done.2.refs_3_ = bf16[200,352]{1,0:T(8,128)(2,1)S(1)} collective-permute-done((bf16[200,352]{1,0:T(8,128)(2,1)S(1)}, bf16[200,352]{1,0:T(8,128)(2,1)S(1)}, u32[]{:S(2)}, u32[]{:S(2)}) %collective-permute-start.2) | collective-permute-done | bytes 140832 | tf_op jit(solution)/shard_map/ppermute | solution.py:346
  13.1 0.5 %shard_map.84 = (bf16[200,1408]{1,0:T(8,128)(2,1)S(1)}, bf16[224,176]{1,0:T(8,128)(2,1)S(1)}) custom-call(s32[2,176]{1,0:T(2,128)S(1)} %pad.18.send_row, s32[1,1408]{1,0:T(1,128)S(1)} %compare_convert_fusion.keep, bf16[16,176]{1,0:T(8,128)(2,1)S(1)} %fusion.2.digits, bf16[2,352,176]{2,1,0:T(8,128)(2,1)S(1)} %get-tuple-element.36.after.to_ghost, ...), custom_call_target="tpu_custom_call" | custom-call | flops 99123200 | bytes 1465728 | tf_op jit(solution)/shard_map/pallas_call | solution.py:59
  13.6 1.5 %collective-permute-start.3 = (bf16[224,176]{1,0:T(8,128)(2,1)S(1)}, bf16[224,176]{1,0:T(8,128)(2,1)S(1)}, u32[]{:S(2)}, u32[]{:S(2)}) collective-permute-start(bf16[224,176]{1,0:T(8,128)(2,1)S(1)} %get-tuple-element.41), channel_id=1, source_target_pairs={{0,1},{1,0},{2,3},{3,2},{4,5},{5,4},{6,7},{7,6},{8,9},{9,8},{10,11... | collective-permute-start | bytes 236552 | tf_op jit(solution)/shard_map/ppermute | solution.py:36
  15.1 0.7 %shard_map.86 = (f32[2,200,176]{2,1,0:T(8,128)S(1)}, bf16[200,176]{1,0:T(8,128)(2,1)S(1)}) custom-call(s32[2,176]{1,0:T(2,128)S(1)} %pad.18.send_row, bf16[352,1408]{1,0:T(8,128)(2,1)S(1)} %get-tuple-element.34.to_own, bf16[200,1408]{1,0:T(8,128)(2,1)S(1)} %get-tuple-element.42.values.refs_0_), custom_call_target="tpu_custom_call" | custom-call | flops 396492800 | bytes 1907840 | tf_op jit(solution)/shard_map/pallas_call | solution.py:59
  15.8 0.3 collective-permute-done.3.first_near.near_ghosts
  16.1 0.2 shard_map.87.after
  16.3 3.5 %collective-permute-start.4 = (bf16[304,352]{1,0:T(8,128)(2,1)S(1)}, bf16[304,352]{1,0:T(8,128)(2,1)S(1)}, u32[]{:S(2)}, u32[]{:S(2)}) collective-permute-start(bf16[304,352]{1,0:T(8,128)(2,1)S(1)} %shard_map.87.after), channel_id=1, source_target_pairs={{1,2},{2,1},{3,4},{4,3},{5,6},{6,5},{9,10},{10,9},{11,12},{12,11},... | collective-permute-start | bytes 642056 | tf_op jit(solution)/shard_map/ppermute | solution.py:36
  19.8 0.0 copy-done
  19.8 3.1 %shard_map.88 = (f32[200,1408]{1,0:T(8,128)S(1)}, f32[200,176]{1,0:T(8,128)S(1)}) custom-call(f32[1,1536]{1,0:T(1,128)S(1)} %bitcast.33, s32[1,1536]{1,0:T(1,128)S(1)} %bitcast.29, bf16[768,768]{1,0:T(8,128)(2,1)S(1)} %pad.19.stiffness, bf16[1536,1408]{1,0:T(8,128)(2,1)S(1)} %get-tuple-element.35.scatter, ...), custom_call_target="tpu_custom_call" | custom-call | flops 2202009600 | bytes 8558592 | tf_op jit(solution)/shard_map/pallas_call | solution.py:59
  22.9 0.9 %collective-permute-done.4.parcel.first_parcel = bf16[304,352]{1,0:T(8,128)(2,1)S(1)} collective-permute-done((bf16[304,352]{1,0:T(8,128)(2,1)S(1)}, bf16[304,352]{1,0:T(8,128)(2,1)S(1)}, u32[]{:S(2)}, u32[]{:S(2)}) %collective-permute-start.4) | collective-permute-done | bytes 214048 | tf_op jit(solution)/shard_map/ppermute | solution.py:36
  23.7 0.7 %shard_map.90.sent = bf16[200,352]{1,0:T(8,128)(2,1)S(1)} custom-call(f32[2,200,176]{2,1,0:T(8,128)S(1)} %get-tuple-element.43.terms, bf16[2,352,176]{2,1,0:T(8,128)(2,1)S(1)} %get-tuple-element.36.after.to_ghost, bf16[224,176]{1,0:T(8,128)(2,1)S(1)} %collective-permute-done.3.first_near.near_ghosts, bf16[200,176]{1,0:T(8,128)(2,1)S(1)} %get-tuple-element.44.far_picked, ...), custom_call_target="tpu_custom_call" | custom-call | flops 74342400 | bytes 1574144 | tf_op jit(solution)/shard_map/pallas_call | solution.py:59
  24.4 0.1 collective-permute-start.5
  24.5 0.1 shard_map.85.same
  24.6 1.0 %shard_map.89.total = f32[200,1408]{1,0:T(8,128)S(1)} custom-call(bf16[352,1408]{1,0:T(8,128)(2,1)S(1)} %get-tuple-element.34.to_own, f32[200,1408]{1,0:T(8,128)S(1)} %get-tuple-element.45.head, bf16[2,176,1408]{2,1,0:T(8,128)(2,1)S(1)} %get-tuple-element.33.spread, bf16[224,176]{1,0:T(8,128)(2,1)S(1)} %collective-permute-done.3.first_near.near_ghosts, ...), custom_call_target="tpu_custom_call" | custom-call | flops 198246400 | bytes 4812544 | tf_op jit(solution)/shard_map/pallas_call | solution.py:59
  25.6 0.2 collective-permute-done.5.arrived
  25.8 1.1 %shard_map.91 = (bf16[200,1408]{1,0:T(8,128)(2,1)S(1)}, bf16[200,176]{1,0:T(8,128)(2,1)S(1)}, bf16[200,176]{1,0:T(8,128)(2,1)S(1)}, f32[2,200,176]{2,1,0:T(8,128)S(1)}, bf16[200,352]{1,0:T(8,128)(2,1)S(1)}) custom-call(bf16[2,176,1408]{2,1,0:T(8,128)(2,1)S(1)} %get-tuple-element.33.spread, bf16[176,176]{1,0:T(8,128)(2,1)S(1)} %shard_map.85.same, ...), custom_call_target="tpu_custom_call" | custom-call | flops 693862400 | bytes 4828032 | tf_op jit(solution)/shard_map/pallas_call | solution.py:59
  26.9 3.6 %collective-permute-start.6 = (bf16[200,352]{1,0:T(8,128)(2,1)S(1)}, bf16[200,352]{1,0:T(8,128)(2,1)S(1)}, u32[]{:S(2)}, u32[]{:S(2)}) collective-permute-start(bf16[200,352]{1,0:T(8,128)(2,1)S(1)} %get-tuple-element.50.after), channel_id=1, source_target_pairs={{1,2},{2,1},{3,4},{4,3},{5,6},{6,5},{9,10},{10,9},{11,12},{12,11},... | collective-permute-start | bytes 422408 | tf_op jit(solution)/shard_map/ppermute | solution.py:36
  30.5 3.1 %shard_map.92 = (f32[200,1408]{1,0:T(8,128)S(1)}, f32[200,176]{1,0:T(8,128)S(1)}) custom-call(f32[1,1536]{1,0:T(1,128)S(1)} %bitcast.34, s32[1,1536]{1,0:T(1,128)S(1)} %bitcast.30, bf16[768,768]{1,0:T(8,128)(2,1)S(1)} %pad.19.stiffness, bf16[1536,1408]{1,0:T(8,128)(2,1)S(1)} %get-tuple-element.35.scatter, ...), custom_call_target="tpu_custom_call" | custom-call | flops 2202009600 | bytes 9048576 | tf_op jit(solution)/shard_map/pallas_call | solution.py:59
  33.6 0.0 collective-permute-done.6.parcel
  33.6 0.7 %shard_map.94.sent = bf16[200,352]{1,0:T(8,128)(2,1)S(1)} custom-call(f32[2,200,176]{2,1,0:T(8,128)S(1)} %get-tuple-element.54.terms, bf16[2,352,176]{2,1,0:T(8,128)(2,1)S(1)} %get-tuple-element.36.after.to_ghost, bf16[200,176]{1,0:T(8,128)(2,1)S(1)} %get-tuple-element.52.near_ghosts, bf16[200,176]{1,0:T(8,128)(2,1)S(1)} %get-tuple-element.53.far_picked, ...), custom_call_target="tpu_custom_call" | custom-call | flops 74342400 | bytes 1492480 | tf_op jit(solution)/shard_map/pallas_call | solution.py:59
  34.3 0.1 collective-permute-start.7
  34.4 1.0 %shard_map.93.total = f32[200,1408]{1,0:T(8,128)S(1)} custom-call(bf16[352,1408]{1,0:T(8,128)(2,1)S(1)} %get-tuple-element.34.to_own, f32[200,1408]{1,0:T(8,128)S(1)} %get-tuple-element.51.head, bf16[2,176,1408]{2,1,0:T(8,128)(2,1)S(1)} %get-tuple-element.33.spread, bf16[200,176]{1,0:T(8,128)(2,1)S(1)} %get-tuple-element.52.near_ghosts, ...), custom_call_target="tpu_custom_call" | custom-call | flops 198246400 | bytes 4730880 | tf_op jit(solution)/shard_map/pallas_call | solution.py:59
  35.4 0.3 collective-permute-done.7.arrived
  35.7 1.1 %shard_map.95 = (bf16[200,1408]{1,0:T(8,128)(2,1)S(1)}, bf16[200,176]{1,0:T(8,128)(2,1)S(1)}, bf16[200,176]{1,0:T(8,128)(2,1)S(1)}, f32[2,200,176]{2,1,0:T(8,128)S(1)}, bf16[200,352]{1,0:T(8,128)(2,1)S(1)}) custom-call(bf16[2,176,1408]{2,1,0:T(8,128)(2,1)S(1)} %get-tuple-element.33.spread, bf16[176,176]{1,0:T(8,128)(2,1)S(1)} %shard_map.85.same, ...), custom_call_target="tpu_custom_call" | custom-call | flops 693862400 | bytes 4828032 | tf_op jit(solution)/shard_map/pallas_call | solution.py:59
  36.8 3.3 %collective-permute-start.8 = (bf16[200,352]{1,0:T(8,128)(2,1)S(1)}, bf16[200,352]{1,0:T(8,128)(2,1)S(1)}, u32[]{:S(2)}, u32[]{:S(2)}) collective-permute-start(bf16[200,352]{1,0:T(8,128)(2,1)S(1)} %get-tuple-element.57.after), channel_id=1, source_target_pairs={{1,2},{2,1},{3,4},{4,3},{5,6},{6,5},{9,10},{10,9},{11,12},{12,11},... | collective-permute-start | bytes 422408 | tf_op jit(solution)/shard_map/ppermute | solution.py:36
  40.1 2.8 %shard_map.96.head.after = f32[200,1408]{1,0:T(8,128)S(1)} custom-call(f32[1,1536]{1,0:T(1,128)S(1)} %bitcast.35, s32[1,1536]{1,0:T(1,128)S(1)} %bitcast.31, bf16[768,768]{1,0:T(8,128)(2,1)S(1)} %pad.19.stiffness, bf16[1536,1408]{1,0:T(8,128)(2,1)S(1)} %get-tuple-element.35.scatter, bf16[2,176,1408]{2,1,0:T(8,128)(2,1)S(1)} %get-tuple-element.33.spread, ...), custom_call_target="tpu_custom_call" | custom-call | flops 2202009600 | bytes 8907776 | tf_op jit(solution)/shard_map/pallas_call | solution.py:59
  42.9 0.4 collective-permute-done.8.parcel
  43.4 0.2 shard_map.98
  43.6 0.1 collective-permute-start.9
  43.6 1.0 %shard_map.97.total = f32[200,1408]{1,0:T(8,128)S(1)} custom-call(bf16[352,1408]{1,0:T(8,128)(2,1)S(1)} %get-tuple-element.34.to_own, f32[200,1408]{1,0:T(8,128)S(1)} %shard_map.96.head.after, bf16[2,176,1408]{2,1,0:T(8,128)(2,1)S(1)} %get-tuple-element.33.spread, bf16[200,176]{1,0:T(8,128)(2,1)S(1)} %get-tuple-element.58.near_ghosts, ...), custom_call_target="tpu_custom_call" | custom-call | flops 198246400 | bytes 4730880 | tf_op jit(solution)/shard_map/pallas_call | solution.py:59
  44.7 0.3 collective-permute-done.9.refs_0_
  44.9 1.1 %shard_map.99 = bf16[200,1408]{1,0:T(8,128)(2,1)} custom-call(bf16[2,176,1408]{2,1,0:T(8,128)(2,1)S(1)} %get-tuple-element.33.spread, f32[200,1408]{1,0:T(8,128)S(1)} %shard_map.97.total, bf16[200,176]{1,0:T(8,128)(2,1)S(1)} %collective-permute-done.9.refs_0_), custom_call_target="tpu_custom_call" | custom-call | flops 297369600 | bytes 2751232 | tf_op jit(solution)/shard_map/pallas_call | solution.py:59
  (14 shorter events, 0.1 us)
Async XLA Ops:
  0.0 6.8 %copy-start.3 = (s32[1,4,162]{2,1,0:T(4,128)S(1)}, s32[1,4,162]{2,1,0:T(4,128)}, u32[]{:S(2)}) copy-start(s32[1,4,162]{2,1,0:T(4,128)} %param.14) | copy-start | bytes 7780
  0.0 6.8 %copy-start.2 = (s32[1,2,729]{2,1,0:T(2,128)S(1)}, s32[1,2,729]{2,1,0:T(2,128)}, u32[]{:S(2)}) copy-start(s32[1,2,729]{2,1,0:T(2,128)} %param.13) | copy-start | bytes 17500
  0.0 6.9 %copy-start.4 = (f32[1,2]{1,0:T(1,128)S(1)}, f32[1,2]{1,0:T(1,128)}, u32[]{:S(2)}) copy-start(f32[1,2]{1,0:T(1,128)} %param.11) | copy-start | bytes 28
  0.0 7.0 %copy-start.1 = (bf16[729,729]{1,0:T(8,128)(2,1)S(1)}, bf16[729,729]{1,0:T(8,128)(2,1)}, u32[]{:S(2)}) copy-start(bf16[729,729]{1,0:T(8,128)(2,1)} %param.10) | copy-start | bytes 3188650
  2.7 8.9 %collective-permute-start = (bf16[200,352]{1,0:T(8,128)(2,1)S(1)}, bf16[200,352]{1,0:T(8,128)(2,1)S(1)}, u32[]{:S(2)}, u32[]{:S(2)}) collective-permute-start(bf16[200,352]{1,0:T(8,128)(2,1)S(1)} %get-tuple-element.38), channel_id=1, source_target_pairs={{0,8},{8,0},{16,24},{24,16},{1,9},{9,1},{17,25},{25,17},{2,10},{10... | collective-permute-start | bytes 422408 | tf_op jit(solution)/shard_map/ppermute | solution.py:346
  4.8 6.8 %collective-permute-start.1 = (bf16[200,352]{1,0:T(8,128)(2,1)S(1)}, bf16[200,352]{1,0:T(8,128)(2,1)S(1)}, u32[]{:S(2)}, u32[]{:S(2)}) collective-permute-start(bf16[200,352]{1,0:T(8,128)(2,1)S(1)} %get-tuple-element.39), channel_id=1, source_target_pairs={{0,16},{8,24},{16,0},{24,8},{1,17},{9,25},{17,1},{25,9},{2,18},{10... | collective-permute-start | bytes 422408 | tf_op jit(solution)/shard_map/ppermute | solution.py:346
  6.1 7.0 %collective-permute-start.2 = (bf16[200,352]{1,0:T(8,128)(2,1)S(1)}, bf16[200,352]{1,0:T(8,128)(2,1)S(1)}, u32[]{:S(2)}, u32[]{:S(2)}) collective-permute-start(bf16[200,352]{1,0:T(8,128)(2,1)S(1)} %get-tuple-element.40), channel_id=1, source_target_pairs={{0,24},{8,16},{16,8},{24,0},{1,25},{9,17},{17,9},{25,1},{2,26},{10... | collective-permute-start | bytes 422408 | tf_op jit(solution)/shard_map/ppermute | solution.py:346
  13.6 2.5 %collective-permute-start.3 = (bf16[224,176]{1,0:T(8,128)(2,1)S(1)}, bf16[224,176]{1,0:T(8,128)(2,1)S(1)}, u32[]{:S(2)}, u32[]{:S(2)}) collective-permute-start(bf16[224,176]{1,0:T(8,128)(2,1)S(1)} %get-tuple-element.41), channel_id=1, source_target_pairs={{0,1},{1,0},{2,3},{3,2},{4,5},{5,4},{6,7},{7,6},{8,9},{9,8},{10,11... | collective-permute-start | bytes 236552 | tf_op jit(solution)/shard_map/ppermute | solution.py:36
  15.1 4.7 %copy-start = (f32[1,1408]{1,0:T(1,128)S(1)}, f32[1,1408]{1,0:T(1,128)}, u32[]{:S(2)}) copy-start(f32[1,1408]{1,0:T(1,128)} %potential.5) | copy-start | bytes 16900
  16.3 7.4 %collective-permute-start.4 = (bf16[304,352]{1,0:T(8,128)(2,1)S(1)}, bf16[304,352]{1,0:T(8,128)(2,1)S(1)}, u32[]{:S(2)}, u32[]{:S(2)}) collective-permute-start(bf16[304,352]{1,0:T(8,128)(2,1)S(1)} %shard_map.87.after), channel_id=1, source_target_pairs={{1,2},{2,1},{3,4},{4,3},{5,6},{6,5},{9,10},{10,9},{11,12},{12,11},... | collective-permute-start | bytes 642056 | tf_op jit(solution)/shard_map/ppermute | solution.py:36
  24.4 1.4 %collective-permute-start.5 = (bf16[200,352]{1,0:T(8,128)(2,1)S(1)}, bf16[200,352]{1,0:T(8,128)(2,1)S(1)}, u32[]{:S(2)}, u32[]{:S(2)}) collective-permute-start(bf16[200,352]{1,0:T(8,128)(2,1)S(1)} %shard_map.90.sent), channel_id=1, source_target_pairs={{0,1},{1,0},{2,3},{3,2},{4,5},{5,4},{6,7},{7,6},{8,9},{9,8},{10,11... | collective-permute-start | bytes 422408 | tf_op jit(solution)/shard_map/ppermute | solution.py:36
  26.9 6.8 %collective-permute-start.6 = (bf16[200,352]{1,0:T(8,128)(2,1)S(1)}, bf16[200,352]{1,0:T(8,128)(2,1)S(1)}, u32[]{:S(2)}, u32[]{:S(2)}) collective-permute-start(bf16[200,352]{1,0:T(8,128)(2,1)S(1)} %get-tuple-element.50.after), channel_id=1, source_target_pairs={{1,2},{2,1},{3,4},{4,3},{5,6},{6,5},{9,10},{10,9},{11,12},{12,11},... | collective-permute-start | bytes 422408 | tf_op jit(solution)/shard_map/ppermute | solution.py:36
  34.3 1.4 %collective-permute-start.7 = (bf16[200,352]{1,0:T(8,128)(2,1)S(1)}, bf16[200,352]{1,0:T(8,128)(2,1)S(1)}, u32[]{:S(2)}, u32[]{:S(2)}) collective-permute-start(bf16[200,352]{1,0:T(8,128)(2,1)S(1)} %shard_map.94.sent), channel_id=1, source_target_pairs={{0,1},{1,0},{2,3},{3,2},{4,5},{5,4},{6,7},{7,6},{8,9},{9,8},{10,11... | collective-permute-start | bytes 422408 | tf_op jit(solution)/shard_map/ppermute | solution.py:36
  36.8 6.5 %collective-permute-start.8 = (bf16[200,352]{1,0:T(8,128)(2,1)S(1)}, bf16[200,352]{1,0:T(8,128)(2,1)S(1)}, u32[]{:S(2)}, u32[]{:S(2)}) collective-permute-start(bf16[200,352]{1,0:T(8,128)(2,1)S(1)} %get-tuple-element.57.after), channel_id=1, source_target_pairs={{1,2},{2,1},{3,4},{4,3},{5,6},{6,5},{9,10},{10,9},{11,12},{12,11},... | collective-permute-start | bytes 422408 | tf_op jit(solution)/shard_map/ppermute | solution.py:36
  43.6 1.4 %collective-permute-start.9 = (bf16[200,176]{1,0:T(8,128)(2,1)S(1)}, bf16[200,176]{1,0:T(8,128)(2,1)S(1)}, u32[]{:S(2)}, u32[]{:S(2)}) collective-permute-start(bf16[200,176]{1,0:T(8,128)(2,1)S(1)} %shard_map.98), channel_id=1, source_target_pairs={{0,1},{1,0},{2,3},{3,2},{4,5},{5,4},{6,7},{7,6},{8,9},{9,8},{10,11... | collective-permute-start | bytes 211208 | tf_op jit(solution)/shard_map/ppermute | solution.py:36

commit v6 on v5

--- a/solution.py
+++ b/solution.py
@@ -116,7 +116,7 @@
         hot[:, i : i + n] = (turned[:, :n] == lanes).astype(BF16)
 
 
-def couple_kernel(capacity, weight, node_row, send_row, stiffness, to_ghost, to_own, scatter, spread, to_near, far_near, local):
+def couple_kernel(capacity, weight, node_row, send_row, stiffness, to_ghost, to_own, scatter, spread, far_near, pairing, local):
     nodes = stiffness.shape[0]
     ghosts = to_own.shape[0]
     slots = to_ghost.shape[2]
@@ -131,8 +131,11 @@
         to_ghost[block] = mm_nt(local[...], picks).astype(BF16)
     for i, n in steps(capacity, 256):
         to_own[:, i : i + n] = mm(local[...], scatter[:, i : i + n]).astype(BF16)
-    to_near[...] = mm_nt(to_own[...], spread[0]).astype(BF16)
     far_near[...] = mm_nt(spread[1], spread[0]).astype(BF16)
+    both = 2 * slots
+    to_near = mm_nt(to_own[:both, :], spread[0]).astype(BF16)
+    pairing[:both, :] = jnp.concatenate([to_ghost[0, :both, :], to_near], axis=1)
+    pairing[both:, :] = jnp.concatenate([jnp.zeros((slots, slots), BF16), far_near[...]], axis=1)
 
 
 def same_kernel(capacity, first_near, same):
@@ -173,6 +176,7 @@
 def cells_kernel(first_step, near_wanted, weight, node_row, stiffness, scatter, spread, potential, values, after, *refs):
     refs = list(refs)
     previous = None if first_step else refs.pop(0)
+    terms = refs.pop(0) if near_wanted else None
     out = refs.pop(0)
     near_out = refs.pop(0) if near_wanted else None
     product, *locals_ = refs
@@ -190,7 +194,8 @@
         result = shifted * scale_of(first_step)
         out[:, at] = result if first_step else result - previous[:, at].astype(F32)
     if near_wanted:
-        near_out[...] = mm_nt(out[...].astype(BF16), spread[0])
+        near_head = mm_nt(out[...].astype(BF16), spread[0])
+        near_out[...] = jnp.concatenate([terms[0], near_head], axis=1)
 
 
 def ghost_sum(block, terms, to_ghost, arrived):
@@ -224,27 +229,34 @@
     parcel[:width, :] = jnp.concatenate([far_picked[...], sums], axis=1)
 
 
+def unpacked_coupling(first_parcel, slots):
+    half = coupling_rows(slots)
+    start = first_parcel.shape[0] - half
+    return jnp.concatenate(
+        [first_parcel[start:, :slots], first_parcel[start : start + slots - half, slots:]], axis=0
+    )
+
+
 def returned_sums(far_picked, parcel, first_parcel):
     width, slots = far_picked.shape
-    half = coupling_rows(slots)
-    start = first_parcel.shape[0] - half
-    coupling = jnp.concatenate(
-        [first_parcel[start:, :slots], first_parcel[start : start + slots - half, slots:]], axis=0
-    )
+    coupling = unpacked_coupling(first_parcel, slots)
     returned = parcel[:width, slots:].astype(F32) + mm(far_picked[...], coupling)
     return returned.astype(BF16)
 
 
-def pair_kernel(
-    first_step, terms, to_ghost, near_ghosts, far_picked, parcel, first_parcel, near_head, to_near, far_near, out
-):
+def pair_kernel(first_step, near_ghosts, far_picked, parcel, near_head, pairing, coupling, *refs):
     width, slots = far_picked.shape
-    far_ghosts = parcel[:width, :slots]
-    sums = ghost_sum(0, terms, to_ghost, [(0, near_ghosts[:width, :]), (1, far_ghosts)])
-    returned = returned_sums(far_picked, parcel, first_parcel)
-    known = mm(near_ghosts[:width, :], to_near[:slots, :]) + mm(far_ghosts, to_near[slots:, :])
-    known = near_head[...] + (known + mm(returned, far_near[...])) * scale_of(first_step)
-    out[...] = jnp.concatenate([sums, known.astype(BF16)], axis=1)
+    if first_step:
+        far_near, out, coupled = refs
+        added = mm(unpacked_coupling(coupling, slots), far_near[...]).astype(BF16)
+        coupled[...] = jnp.concatenate([jnp.zeros((slots, slots), BF16), added], axis=1)
+    else:
+        (out,), coupled = refs, coupling
+    both = mm(near_ghosts[:width, :], pairing[:slots, :])
+    both = both + mm(parcel[:width, :], pairing[slots:, :]) + mm(far_picked[...], coupled[...])
+    lanes = lax.broadcasted_iota(jnp.int32, (1, 2 * slots), 1)
+    scale = jnp.where(lanes < slots, 1.0, scale_of(first_step))
+    out[...] = (near_head[...] + both * scale).astype(BF16)
 
 
 def advance_kernel(
@@ -381,15 +393,15 @@
 
     local_rows = cells * nodes_pad
     cell_flops = 2 * local_rows * nodes_pad
-    to_ghost, to_own, scatter, spread, to_near, far_near = call(
+    to_ghost, to_own, scatter, spread, far_near, pairing = call(
         functools.partial(couple_kernel, capacity),
         (
             shape((blocks, ghosts, slots_pad), BF16),
             shape((ghosts, capacity), BF16),
             shape((local_rows, capacity), BF16),
             shape((blocks, slots_pad, capacity), BF16),
-            shape((ghosts, slots_pad), BF16),
             shape((slots_pad, slots_pad), BF16),
+            shape((3 * slots_pad, 2 * slots_pad), BF16),
         ),
         (weight, node_row, send_row, stiffness),
         (cell_flops + 2 * local_rows * (ghosts + capacity)) * ghosts,
@@ -444,13 +456,14 @@
             first_parcel = parcel if first else first_parcel
         history = () if first else (previous,)
         near_wanted = not far and not last
+        wanted = (terms,) if near_wanted else ()
         head, *near_head = call(
             functools.partial(cells_kernel, first, near_wanted),
-            (shape((width, capacity), F32),) + (shape((width, slots_pad), F32),) * near_wanted,
-            (weight, node_row, stiffness, scatter, spread, potential, current, ready, *history),
+            (shape((width, capacity), F32),) + (shape((width, 2 * slots_pad), F32),) * near_wanted,
+            (weight, node_row, stiffness, scatter, spread, potential, current, ready, *history, *wanted),
             (cell_flops + 4 * local_rows * capacity) * width,
             scratch=[pltpu.VMEM((width, local_rows), BF16)] + [pltpu.VMEM((width, nodes_pad), BF16)] * cells,
-            in_specs=[VMEM] * 7 + [ANY] + [VMEM] * len(history),
+            in_specs=[VMEM] * 7 + [ANY] + [VMEM] * len((*history, *wanted)),
         )
         own_flops = 2 * capacity * ghosts * width
         if far:
@@ -477,12 +490,16 @@
                     in_specs=[VMEM] * 4 + [ANY],
                 )
             else:
-                sent = call(
+                sent_shape = shape((width, 2 * slots_pad), BF16)
+                coupled_shape = shape((slots_pad, 2 * slots_pad), BF16)
+                sent, *coupled_out = call(
                     functools.partial(pair_kernel, first),
-                    shape((width, 2 * slots_pad), BF16),
-                    (terms, to_ghost, near, picked[0], parcel, first_parcel, *near_head, to_near, far_near),
-                    6 * ghosts * slots_pad * width,
+                    (sent_shape, coupled_shape) if first else (sent_shape,),
+                    (near, picked[0], parcel, *near_head, pairing)
+                    + ((first_parcel, far_near) if first else (coupled,)),
+                    8 * ghosts * slots_pad * width,
                 )
+                coupled = coupled_out[0] if first else coupled
             returned = [swap(sent, 0)]
             total = call(
                 functools.partial(paired_own_kernel, first),

time: 46.5 us -> 46.1 us (level)
  Pallas kernels: 25.4 us -> 24.8 us
    pallas_call x18, Pallas kernels: 25.4 us -> 24.8 us  [call(): pl.pallas_call(kernel, out_shape=out_shape, in_specs=in_specs or [VMEM] *...]
where the time goes in v6:
time: 46.1 us; the launch traced here: 45.7 us
  Pallas kernels  24.8 us (54%)
  starting transfers between devices  15.5 us (34%)
  waiting for transfers between devices  3.91 us (8%)
  between operations  1.18 us (3%)
    pallas_call x18, Pallas kernels, call(): pl.pallas_call(kernel, out_shape=out_shape, in_specs=in_specs or [VMEM] *...  24.8 us
    ppermute x7, starting transfers between devices, swap(): return lax.ppermute(value, 'dom', pairs)  12.1 us
    ppermute x3, starting transfers between devices, shards(): lax.ppermute(pieces[k], 'band', [(i, i ^ k) for i in range(bands)])  3.37 us
    ppermute x7, waiting for transfers between devices, swap(): return lax.ppermute(value, 'dom', pairs)  2.39 us
    ppermute x3, waiting for transfers between devices, shards(): lax.ppermute(pieces[k], 'band', [(i, i ^ k) for i in range(bands)])  1.53 us
  transfers between devices with their start and end apart: 10, of which 7 were waited for; matrix products, arithmetic and copies ran while one was open for 1% of the time, Pallas kernels for 37%

profile of v6, /device:TPU:1, one launch (start us, length us, event | category | flops | bytes accessed | tf_op | source)
XLA Modules:
  0.0 45.7 jit_solution(1674398380257608234)
XLA Ops:
  0.0 0.0 copy-start.3
  0.0 0.0 copy-start.4
  0.0 0.0 copy-start.1
  0.0 2.7 %shard_map.83 = (bf16[200,352]{1,0:T(8,128)(2,1)S(1)}, bf16[200,352]{1,0:T(8,128)(2,1)S(1)}, bf16[200,352]{1,0:T(8,128)(2,1)S(1)}, bf16[200,352]{1,0:T(8,128)(2,1)S(1)}) custom-call(bf16[800,352]{1,0:T(8,128)(2,1)} %bitcast.36, bf16[800,800]{1,0:T(8,128)(2,1)} %rotation.1), custom_call_target="tpu_custom_call" | custom-call | flops 450560000 | bytes 2406400 | tf_op jit(solution)/shard_map/pallas_call | solution.py:59
  2.7 2.1 %collective-permute-start = (bf16[200,352]{1,0:T(8,128)(2,1)S(1)}, bf16[200,352]{1,0:T(8,128)(2,1)S(1)}, u32[]{:S(2)}, u32[]{:S(2)}) collective-permute-start(bf16[200,352]{1,0:T(8,128)(2,1)S(1)} %get-tuple-element.40), channel_id=1, source_target_pairs={{0,8},{8,0},{16,24},{24,16},{1,9},{9,1},{17,25},{25,17},{2,10},{10... | collective-permute-start | bytes 422408 | tf_op jit(solution)/shard_map/ppermute | solution.py:358
  4.8 1.3 %collective-permute-start.1 = (bf16[200,352]{1,0:T(8,128)(2,1)S(1)}, bf16[200,352]{1,0:T(8,128)(2,1)S(1)}, u32[]{:S(2)}, u32[]{:S(2)}) collective-permute-start(bf16[200,352]{1,0:T(8,128)(2,1)S(1)} %get-tuple-element.41), channel_id=1, source_target_pairs={{0,16},{8,24},{16,0},{24,8},{1,17},{9,25},{17,1},{25,9},{2,18},{10... | collective-permute-start | bytes 422408 | tf_op jit(solution)/shard_map/ppermute | solution.py:358
  6.1 0.0 collective-permute-start.2
  6.8 0.0 copy-done.3
  6.8 0.0 copy-done.2
  6.9 0.0 copy-done.4
  7.0 0.1 broadcast_bitcast_fusion
  7.1 0.0 copy-done.1
  7.1 0.1 pad.19.stiffness
  7.2 4.3 %shard_map.82 = (bf16[2,352,176]{2,1,0:T(8,128)(2,1)S(1)}, bf16[352,1408]{1,0:T(8,128)(2,1)S(1)}, bf16[1536,1408]{1,0:T(8,128)(2,1)S(1)}, bf16[2,176,1408]{2,1,0...) custom-call(f32[1,1536]{1,0:T(1,128)S(1)} %bitcast.32, s32[1,1536]{1,0:T(1,128)S(1)} %bitcast.28, ...), custom_call_target="tpu_custom_call" | custom-call | flops 2733637632 | bytes 8182656 | tf_op jit(solution)/shard_map/pallas_call | solution.py:59
  11.5 0.0 collective-permute-done.refs_1_
  11.5 0.0 collective-permute-done.1.refs_2_
  11.5 1.5 %collective-permute-done.2.refs_3_ = bf16[200,352]{1,0:T(8,128)(2,1)S(1)} collective-permute-done((bf16[200,352]{1,0:T(8,128)(2,1)S(1)}, bf16[200,352]{1,0:T(8,128)(2,1)S(1)}, u32[]{:S(2)}, u32[]{:S(2)}) %collective-permute-start.2) | collective-permute-done | bytes 140832 | tf_op jit(solution)/shard_map/ppermute | solution.py:358
  13.1 0.5 %shard_map.84 = (bf16[200,1408]{1,0:T(8,128)(2,1)S(1)}, bf16[224,176]{1,0:T(8,128)(2,1)S(1)}) custom-call(s32[2,176]{1,0:T(2,128)S(1)} %pad.18.send_row, s32[1,1408]{1,0:T(1,128)S(1)} %compare_convert_fusion.keep, bf16[16,176]{1,0:T(8,128)(2,1)S(1)} %fusion.2.digits, bf16[2,352,176]{2,1,0:T(8,128)(2,1)S(1)} %get-tuple-element.38.after.to_ghost, ...), custom_call_target="tpu_custom_call" | custom-call | flops 99123200 | bytes 1465728 | tf_op jit(solution)/shard_map/pallas_call | solution.py:59
  13.6 1.5 %collective-permute-start.3 = (bf16[224,176]{1,0:T(8,128)(2,1)S(1)}, bf16[224,176]{1,0:T(8,128)(2,1)S(1)}, u32[]{:S(2)}, u32[]{:S(2)}) collective-permute-start(bf16[224,176]{1,0:T(8,128)(2,1)S(1)} %get-tuple-element.43), channel_id=1, source_target_pairs={{0,1},{1,0},{2,3},{3,2},{4,5},{5,4},{6,7},{7,6},{8,9},{9,8},{10,11... | collective-permute-start | bytes 236552 | tf_op jit(solution)/shard_map/ppermute | solution.py:36
  15.1 0.7 %shard_map.86 = (f32[2,200,176]{2,1,0:T(8,128)S(1)}, bf16[200,176]{1,0:T(8,128)(2,1)S(1)}) custom-call(s32[2,176]{1,0:T(2,128)S(1)} %pad.18.send_row, bf16[352,1408]{1,0:T(8,128)(2,1)S(1)} %get-tuple-element.36.to_own, bf16[200,1408]{1,0:T(8,128)(2,1)S(1)} %get-tuple-element.44.values.refs_0_), custom_call_target="tpu_custom_call" | custom-call | flops 396492800 | bytes 1907840 | tf_op jit(solution)/shard_map/pallas_call | solution.py:59
  15.8 0.3 collective-permute-done.3.first_near.near_ghosts
  16.1 0.2 shard_map.87.after
  16.3 3.5 %collective-permute-start.4 = (bf16[304,352]{1,0:T(8,128)(2,1)S(1)}, bf16[304,352]{1,0:T(8,128)(2,1)S(1)}, u32[]{:S(2)}, u32[]{:S(2)}) collective-permute-start(bf16[304,352]{1,0:T(8,128)(2,1)S(1)} %shard_map.87.after), channel_id=1, source_target_pairs={{1,2},{2,1},{3,4},{4,3},{5,6},{6,5},{9,10},{10,9},{11,12},{12,11},... | collective-permute-start | bytes 642056 | tf_op jit(solution)/shard_map/ppermute | solution.py:36
  19.8 0.0 copy-done
  19.8 3.1 %shard_map.88 = (f32[200,1408]{1,0:T(8,128)S(1)}, f32[200,352]{1,0:T(8,128)S(1)}) custom-call(f32[1,1536]{1,0:T(1,128)S(1)} %bitcast.33, s32[1,1536]{1,0:T(1,128)S(1)} %bitcast.29, bf16[768,768]{1,0:T(8,128)(2,1)S(1)} %pad.19.stiffness, bf16[1536,1408]{1,0:T(8,128)(2,1)S(1)} %get-tuple-element.37.scatter, ...), custom_call_target="tpu_custom_call" | custom-call | flops 2202009600 | bytes 8980992 | tf_op jit(solution)/shard_map/pallas_call | solution.py:59
  22.9 0.8 %collective-permute-done.4.parcel.first_parcel.coupling = bf16[304,352]{1,0:T(8,128)(2,1)S(1)} collective-permute-done((bf16[304,352]{1,0:T(8,128)(2,1)S(1)}, bf16[304,352]{1,0:T(8,128)(2,1)S(1)}, u32[]{:S(2)}, u32[]{:S(2)}) %collective-permute-start.4) | collective-permute-done | bytes 214048 | tf_op jit(solution)/shard_map/ppermute | solution.py:36
  23.7 0.5 %shard_map.90 = (bf16[200,352]{1,0:T(8,128)(2,1)S(1)}, bf16[176,352]{1,0:T(8,128)(2,1)S(1)}) custom-call(bf16[224,176]{1,0:T(8,128)(2,1)S(1)} %collective-permute-done.3.first_near.near_ghosts, bf16[200,176]{1,0:T(8,128)(2,1)S(1)} %get-tuple-element.46.far_picked, bf16[304,352]{1,0:T(8,128)(2,1)S(1)} %collective-permute-done.4.parcel.first_parcel.coupling, ...), custom_call_target="tpu_custom_call" | custom-call | flops 99123200 | bytes 1557248 | tf_op jit(solution)/shard_map/pallas_call | solution.py:59
  24.2 0.1 collective-permute-start.5
  24.3 0.1 shard_map.85.same
  24.4 1.0 %shard_map.89.total = f32[200,1408]{1,0:T(8,128)S(1)} custom-call(bf16[352,1408]{1,0:T(8,128)(2,1)S(1)} %get-tuple-element.36.to_own, f32[200,1408]{1,0:T(8,128)S(1)} %get-tuple-element.47.head, bf16[2,176,1408]{2,1,0:T(8,128)(2,1)S(1)} %get-tuple-element.35.spread, bf16[224,176]{1,0:T(8,128)(2,1)S(1)} %collective-permute-done.3.first_near.near_ghosts, ...), custom_call_target="tpu_custom_call" | custom-call | flops 198246400 | bytes 4812544 | tf_op jit(solution)/shard_map/pallas_call | solution.py:59
  25.5 0.2 collective-permute-done.5.arrived
  25.7 1.1 %shard_map.91 = (bf16[200,1408]{1,0:T(8,128)(2,1)S(1)}, bf16[200,176]{1,0:T(8,128)(2,1)S(1)}, bf16[200,176]{1,0:T(8,128)(2,1)S(1)}, f32[2,200,176]{2,1,0:T(8,128)S(1)}, bf16[200,352]{1,0:T(8,128)(2,1)S(1)}) custom-call(bf16[2,176,1408]{2,1,0:T(8,128)(2,1)S(1)} %get-tuple-element.35.spread, bf16[176,176]{1,0:T(8,128)(2,1)S(1)} %shard_map.85.same, ...), custom_call_target="tpu_custom_call" | custom-call | flops 693862400 | bytes 4828032 | tf_op jit(solution)/shard_map/pallas_call | solution.py:59
  26.7 3.6 %collective-permute-start.6 = (bf16[200,352]{1,0:T(8,128)(2,1)S(1)}, bf16[200,352]{1,0:T(8,128)(2,1)S(1)}, u32[]{:S(2)}, u32[]{:S(2)}) collective-permute-start(bf16[200,352]{1,0:T(8,128)(2,1)S(1)} %get-tuple-element.53.after), channel_id=1, source_target_pairs={{1,2},{2,1},{3,4},{4,3},{5,6},{6,5},{9,10},{10,9},{11,12},{12,11},... | collective-permute-start | bytes 422408 | tf_op jit(solution)/shard_map/ppermute | solution.py:36
  30.4 3.1 %shard_map.92 = (f32[200,1408]{1,0:T(8,128)S(1)}, f32[200,352]{1,0:T(8,128)S(1)}) custom-call(f32[1,1536]{1,0:T(1,128)S(1)} %bitcast.34, s32[1,1536]{1,0:T(1,128)S(1)} %bitcast.30, bf16[768,768]{1,0:T(8,128)(2,1)S(1)} %pad.19.stiffness, bf16[1536,1408]{1,0:T(8,128)(2,1)S(1)} %get-tuple-element.37.scatter, ...), custom_call_target="tpu_custom_call" | custom-call | flops 2202009600 | bytes 9470976 | tf_op jit(solution)/shard_map/pallas_call | solution.py:59
  33.5 0.0 collective-permute-done.6.parcel
  33.5 0.4 shard_map.94.sent
  33.9 0.1 collective-permute-start.7
  33.9 1.0 %shard_map.93.total = f32[200,1408]{1,0:T(8,128)S(1)} custom-call(bf16[352,1408]{1,0:T(8,128)(2,1)S(1)} %get-tuple-element.36.to_own, f32[200,1408]{1,0:T(8,128)S(1)} %get-tuple-element.55.head, bf16[2,176,1408]{2,1,0:T(8,128)(2,1)S(1)} %get-tuple-element.35.spread, bf16[200,176]{1,0:T(8,128)(2,1)S(1)} %get-tuple-element.56.near_ghosts, ...), custom_call_target="tpu_custom_call" | custom-call | flops 198246400 | bytes 4730880 | tf_op jit(solution)/shard_map/pallas_call | solution.py:59
  35.0 0.3 collective-permute-done.7.arrived
  35.3 1.1 %shard_map.95 = (bf16[200,1408]{1,0:T(8,128)(2,1)S(1)}, bf16[200,176]{1,0:T(8,128)(2,1)S(1)}, bf16[200,176]{1,0:T(8,128)(2,1)S(1)}, f32[2,200,176]{2,1,0:T(8,128)S(1)}, bf16[200,352]{1,0:T(8,128)(2,1)S(1)}) custom-call(bf16[2,176,1408]{2,1,0:T(8,128)(2,1)S(1)} %get-tuple-element.35.spread, bf16[176,176]{1,0:T(8,128)(2,1)S(1)} %shard_map.85.same, ...), custom_call_target="tpu_custom_call" | custom-call | flops 693862400 | bytes 4828032 | tf_op jit(solution)/shard_map/pallas_call | solution.py:59
  36.4 3.3 %collective-permute-start.8 = (bf16[200,352]{1,0:T(8,128)(2,1)S(1)}, bf16[200,352]{1,0:T(8,128)(2,1)S(1)}, u32[]{:S(2)}, u32[]{:S(2)}) collective-permute-start(bf16[200,352]{1,0:T(8,128)(2,1)S(1)} %get-tuple-element.61.after), channel_id=1, source_target_pairs={{1,2},{2,1},{3,4},{4,3},{5,6},{6,5},{9,10},{10,9},{11,12},{12,11},... | collective-permute-start | bytes 422408 | tf_op jit(solution)/shard_map/ppermute | solution.py:36
  39.6 2.8 %shard_map.96.head.after = f32[200,1408]{1,0:T(8,128)S(1)} custom-call(f32[1,1536]{1,0:T(1,128)S(1)} %bitcast.35, s32[1,1536]{1,0:T(1,128)S(1)} %bitcast.31, bf16[768,768]{1,0:T(8,128)(2,1)S(1)} %pad.19.stiffness, bf16[1536,1408]{1,0:T(8,128)(2,1)S(1)} %get-tuple-element.37.scatter, bf16[2,176,1408]{2,1,0:T(8,128)(2,1)S(1)} %get-tuple-element.35.spread, ...), custom_call_target="tpu_custom_call" | custom-call | flops 2202009600 | bytes 8907776 | tf_op jit(solution)/shard_map/pallas_call | solution.py:59
  42.4 0.5 %collective-permute-done.8.parcel = bf16[200,352]{1,0:T(8,128)(2,1)S(1)} collective-permute-done((bf16[200,352]{1,0:T(8,128)(2,1)S(1)}, bf16[200,352]{1,0:T(8,128)(2,1)S(1)}, u32[]{:S(2)}, u32[]{:S(2)}) %collective-permute-start.8) | collective-permute-done | bytes 140832 | tf_op jit(solution)/shard_map/ppermute | solution.py:36
  42.9 0.2 shard_map.98
  43.1 0.1 collective-permute-start.9
  43.2 1.0 %shard_map.97.total = f32[200,1408]{1,0:T(8,128)S(1)} custom-call(bf16[352,1408]{1,0:T(8,128)(2,1)S(1)} %get-tuple-element.36.to_own, f32[200,1408]{1,0:T(8,128)S(1)} %shard_map.96.head.after, bf16[2,176,1408]{2,1,0:T(8,128)(2,1)S(1)} %get-tuple-element.35.spread, bf16[200,176]{1,0:T(8,128)(2,1)S(1)} %get-tuple-element.62.near_ghosts, ...), custom_call_target="tpu_custom_call" | custom-call | flops 198246400 | bytes 4730880 | tf_op jit(solution)/shard_map/pallas_call | solution.py:59
  44.2 0.3 collective-permute-done.9.refs_0_
  44.5 1.1 %shard_map.99 = bf16[200,1408]{1,0:T(8,128)(2,1)} custom-call(bf16[2,176,1408]{2,1,0:T(8,128)(2,1)S(1)} %get-tuple-element.35.spread, f32[200,1408]{1,0:T(8,128)S(1)} %shard_map.97.total, bf16[200,176]{1,0:T(8,128)(2,1)S(1)} %collective-permute-done.9.refs_0_), custom_call_target="tpu_custom_call" | custom-call | flops 297369600 | bytes 2751232 | tf_op jit(solution)/shard_map/pallas_call | solution.py:59
  (14 shorter events, 0.1 us)
Async XLA Ops:
  0.0 6.8 %copy-start.3 = (s32[1,4,162]{2,1,0:T(4,128)S(1)}, s32[1,4,162]{2,1,0:T(4,128)}, u32[]{:S(2)}) copy-start(s32[1,4,162]{2,1,0:T(4,128)} %param.14) | copy-start | bytes 7780
  0.0 6.8 %copy-start.2 = (s32[1,2,729]{2,1,0:T(2,128)S(1)}, s32[1,2,729]{2,1,0:T(2,128)}, u32[]{:S(2)}) copy-start(s32[1,2,729]{2,1,0:T(2,128)} %param.13) | copy-start | bytes 17500
  0.0 6.9 %copy-start.4 = (f32[1,2]{1,0:T(1,128)S(1)}, f32[1,2]{1,0:T(1,128)}, u32[]{:S(2)}) copy-start(f32[1,2]{1,0:T(1,128)} %param.11) | copy-start | bytes 28
  0.0 7.0 %copy-start.1 = (bf16[729,729]{1,0:T(8,128)(2,1)S(1)}, bf16[729,729]{1,0:T(8,128)(2,1)}, u32[]{:S(2)}) copy-start(bf16[729,729]{1,0:T(8,128)(2,1)} %param.10) | copy-start | bytes 3188650
  2.7 8.8 %collective-permute-start = (bf16[200,352]{1,0:T(8,128)(2,1)S(1)}, bf16[200,352]{1,0:T(8,128)(2,1)S(1)}, u32[]{:S(2)}, u32[]{:S(2)}) collective-permute-start(bf16[200,352]{1,0:T(8,128)(2,1)S(1)} %get-tuple-element.40), channel_id=1, source_target_pairs={{0,8},{8,0},{16,24},{24,16},{1,9},{9,1},{17,25},{25,17},{2,10},{10... | collective-permute-start | bytes 422408 | tf_op jit(solution)/shard_map/ppermute | solution.py:358
  4.8 6.7 %collective-permute-start.1 = (bf16[200,352]{1,0:T(8,128)(2,1)S(1)}, bf16[200,352]{1,0:T(8,128)(2,1)S(1)}, u32[]{:S(2)}, u32[]{:S(2)}) collective-permute-start(bf16[200,352]{1,0:T(8,128)(2,1)S(1)} %get-tuple-element.41), channel_id=1, source_target_pairs={{0,16},{8,24},{16,0},{24,8},{1,17},{9,25},{17,1},{25,9},{2,18},{10... | collective-permute-start | bytes 422408 | tf_op jit(solution)/shard_map/ppermute | solution.py:358
  6.1 7.0 %collective-permute-start.2 = (bf16[200,352]{1,0:T(8,128)(2,1)S(1)}, bf16[200,352]{1,0:T(8,128)(2,1)S(1)}, u32[]{:S(2)}, u32[]{:S(2)}) collective-permute-start(bf16[200,352]{1,0:T(8,128)(2,1)S(1)} %get-tuple-element.42), channel_id=1, source_target_pairs={{0,24},{8,16},{16,8},{24,0},{1,25},{9,17},{17,9},{25,1},{2,26},{10... | collective-permute-start | bytes 422408 | tf_op jit(solution)/shard_map/ppermute | solution.py:358
  13.6 2.5 %collective-permute-start.3 = (bf16[224,176]{1,0:T(8,128)(2,1)S(1)}, bf16[224,176]{1,0:T(8,128)(2,1)S(1)}, u32[]{:S(2)}, u32[]{:S(2)}) collective-permute-start(bf16[224,176]{1,0:T(8,128)(2,1)S(1)} %get-tuple-element.43), channel_id=1, source_target_pairs={{0,1},{1,0},{2,3},{3,2},{4,5},{5,4},{6,7},{7,6},{8,9},{9,8},{10,11... | collective-permute-start | bytes 236552 | tf_op jit(solution)/shard_map/ppermute | solution.py:36
  15.1 4.7 %copy-start = (f32[1,1408]{1,0:T(1,128)S(1)}, f32[1,1408]{1,0:T(1,128)}, u32[]{:S(2)}) copy-start(f32[1,1408]{1,0:T(1,128)} %potential.5) | copy-start | bytes 16900
  16.3 7.4 %collective-permute-start.4 = (bf16[304,352]{1,0:T(8,128)(2,1)S(1)}, bf16[304,352]{1,0:T(8,128)(2,1)S(1)}, u32[]{:S(2)}, u32[]{:S(2)}) collective-permute-start(bf16[304,352]{1,0:T(8,128)(2,1)S(1)} %shard_map.87.after), channel_id=1, source_target_pairs={{1,2},{2,1},{3,4},{4,3},{5,6},{6,5},{9,10},{10,9},{11,12},{12,11},... | collective-permute-start | bytes 642056 | tf_op jit(solution)/shard_map/ppermute | solution.py:36
  24.2 1.4 %collective-permute-start.5 = (bf16[200,352]{1,0:T(8,128)(2,1)S(1)}, bf16[200,352]{1,0:T(8,128)(2,1)S(1)}, u32[]{:S(2)}, u32[]{:S(2)}) collective-permute-start(bf16[200,352]{1,0:T(8,128)(2,1)S(1)} %get-tuple-element.51.sent), channel_id=1, source_target_pairs={{0,1},{1,0},{2,3},{3,2},{4,5},{5,4},{6,7},{7,6},{8,9},{9,8},{10,11... | collective-permute-start | bytes 422408 | tf_op jit(solution)/shard_map/ppermute | solution.py:36
  26.7 6.7 %collective-permute-start.6 = (bf16[200,352]{1,0:T(8,128)(2,1)S(1)}, bf16[200,352]{1,0:T(8,128)(2,1)S(1)}, u32[]{:S(2)}, u32[]{:S(2)}) collective-permute-start(bf16[200,352]{1,0:T(8,128)(2,1)S(1)} %get-tuple-element.53.after), channel_id=1, source_target_pairs={{1,2},{2,1},{3,4},{4,3},{5,6},{6,5},{9,10},{10,9},{11,12},{12,11},... | collective-permute-start | bytes 422408 | tf_op jit(solution)/shard_map/ppermute | solution.py:36
  33.9 1.4 %collective-permute-start.7 = (bf16[200,352]{1,0:T(8,128)(2,1)S(1)}, bf16[200,352]{1,0:T(8,128)(2,1)S(1)}, u32[]{:S(2)}, u32[]{:S(2)}) collective-permute-start(bf16[200,352]{1,0:T(8,128)(2,1)S(1)} %shard_map.94.sent), channel_id=1, source_target_pairs={{0,1},{1,0},{2,3},{3,2},{4,5},{5,4},{6,7},{7,6},{8,9},{9,8},{10,11... | collective-permute-start | bytes 422408 | tf_op jit(solution)/shard_map/ppermute | solution.py:36
  36.4 6.5 %collective-permute-start.8 = (bf16[200,352]{1,0:T(8,128)(2,1)S(1)}, bf16[200,352]{1,0:T(8,128)(2,1)S(1)}, u32[]{:S(2)}, u32[]{:S(2)}) collective-permute-start(bf16[200,352]{1,0:T(8,128)(2,1)S(1)} %get-tuple-element.61.after), channel_id=1, source_target_pairs={{1,2},{2,1},{3,4},{4,3},{5,6},{6,5},{9,10},{10,9},{11,12},{12,11},... | collective-permute-start | bytes 422408 | tf_op jit(solution)/shard_map/ppermute | solution.py:36
  43.1 1.4 %collective-permute-start.9 = (bf16[200,176]{1,0:T(8,128)(2,1)S(1)}, bf16[200,176]{1,0:T(8,128)(2,1)S(1)}, u32[]{:S(2)}, u32[]{:S(2)}) collective-permute-start(bf16[200,176]{1,0:T(8,128)(2,1)S(1)} %shard_map.98), channel_id=1, source_target_pairs={{0,1},{1,0},{2,3},{3,2},{4,5},{5,4},{6,7},{7,6},{8,9},{9,8},{10,11... | collective-permute-start | bytes 211208 | tf_op jit(solution)/shard_map/ppermute | solution.py:36

commit v7 on v6

--- a/solution.py
+++ b/solution.py
@@ -20,6 +20,7 @@
 ANY = pl.BlockSpec(memory_space=pl.ANY)
 LANES = 128
 DIGIT = 64
+LAST_COLUMNS = 512
 DIGIT_ROWS = 16
 ROTATE_VMEM = 53 << 20
 
@@ -165,10 +166,10 @@
     pick_rows(send_row, 0, values, near_picked)
 
 
-def terms_kernel(send_row, to_own, values, terms, *picked):
+def terms_kernel(spread, to_own, values, terms, *picked):
     slots = terms.shape[2]
     for block, out in enumerate(picked):
-        pick_rows(send_row, block + 1, values, out)
+        out[...] = mm_nt(values[...], spread[block + 1]).astype(BF16)
     for block in range(terms.shape[0]):
         terms[block] = mm_nt(values[...], to_own[block * slots : (block + 1) * slots, :])
 
@@ -260,7 +261,7 @@
 
 
 def advance_kernel(
-    first_step, spread, same, send_row, to_own, to_ghost, total, sent, arrived, values, near_ghosts, far_picked, terms, parcel
+    first_step, spread, same, to_own, to_ghost, total, sent, arrived, values, near_ghosts, far_picked, terms, parcel
 ):
     slots = far_picked.shape[1]
     sums = arrived[:, :slots]
@@ -269,7 +270,7 @@
         values[:, i : i + n] = (total[:, i : i + n] + added).astype(BF16)
     near = mm(sent[:, :slots], same[...]) * scale_of(first_step) + arrived[:, slots:].astype(F32)
     near_ghosts[...] = near.astype(BF16)
-    terms_kernel(send_row, to_own, values, terms, far_picked)
+    terms_kernel(spread, to_own, values, terms, far_picked)
     parcel_kernel(terms, to_ghost, near_ghosts, far_picked, parcel)
 
 
@@ -320,7 +321,7 @@
 def last_kernel(blocks, first_step, spread, total, *refs):
     arrived, (out, held, sems) = refs[:blocks], refs[blocks:]
     copies = []
-    for part, (i, n) in enumerate(steps(out.shape[1], 256)):
+    for part, (i, n) in enumerate(steps(out.shape[1], LAST_COLUMNS)):
         held[:, i : i + n] = updated_columns(first_step, spread, i, n, total, arrived)
         at = pl.ds(i, n)
         copies.append(pltpu.make_async_copy(held.at[:, at], out.at[:, at], sems.at[part]))
@@ -432,7 +433,7 @@
             terms, *picked = call(
                 terms_kernel,
                 (terms_shape,) + (block_shape,) * (blocks - 1),
-                (send_row, to_own, current),
+                (spread, to_own, current),
                 terms_flops,
             )
         if far:
@@ -516,7 +517,7 @@
                 update_flops,
                 scratch=[
                     pltpu.VMEM((width, capacity), BF16),
-                    pltpu.SemaphoreType.DMA((len(steps(capacity, 256)),)),
+                    pltpu.SemaphoreType.DMA((len(steps(capacity, LAST_COLUMNS)),)),
                 ],
                 out_specs=ANY,
             )
@@ -530,7 +531,7 @@
                     terms_shape,
                     shape((width, 2 * slots_pad), BF16),
                 ),
-                (spread, same, send_row, to_own, to_ghost, total, sent, *returned),
+                (spread, same, to_own, to_ghost, total, sent, *returned),
                 update_flops + terms_flops,
             )
             picked = [far_picked]

time: 46.1 us -> 46.1 us (level)
  transfers between devices with their start and end apart: 10 -> 10, of which waited for: 7 -> 7; matrix products, arithmetic and copies ran while one was open for 1% -> 1% of each run, Pallas kernels for 37% -> 38%
where the time goes in v7:
time: 46.1 us; the launch traced here: 45.7 us
  Pallas kernels  24.9 us (54%)
  starting transfers between devices  15.4 us (33%)
  waiting for transfers between devices  3.89 us (8%)
  between operations  1.19 us (3%)
    pallas_call x18, Pallas kernels, call(): pl.pallas_call(kernel, out_shape=out_shape, in_specs=in_specs or [VMEM] *...  24.9 us
    ppermute x7, starting transfers between devices, swap(): return lax.ppermute(value, 'dom', pairs)  12.1 us
    ppermute x3, starting transfers between devices, shards(): lax.ppermute(pieces[k], 'band', [(i, i ^ k) for i in range(bands)])  3.37 us
    ppermute x7, waiting for transfers between devices, swap(): return lax.ppermute(value, 'dom', pairs)  2.37 us
    ppermute x3, waiting for transfers between devices, shards(): lax.ppermute(pieces[k], 'band', [(i, i ^ k) for i in range(bands)])  1.52 us
  transfers between devices with their start and end apart: 10, of which 7 were waited for; matrix products, arithmetic and copies ran while one was open for 1% of the time, Pallas kernels for 38%

profile of v7, /device:TPU:1, one launch (start us, length us, event | category | flops | bytes accessed | tf_op | source)
XLA Modules:
  0.0 45.7 jit_solution(12251174333036716687)
XLA Ops:
  0.0 0.0 copy-start.3
  0.0 0.0 copy-start.1
  0.0 2.7 %shard_map.83 = (bf16[200,352]{1,0:T(8,128)(2,1)S(1)}, bf16[200,352]{1,0:T(8,128)(2,1)S(1)}, bf16[200,352]{1,0:T(8,128)(2,1)S(1)}, bf16[200,352]{1,0:T(8,128)(2,1)S(1)}) custom-call(bf16[800,352]{1,0:T(8,128)(2,1)} %bitcast.36, bf16[800,800]{1,0:T(8,128)(2,1)} %rotation.1), custom_call_target="tpu_custom_call" | custom-call | flops 450560000 | bytes 2406400 | tf_op jit(solution)/shard_map/pallas_call | solution.py:60
  2.7 2.1 %collective-permute-start = (bf16[200,352]{1,0:T(8,128)(2,1)S(1)}, bf16[200,352]{1,0:T(8,128)(2,1)S(1)}, u32[]{:S(2)}, u32[]{:S(2)}) collective-permute-start(bf16[200,352]{1,0:T(8,128)(2,1)S(1)} %get-tuple-element.40), channel_id=1, source_target_pairs={{0,8},{8,0},{16,24},{24,16},{1,9},{9,1},{17,25},{25,17},{2,10},{10... | collective-permute-start | bytes 422408 | tf_op jit(solution)/shard_map/ppermute | solution.py:359
  4.8 1.3 %collective-permute-start.1 = (bf16[200,352]{1,0:T(8,128)(2,1)S(1)}, bf16[200,352]{1,0:T(8,128)(2,1)S(1)}, u32[]{:S(2)}, u32[]{:S(2)}) collective-permute-start(bf16[200,352]{1,0:T(8,128)(2,1)S(1)} %get-tuple-element.41), channel_id=1, source_target_pairs={{0,16},{8,24},{16,0},{24,8},{1,17},{9,25},{17,1},{25,9},{2,18},{10... | collective-permute-start | bytes 422408 | tf_op jit(solution)/shard_map/ppermute | solution.py:359
  6.1 0.0 collective-permute-start.2
  6.8 0.0 copy-done.3
  6.8 0.0 copy-done.2
  6.9 0.0 copy-done.4
  7.0 0.1 broadcast_bitcast_fusion
  7.1 0.0 copy-done.1
  7.1 0.1 pad.19.stiffness
  7.2 4.3 %shard_map.82 = (bf16[2,352,176]{2,1,0:T(8,128)(2,1)S(1)}, bf16[352,1408]{1,0:T(8,128)(2,1)S(1)}, bf16[1536,1408]{1,0:T(8,128)(2,1)S(1)}, bf16[2,176,1408]{2,1,0...) custom-call(f32[1,1536]{1,0:T(1,128)S(1)} %bitcast.32, s32[1,1536]{1,0:T(1,128)S(1)} %bitcast.28, ...), custom_call_target="tpu_custom_call" | custom-call | flops 2733637632 | bytes 8182656 | tf_op jit(solution)/shard_map/pallas_call | solution.py:60
  11.5 0.0 collective-permute-done.refs_1_
  11.5 0.0 collective-permute-done.1.refs_2_
  11.6 1.5 %collective-permute-done.2.refs_3_ = bf16[200,352]{1,0:T(8,128)(2,1)S(1)} collective-permute-done((bf16[200,352]{1,0:T(8,128)(2,1)S(1)}, bf16[200,352]{1,0:T(8,128)(2,1)S(1)}, u32[]{:S(2)}, u32[]{:S(2)}) %collective-permute-start.2) | collective-permute-done | bytes 140832 | tf_op jit(solution)/shard_map/ppermute | solution.py:359
  13.1 0.5 %shard_map.84 = (bf16[200,1408]{1,0:T(8,128)(2,1)S(1)}, bf16[224,176]{1,0:T(8,128)(2,1)S(1)}) custom-call(s32[2,176]{1,0:T(2,128)S(1)} %pad.18.send_row, s32[1,1408]{1,0:T(1,128)S(1)} %compare_convert_fusion.keep, bf16[16,176]{1,0:T(8,128)(2,1)S(1)} %fusion.2.digits, bf16[2,352,176]{2,1,0:T(8,128)(2,1)S(1)} %get-tuple-element.38.after.to_ghost, ...), custom_call_target="tpu_custom_call" | custom-call | flops 99123200 | bytes 1465728 | tf_op jit(solution)/shard_map/pallas_call | solution.py:60
  13.6 1.5 %collective-permute-start.3 = (bf16[224,176]{1,0:T(8,128)(2,1)S(1)}, bf16[224,176]{1,0:T(8,128)(2,1)S(1)}, u32[]{:S(2)}, u32[]{:S(2)}) collective-permute-start(bf16[224,176]{1,0:T(8,128)(2,1)S(1)} %get-tuple-element.43), channel_id=1, source_target_pairs={{0,1},{1,0},{2,3},{3,2},{4,5},{5,4},{6,7},{7,6},{8,9},{9,8},{10,11... | collective-permute-start | bytes 236552 | tf_op jit(solution)/shard_map/ppermute | solution.py:37
  15.1 0.7 %shard_map.86 = (f32[2,200,176]{2,1,0:T(8,128)S(1)}, bf16[200,176]{1,0:T(8,128)(2,1)S(1)}) custom-call(bf16[2,176,1408]{2,1,0:T(8,128)(2,1)S(1)} %get-tuple-element.35.spread, bf16[352,1408]{1,0:T(8,128)(2,1)S(1)} %get-tuple-element.36.to_own, bf16[200,1408]{1,0:T(8,128)(2,1)S(1)} %get-tuple-element.44.values.refs_0_), custom_call_target="tpu_custom_call" | custom-call | flops 396492800 | bytes 2897664 | tf_op jit(solution)/shard_map/pallas_call | solution.py:60
  15.8 0.0 copy-start
  15.8 0.3 collective-permute-done.3.first_near.near_ghosts
  16.1 0.2 shard_map.87.after
  16.3 3.5 %collective-permute-start.4 = (bf16[304,352]{1,0:T(8,128)(2,1)S(1)}, bf16[304,352]{1,0:T(8,128)(2,1)S(1)}, u32[]{:S(2)}, u32[]{:S(2)}) collective-permute-start(bf16[304,352]{1,0:T(8,128)(2,1)S(1)} %shard_map.87.after), channel_id=1, source_target_pairs={{1,2},{2,1},{3,4},{4,3},{5,6},{6,5},{9,10},{10,9},{11,12},{12,11},... | collective-permute-start | bytes 642056 | tf_op jit(solution)/shard_map/ppermute | solution.py:37
  19.8 0.0 copy-done
  19.8 3.1 %shard_map.88 = (f32[200,1408]{1,0:T(8,128)S(1)}, f32[200,352]{1,0:T(8,128)S(1)}) custom-call(f32[1,1536]{1,0:T(1,128)S(1)} %bitcast.33, s32[1,1536]{1,0:T(1,128)S(1)} %bitcast.29, bf16[768,768]{1,0:T(8,128)(2,1)S(1)} %pad.19.stiffness, bf16[1536,1408]{1,0:T(8,128)(2,1)S(1)} %get-tuple-element.37.scatter, ...), custom_call_target="tpu_custom_call" | custom-call | flops 2202009600 | bytes 8980992 | tf_op jit(solution)/shard_map/pallas_call | solution.py:60
  22.9 0.8 %collective-permute-done.4.parcel.first_parcel.coupling = bf16[304,352]{1,0:T(8,128)(2,1)S(1)} collective-permute-done((bf16[304,352]{1,0:T(8,128)(2,1)S(1)}, bf16[304,352]{1,0:T(8,128)(2,1)S(1)}, u32[]{:S(2)}, u32[]{:S(2)}) %collective-permute-start.4) | collective-permute-done | bytes 214048 | tf_op jit(solution)/shard_map/ppermute | solution.py:37
  23.7 0.5 %shard_map.90 = (bf16[200,352]{1,0:T(8,128)(2,1)S(1)}, bf16[176,352]{1,0:T(8,128)(2,1)S(1)}) custom-call(bf16[224,176]{1,0:T(8,128)(2,1)S(1)} %collective-permute-done.3.first_near.near_ghosts, bf16[200,176]{1,0:T(8,128)(2,1)S(1)} %get-tuple-element.46.far_picked, bf16[304,352]{1,0:T(8,128)(2,1)S(1)} %collective-permute-done.4.parcel.first_parcel.coupling, ...), custom_call_target="tpu_custom_call" | custom-call | flops 99123200 | bytes 1557248 | tf_op jit(solution)/shard_map/pallas_call | solution.py:60
  24.2 0.1 collective-permute-start.5
  24.3 0.1 shard_map.85.same
  24.4 1.0 %shard_map.89.total = f32[200,1408]{1,0:T(8,128)S(1)} custom-call(bf16[352,1408]{1,0:T(8,128)(2,1)S(1)} %get-tuple-element.36.to_own, f32[200,1408]{1,0:T(8,128)S(1)} %get-tuple-element.47.head, bf16[2,176,1408]{2,1,0:T(8,128)(2,1)S(1)} %get-tuple-element.35.spread, bf16[224,176]{1,0:T(8,128)(2,1)S(1)} %collective-permute-done.3.first_near.near_ghosts, ...), custom_call_target="tpu_custom_call" | custom-call | flops 198246400 | bytes 4812544 | tf_op jit(solution)/shard_map/pallas_call | solution.py:60
  25.5 0.2 collective-permute-done.5.arrived
  25.7 1.1 %shard_map.91 = (bf16[200,1408]{1,0:T(8,128)(2,1)S(1)}, bf16[200,176]{1,0:T(8,128)(2,1)S(1)}, bf16[200,176]{1,0:T(8,128)(2,1)S(1)}, f32[2,200,176]{2,1,0:T(8,128)S(1)}, bf16[200,352]{1,0:T(8,128)(2,1)S(1)}) custom-call(bf16[2,176,1408]{2,1,0:T(8,128)(2,1)S(1)} %get-tuple-element.35.spread, bf16[176,176]{1,0:T(8,128)(2,1)S(1)} %shard_map.85.same, ...), custom_call_target="tpu_custom_call" | custom-call | flops 693862400 | bytes 4826624 | tf_op jit(solution)/shard_map/pallas_call | solution.py:60
  26.7 3.6 %collective-permute-start.6 = (bf16[200,352]{1,0:T(8,128)(2,1)S(1)}, bf16[200,352]{1,0:T(8,128)(2,1)S(1)}, u32[]{:S(2)}, u32[]{:S(2)}) collective-permute-start(bf16[200,352]{1,0:T(8,128)(2,1)S(1)} %get-tuple-element.53.after), channel_id=1, source_target_pairs={{1,2},{2,1},{3,4},{4,3},{5,6},{6,5},{9,10},{10,9},{11,12},{12,11},... | collective-permute-start | bytes 422408 | tf_op jit(solution)/shard_map/ppermute | solution.py:37
  30.4 3.1 %shard_map.92 = (f32[200,1408]{1,0:T(8,128)S(1)}, f32[200,352]{1,0:T(8,128)S(1)}) custom-call(f32[1,1536]{1,0:T(1,128)S(1)} %bitcast.34, s32[1,1536]{1,0:T(1,128)S(1)} %bitcast.30, bf16[768,768]{1,0:T(8,128)(2,1)S(1)} %pad.19.stiffness, bf16[1536,1408]{1,0:T(8,128)(2,1)S(1)} %get-tuple-element.37.scatter, ...), custom_call_target="tpu_custom_call" | custom-call | flops 2202009600 | bytes 9470976 | tf_op jit(solution)/shard_map/pallas_call | solution.py:60
  33.5 0.0 collective-permute-done.6.parcel
  33.5 0.4 shard_map.94.sent
  33.9 0.1 collective-permute-start.7
  34.0 1.0 %shard_map.93.total = f32[200,1408]{1,0:T(8,128)S(1)} custom-call(bf16[352,1408]{1,0:T(8,128)(2,1)S(1)} %get-tuple-element.36.to_own, f32[200,1408]{1,0:T(8,128)S(1)} %get-tuple-element.55.head, bf16[2,176,1408]{2,1,0:T(8,128)(2,1)S(1)} %get-tuple-element.35.spread, bf16[200,176]{1,0:T(8,128)(2,1)S(1)} %get-tuple-element.56.near_ghosts, ...), custom_call_target="tpu_custom_call" | custom-call | flops 198246400 | bytes 4730880 | tf_op jit(solution)/shard_map/pallas_call | solution.py:60
  35.0 0.3 collective-permute-done.7.arrived
  35.3 1.1 %shard_map.95 = (bf16[200,1408]{1,0:T(8,128)(2,1)S(1)}, bf16[200,176]{1,0:T(8,128)(2,1)S(1)}, bf16[200,176]{1,0:T(8,128)(2,1)S(1)}, f32[2,200,176]{2,1,0:T(8,128)S(1)}, bf16[200,352]{1,0:T(8,128)(2,1)S(1)}) custom-call(bf16[2,176,1408]{2,1,0:T(8,128)(2,1)S(1)} %get-tuple-element.35.spread, bf16[176,176]{1,0:T(8,128)(2,1)S(1)} %shard_map.85.same, ...), custom_call_target="tpu_custom_call" | custom-call | flops 693862400 | bytes 4826624 | tf_op jit(solution)/shard_map/pallas_call | solution.py:60
  36.4 3.3 %collective-permute-start.8 = (bf16[200,352]{1,0:T(8,128)(2,1)S(1)}, bf16[200,352]{1,0:T(8,128)(2,1)S(1)}, u32[]{:S(2)}, u32[]{:S(2)}) collective-permute-start(bf16[200,352]{1,0:T(8,128)(2,1)S(1)} %get-tuple-element.61.after), channel_id=1, source_target_pairs={{1,2},{2,1},{3,4},{4,3},{5,6},{6,5},{9,10},{10,9},{11,12},{12,11},... | collective-permute-start | bytes 422408 | tf_op jit(solution)/shard_map/ppermute | solution.py:37
  39.7 2.8 %shard_map.96.head.after = f32[200,1408]{1,0:T(8,128)S(1)} custom-call(f32[1,1536]{1,0:T(1,128)S(1)} %bitcast.35, s32[1,1536]{1,0:T(1,128)S(1)} %bitcast.31, bf16[768,768]{1,0:T(8,128)(2,1)S(1)} %pad.19.stiffness, bf16[1536,1408]{1,0:T(8,128)(2,1)S(1)} %get-tuple-element.37.scatter, bf16[2,176,1408]{2,1,0:T(8,128)(2,1)S(1)} %get-tuple-element.35.spread, ...), custom_call_target="tpu_custom_call" | custom-call | flops 2202009600 | bytes 8907776 | tf_op jit(solution)/shard_map/pallas_call | solution.py:60
  42.5 0.5 %collective-permute-done.8.parcel = bf16[200,352]{1,0:T(8,128)(2,1)S(1)} collective-permute-done((bf16[200,352]{1,0:T(8,128)(2,1)S(1)}, bf16[200,352]{1,0:T(8,128)(2,1)S(1)}, u32[]{:S(2)}, u32[]{:S(2)}) %collective-permute-start.8) | collective-permute-done | bytes 140832 | tf_op jit(solution)/shard_map/ppermute | solution.py:37
  43.0 0.2 shard_map.98
  43.2 0.1 collective-permute-start.9
  43.2 1.0 %shard_map.97.total = f32[200,1408]{1,0:T(8,128)S(1)} custom-call(bf16[352,1408]{1,0:T(8,128)(2,1)S(1)} %get-tuple-element.36.to_own, f32[200,1408]{1,0:T(8,128)S(1)} %shard_map.96.head.after, bf16[2,176,1408]{2,1,0:T(8,128)(2,1)S(1)} %get-tuple-element.35.spread, bf16[200,176]{1,0:T(8,128)(2,1)S(1)} %get-tuple-element.62.near_ghosts, ...), custom_call_target="tpu_custom_call" | custom-call | flops 198246400 | bytes 4730880 | tf_op jit(solution)/shard_map/pallas_call | solution.py:60
  44.3 0.3 collective-permute-done.9.refs_0_
  44.5 1.0 %shard_map.99 = bf16[200,1408]{1,0:T(8,128)(2,1)} custom-call(bf16[2,176,1408]{2,1,0:T(8,128)(2,1)S(1)} %get-tuple-element.35.spread, f32[200,1408]{1,0:T(8,128)S(1)} %shard_map.97.total, bf16[200,176]{1,0:T(8,128)(2,1)S(1)} %collective-permute-done.9.refs_0_), custom_call_target="tpu_custom_call" | custom-call | flops 297369600 | bytes 2751232 | tf_op jit(solution)/shard_map/pallas_call | solution.py:60
  (14 shorter events, 0.1 us)
Async XLA Ops:
  0.0 6.8 %copy-start.3 = (s32[1,4,162]{2,1,0:T(4,128)S(1)}, s32[1,4,162]{2,1,0:T(4,128)}, u32[]{:S(2)}) copy-start(s32[1,4,162]{2,1,0:T(4,128)} %param.14) | copy-start | bytes 7780
  0.0 6.8 %copy-start.2 = (s32[1,2,729]{2,1,0:T(2,128)S(1)}, s32[1,2,729]{2,1,0:T(2,128)}, u32[]{:S(2)}) copy-start(s32[1,2,729]{2,1,0:T(2,128)} %param.13) | copy-start | bytes 17500
  0.0 6.9 %copy-start.4 = (f32[1,2]{1,0:T(1,128)S(1)}, f32[1,2]{1,0:T(1,128)}, u32[]{:S(2)}) copy-start(f32[1,2]{1,0:T(1,128)} %param.11) | copy-start | bytes 28
  0.0 7.0 %copy-start.1 = (bf16[729,729]{1,0:T(8,128)(2,1)S(1)}, bf16[729,729]{1,0:T(8,128)(2,1)}, u32[]{:S(2)}) copy-start(bf16[729,729]{1,0:T(8,128)(2,1)} %param.10) | copy-start | bytes 3188650
  2.7 8.8 %collective-permute-start = (bf16[200,352]{1,0:T(8,128)(2,1)S(1)}, bf16[200,352]{1,0:T(8,128)(2,1)S(1)}, u32[]{:S(2)}, u32[]{:S(2)}) collective-permute-start(bf16[200,352]{1,0:T(8,128)(2,1)S(1)} %get-tuple-element.40), channel_id=1, source_target_pairs={{0,8},{8,0},{16,24},{24,16},{1,9},{9,1},{17,25},{25,17},{2,10},{10... | collective-permute-start | bytes 422408 | tf_op jit(solution)/shard_map/ppermute | solution.py:359
  4.8 6.7 %collective-permute-start.1 = (bf16[200,352]{1,0:T(8,128)(2,1)S(1)}, bf16[200,352]{1,0:T(8,128)(2,1)S(1)}, u32[]{:S(2)}, u32[]{:S(2)}) collective-permute-start(bf16[200,352]{1,0:T(8,128)(2,1)S(1)} %get-tuple-element.41), channel_id=1, source_target_pairs={{0,16},{8,24},{16,0},{24,8},{1,17},{9,25},{17,1},{25,9},{2,18},{10... | collective-permute-start | bytes 422408 | tf_op jit(solution)/shard_map/ppermute | solution.py:359
  6.1 7.0 %collective-permute-start.2 = (bf16[200,352]{1,0:T(8,128)(2,1)S(1)}, bf16[200,352]{1,0:T(8,128)(2,1)S(1)}, u32[]{:S(2)}, u32[]{:S(2)}) collective-permute-start(bf16[200,352]{1,0:T(8,128)(2,1)S(1)} %get-tuple-element.42), channel_id=1, source_target_pairs={{0,24},{8,16},{16,8},{24,0},{1,25},{9,17},{17,9},{25,1},{2,26},{10... | collective-permute-start | bytes 422408 | tf_op jit(solution)/shard_map/ppermute | solution.py:359
  13.6 2.5 %collective-permute-start.3 = (bf16[224,176]{1,0:T(8,128)(2,1)S(1)}, bf16[224,176]{1,0:T(8,128)(2,1)S(1)}, u32[]{:S(2)}, u32[]{:S(2)}) collective-permute-start(bf16[224,176]{1,0:T(8,128)(2,1)S(1)} %get-tuple-element.43), channel_id=1, source_target_pairs={{0,1},{1,0},{2,3},{3,2},{4,5},{5,4},{6,7},{7,6},{8,9},{9,8},{10,11... | collective-permute-start | bytes 236552 | tf_op jit(solution)/shard_map/ppermute | solution.py:37
  15.8 4.0 %copy-start = (f32[1,1408]{1,0:T(1,128)S(1)}, f32[1,1408]{1,0:T(1,128)}, u32[]{:S(2)}) copy-start(f32[1,1408]{1,0:T(1,128)} %potential.5) | copy-start | bytes 16900
  16.3 7.4 %collective-permute-start.4 = (bf16[304,352]{1,0:T(8,128)(2,1)S(1)}, bf16[304,352]{1,0:T(8,128)(2,1)S(1)}, u32[]{:S(2)}, u32[]{:S(2)}) collective-permute-start(bf16[304,352]{1,0:T(8,128)(2,1)S(1)} %shard_map.87.after), channel_id=1, source_target_pairs={{1,2},{2,1},{3,4},{4,3},{5,6},{6,5},{9,10},{10,9},{11,12},{12,11},... | collective-permute-start | bytes 642056 | tf_op jit(solution)/shard_map/ppermute | solution.py:37
  24.2 1.4 %collective-permute-start.5 = (bf16[200,352]{1,0:T(8,128)(2,1)S(1)}, bf16[200,352]{1,0:T(8,128)(2,1)S(1)}, u32[]{:S(2)}, u32[]{:S(2)}) collective-permute-start(bf16[200,352]{1,0:T(8,128)(2,1)S(1)} %get-tuple-element.51.sent), channel_id=1, source_target_pairs={{0,1},{1,0},{2,3},{3,2},{4,5},{5,4},{6,7},{7,6},{8,9},{9,8},{10,11... | collective-permute-start | bytes 422408 | tf_op jit(solution)/shard_map/ppermute | solution.py:37
  26.7 6.8 %collective-permute-start.6 = (bf16[200,352]{1,0:T(8,128)(2,1)S(1)}, bf16[200,352]{1,0:T(8,128)(2,1)S(1)}, u32[]{:S(2)}, u32[]{:S(2)}) collective-permute-start(bf16[200,352]{1,0:T(8,128)(2,1)S(1)} %get-tuple-element.53.after), channel_id=1, source_target_pairs={{1,2},{2,1},{3,4},{4,3},{5,6},{6,5},{9,10},{10,9},{11,12},{12,11},... | collective-permute-start | bytes 422408 | tf_op jit(solution)/shard_map/ppermute | solution.py:37
  33.9 1.4 %collective-permute-start.7 = (bf16[200,352]{1,0:T(8,128)(2,1)S(1)}, bf16[200,352]{1,0:T(8,128)(2,1)S(1)}, u32[]{:S(2)}, u32[]{:S(2)}) collective-permute-start(bf16[200,352]{1,0:T(8,128)(2,1)S(1)} %shard_map.94.sent), channel_id=1, source_target_pairs={{0,1},{1,0},{2,3},{3,2},{4,5},{5,4},{6,7},{7,6},{8,9},{9,8},{10,11... | collective-permute-start | bytes 422408 | tf_op jit(solution)/shard_map/ppermute | solution.py:37
  36.4 6.5 %collective-permute-start.8 = (bf16[200,352]{1,0:T(8,128)(2,1)S(1)}, bf16[200,352]{1,0:T(8,128)(2,1)S(1)}, u32[]{:S(2)}, u32[]{:S(2)}) collective-permute-start(bf16[200,352]{1,0:T(8,128)(2,1)S(1)} %get-tuple-element.61.after), channel_id=1, source_target_pairs={{1,2},{2,1},{3,4},{4,3},{5,6},{6,5},{9,10},{10,9},{11,12},{12,11},... | collective-permute-start | bytes 422408 | tf_op jit(solution)/shard_map/ppermute | solution.py:37
  43.2 1.4 %collective-permute-start.9 = (bf16[200,176]{1,0:T(8,128)(2,1)S(1)}, bf16[200,176]{1,0:T(8,128)(2,1)S(1)}, u32[]{:S(2)}, u32[]{:S(2)}) collective-permute-start(bf16[200,176]{1,0:T(8,128)(2,1)S(1)} %shard_map.98), channel_id=1, source_target_pairs={{0,1},{1,0},{2,3},{3,2},{4,5},{5,4},{6,7},{7,6},{8,9},{9,8},{10,11... | collective-permute-start | bytes 211208 | tf_op jit(solution)/shard_map/ppermute | solution.py:37
